TPU v7x, 32 devices: a whole 2x2x4 slice. The times are simulated.
32 devices in a mesh: section: 2 (over core), dp: 16 (over z, y, x).
Axes of the slice: x: 2, y: 2, z: 4, core: 2. Of those that a mesh axis runs over, the one named last changes fastest.
Arguments:
- section_inputs: bfloat16 [2, 2, 16384, 800], P('section', None, 'dp'), may hold values from -6 to 6
- seq_lengths: int32 [2, 128], P(None, 'dp'), may hold values from 0 to 1024, as said below
- dilations: int32 [2], P('section'), may hold values from 1 to 16, as said below
- gains_in: float32 [2, 800], P('section'), may hold values from 0.5 to 1.5
- biases_in: float32 [2, 800], P('section'), may hold values from -1.5 to 1.5
- gains_mid: float32 [2, 2, 400], P('section'), may hold values from 0.5 to 1.5
- biases_mid: float32 [2, 2, 400], P('section'), may hold values from -1.5 to 1.5
- out_bias: float32 [2, 800], P('section'), may hold values from -1.5 to 1.5
- w_in: bfloat16 [2, 800, 400], P('section'), may hold values from -0.21875 to 0.21875
- w_out: bfloat16 [2, 400, 800], P('section'), may hold values from -0.625 to 0.625
- conv_taps: bfloat16 [2, 5, 400, 400], P('section'), may hold values from -0.125 to 0.125
Outputs:
- block_out: bfloat16 [2, 2, 16384, 800], P('section', None, 'dp')
- input_grad: bfloat16 [2, 2, 16384, 800], P('section', None, 'dp')
- grad_gains_in: float32 [2, 800], P('section')
- grad_biases_in: float32 [2, 800], P('section')
- grad_gains_mid: float32 [2, 2, 400], P('section')
- grad_biases_mid: float32 [2, 2, 400], P('section')
- grad_out_bias: float32 [2, 800], P('section')
- grad_w_in: float32 [2, 800, 400], P('section')
- grad_w_out: float32 [2, 400, 800], P('section')
- grad_conv_taps: float32 [2, 5, 400, 400], P('section')
Inputs may be any that keep to these rules, and one draw needn't show every extreme that they name: `seq_lengths`: each index of dp holds, in each micro-batch, 1024 tokens made of whole sequences of 128, 256, 512 or 1024 tokens, each beginning at a multiple of its own length within those tokens; an entry is the length of the sequence that begins at that unit, 0 where none begins; some index holds one sequence of 1024 tokens. `dilations`: powers of two; one of the two is 16.
All inputs are finite; a program needn't handle non-finite values.
Results may differ from a plain program's by a relative error of at most 0.012.
Values may be sent and summed in bfloat16 or wider, within the bound.
No kernel may reach another device: no remote copies, remote signals or barrier semaphores. Data moves between devices by JAX's collectives and lax.ppermute only.
A program may use at most 192 MiB of HBM per device.

v0:
```python
import jax
import jax.numpy as jnp
from jax import lax
from jax.sharding import PartitionSpec as P

DEC_TAPS = 3


EPS = 1e-05


def from_behind(x, axis, by):
    count = lax.axis_size(axis)
    pairs = [(i, i + by) for i in range(count) if 0 <= i + by < count]
    return lax.ppermute(x, axis, pairs)


def normalize(values):
    average = jnp.mean(values, axis=-1, keepdims=True)
    centered = values - average
    inverse_dev = lax.rsqrt(jnp.mean(centered * centered, axis=-1, keepdims=True) + EPS)
    return (centered * inverse_dev, inverse_dev)


def norm_back(gradient, normed, inverse_dev, gain_vec):
    scaled = gradient * gain_vec
    first_mean = jnp.mean(scaled, axis=-1, keepdims=True)
    second_mean = jnp.mean(scaled * normed, axis=-1, keepdims=True)
    through = inverse_dev * (scaled - first_mean - normed * second_mean)
    return (through, jnp.sum(gradient * normed, axis=0), jnp.sum(gradient, axis=0))


def silu_slope(values):
    sigmoid_value = jax.nn.sigmoid(values)
    return sigmoid_value * (1.0 + values * (1.0 - sigmoid_value))


def shift_rows(token_rows, segment, offset):
    length_rows = token_rows.shape[0]
    padded = jnp.pad(token_rows, ((length_rows, length_rows), (0, 0)))
    shifted = lax.dynamic_slice_in_dim(padded, length_rows + offset, length_rows, 0)
    labels = jnp.pad(segment, (length_rows, length_rows), constant_values=-1)
    shifted_labels = lax.dynamic_slice_in_dim(labels, length_rows + offset, length_rows, 0)
    return jnp.where((shifted_labels == segment)[:, None], shifted, jnp.zeros_like(shifted))


def stacked_shifts(token_rows, segment, offsets):
    return jnp.stack([shift_rows(token_rows, segment, offset) for offset in offsets], axis=1)


def inner_rows(left_matrix, right_matrix):
    return lax.dot_general(
        left_matrix, right_matrix, (((0,), (0,)), ((), ())), preferred_element_type=jnp.float32
    )


def times_transpose(left_matrix, right_matrix):
    return lax.dot_general(
        left_matrix, right_matrix, (((1,), (1,)), ((), ())), preferred_element_type=jnp.float32
    )


def place(stacked, member, slot, active):
    current = lax.dynamic_index_in_dim(stacked, slot, 0, keepdims=False)
    return lax.dynamic_update_index_in_dim(stacked, jnp.where(active, member, current), slot, 0)


def block_forward(token_rows, segment, offsets, weights):
    gain_in, bias_in, gain_mid, bias_mid, bias_out, weight_in, weight_out, kernel = weights
    source = token_rows.astype(jnp.float32)
    normed_in, spread_in = normalize(source)
    hidden_in = jax.nn.silu(normed_in * gain_in + bias_in).astype(jnp.bfloat16)
    projected = jnp.dot(hidden_in, weight_in, preferred_element_type=jnp.float32)
    normed_mid, spread_mid = normalize(projected)
    hidden_mid = jax.nn.silu(normed_mid * gain_mid[0] + bias_mid[0]).astype(jnp.bfloat16)
    shifted = stacked_shifts(hidden_mid, segment, offsets)
    mixed = jnp.einsum("tki,kij->tj", shifted, kernel, preferred_element_type=jnp.float32)
    normed_out, spread_out = normalize(mixed)
    hidden_out = jax.nn.silu(normed_out * gain_mid[1] + bias_mid[1]).astype(jnp.bfloat16)
    result = source + jnp.dot(hidden_out, weight_out, preferred_element_type=jnp.float32) + bias_out
    kept = (
        normed_in,
        spread_in,
        hidden_in,
        normed_mid,
        spread_mid,
        hidden_mid,
        normed_out,
        spread_out,
        hidden_out,
    )
    return (result.astype(jnp.bfloat16), kept)


def block_backward(gradient_rows, segment, offsets, weights, kept):
    gain_in, bias_in, gain_mid, bias_mid, bias_out, weight_in, weight_out, kernel = weights
    (
        normed_in,
        spread_in,
        hidden_in,
        normed_mid,
        spread_mid,
        hidden_mid,
        normed_out,
        spread_out,
        hidden_out,
    ) = kept
    upstream = gradient_rows.astype(jnp.float32)
    grad_bias_out = jnp.sum(upstream, axis=0)
    grad_weight_out = inner_rows(hidden_out, gradient_rows)
    back_out = times_transpose(gradient_rows, weight_out)
    pre_out = normed_out * gain_mid[1] + bias_mid[1]
    grad_mixed, grad_gain_out, grad_shift_out = norm_back(
        back_out * silu_slope(pre_out), normed_out, spread_out, gain_mid[1]
    )
    grad_mixed = grad_mixed.astype(jnp.bfloat16)
    shifted = stacked_shifts(hidden_mid, segment, offsets)
    grad_kernel = jnp.einsum("tki,tj->kij", shifted, grad_mixed, preferred_element_type=jnp.float32)
    spread_back = jnp.einsum("tj,kij->tki", grad_mixed, kernel, preferred_element_type=jnp.float32)
    back_mid = jnp.zeros_like(normed_mid)
    for position in range(len(offsets)):
        back_mid = back_mid + shift_rows(spread_back[:, position], segment, -offsets[position])
    pre_mid = normed_mid * gain_mid[0] + bias_mid[0]
    grad_projected, grad_gain_mid, grad_shift_mid = norm_back(
        back_mid * silu_slope(pre_mid), normed_mid, spread_mid, gain_mid[0]
    )
    grad_projected = grad_projected.astype(jnp.bfloat16)
    grad_weight_in = inner_rows(hidden_in, grad_projected)
    back_in = times_transpose(grad_projected, weight_in)
    pre_in = normed_in * gain_in + bias_in
    grad_source, grad_gain_in, grad_bias_in = norm_back(
        back_in * silu_slope(pre_in), normed_in, spread_in, gain_in
    )
    grads = (
        grad_gain_in,
        grad_bias_in,
        jnp.stack([grad_gain_mid, grad_gain_out]),
        jnp.stack([grad_shift_mid, grad_shift_out]),
        grad_bias_out,
        grad_weight_in,
        grad_weight_out,
        grad_kernel,
    )
    return ((upstream + grad_source).astype(jnp.bfloat16), grads)


def shards(
    section_inputs,
    seq_lengths,
    dilations,
    gains_in,
    biases_in,
    gains_mid,
    biases_mid,
    out_bias,
    w_in,
    w_out,
    conv_taps,
):
    section_index = lax.axis_index("section")
    leading = section_index == 0
    own_rows = section_inputs[0]
    micro, tokens_dev, width = own_rows.shape
    units = seq_lengths.shape[1]
    starts = (seq_lengths > 0).astype(jnp.int32)
    segments = jnp.repeat(jnp.cumsum(starts, axis=1), tokens_dev // units, axis=1)
    tap_total = conv_taps.shape[1]
    live_taps = jnp.arange(tap_total) < jnp.where(leading, tap_total, DEC_TAPS)
    offsets = [(position - 2) * dilations[0] for position in range(tap_total)]
    kernel = jnp.where(live_taps[:, None, None], conv_taps[0], jnp.zeros_like(conv_taps[0]))
    weights = (
        gains_in[0],
        biases_in[0],
        gains_mid[0],
        biases_mid[0],
        out_bias[0],
        w_in[0],
        w_out[0],
        kernel,
    )
    arriving = jnp.zeros((tokens_dev, width), jnp.bfloat16)
    outputs = jnp.zeros_like(own_rows)
    kept_all = None
    for moment in range(micro + 1):
        slot = jnp.where(leading, min(moment, micro - 1), max(moment - 1, 0))
        active = jnp.where(leading, moment < micro, moment >= 1)
        token_rows = jnp.where(leading, own_rows[min(moment, micro - 1)], arriving)
        segment = lax.dynamic_index_in_dim(segments, slot, 0, keepdims=False)
        result, kept = block_forward(token_rows, segment, offsets, weights)
        if moment < micro:
            arriving = from_behind(result, "section", 1)
        outputs = place(outputs, result, slot, active)
        if kept_all is None:
            kept_all = tuple((jnp.zeros((micro,) + member.shape, member.dtype) for member in kept))
        kept_all = tuple(
            (place(whole, member, slot, active) for whole, member in zip(kept_all, kept))
        )
    arriving = jnp.zeros((tokens_dev, width), jnp.bfloat16)
    input_grads = jnp.zeros_like(own_rows)
    totals = None
    for moment in range(micro + 1):
        slot = jnp.where(leading, min(micro - moment, micro - 1), max(micro - 1 - moment, 0))
        active = jnp.where(leading, moment >= 1, moment < micro)
        gradient_rows = jnp.where(leading, arriving, own_rows[max(micro - 1 - moment, 0)])
        segment = lax.dynamic_index_in_dim(segments, slot, 0, keepdims=False)
        kept = tuple(
            (lax.dynamic_index_in_dim(whole, slot, 0, keepdims=False) for whole in kept_all)
        )
        sent, grads = block_backward(gradient_rows, segment, offsets, weights, kept)
        if moment < micro:
            arriving = from_behind(sent, "section", -1)
        input_grads = place(input_grads, sent, slot, active)
        grads = tuple((jnp.where(active, member, jnp.zeros_like(member)) for member in grads))
        grads = grads[:7] + (
            jnp.where(live_taps[:, None, None], grads[7], jnp.zeros_like(grads[7])),
        )
        if totals is None:
            totals = grads
        else:
            totals = tuple((earlier + later for earlier, later in zip(totals, grads)))
    totals = lax.psum(
        (totals[0], totals[1], totals[2], totals[3], totals[4], totals[5], totals[6], totals[7]),
        "dp",
    )
    return (
        outputs[None],
        input_grads[None],
        totals[0][None],
        totals[1][None],
        totals[2][None],
        totals[3][None],
        totals[4][None],
        totals[5][None],
        totals[6][None],
        totals[7][None],
    )


def solution(mesh):
    in_specs = (
        P("section", None, "dp", None),
        P(None, "dp"),
        P("section"),
        P("section", None),
        P("section", None),
        P("section", None, None),
        P("section", None, None),
        P("section", None),
        P("section", None, None),
        P("section", None, None),
        P("section", None, None, None),
    )
    out_specs = (
        P("section", None, "dp", None),
        P("section", None, "dp", None),
        P("section", None),
        P("section", None),
        P("section", None, None),
        P("section", None, None),
        P("section", None),
        P("section", None, None),
        P("section", None, None),
        P("section", None, None, None),
    )
    return jax.shard_map(shards, mesh=mesh, in_specs=in_specs, out_specs=out_specs, check_vma=False)
```

profile of v0, /device:TPU:0, one launch (start us, length us, event | category | flops | bytes accessed | tf_op | source)
XLA Modules:
  0.0 461.1 jit_solution(5394164643027310094)
XLA Ops:
  10.9 1.9 convert_reduce_fusion.2
  12.8 3.6 convert_reduce_fusion.5
  16.4 1.8 fusion.268
  19.1 1.6 select_bitcast_fusion.4
  21.4 1.3 fusion.135
  22.7 1.3 fusion.138
  25.0 1.3 fusion.141
  26.3 1.3 fusion.144
  27.6 5.3 %bitcast_reduce_fusion.2 = (f32[1024]{0:T(1024)S(1)}, f32[1024,400,1]{0,1,2:T(8,128)}) fusion(bf16[1024,5,400]{0,2,1:T(8,128)(2,1)} %fusion.144, bf16[1,5,400,400]{3,2,1,0:T(8,128)(2,1)S(1)} %copy-done.52, pred[5]{0:T(512)(128)(4,1)S(1)} %iota_compare_fusion), kind=kOutput, calls=%fused_computation.237 | convolution fusion | flops 1639608576 | bytes 7338501 | tf_op jit(solution)/shard_map/tki,kij->tj/dot_general | solution.py:77
  32.9 1.6 multiply_reduce_fusion.19
  34.6 3.2 select_bitcast_fusion.5
  37.8 2.4 fusion.51
  40.1 3.8 collective-permute-start
  43.9 2.7 select_bitcast_fusion.3
  46.6 2.6 fusion.64
  49.3 1.9 dynamic_update_slice.106
  53.0 1.5 copy-done.3
  56.0 1.7 select_bitcast_fusion.2
  61.2 1.7 bitcast_dynamic-update-slice_fusion.2
  67.4 2.0 bitcast_reduce_fusion.1
  69.6 1.4 bitcast_dynamic-update-slice_fusion.8
  71.1 1.4 collective-permute-start.1
  76.8 11.2 %fusion.94 = (bf16[1024,800]{0,1:T(8,128)(2,1)}, bf16[1024,800]{0,1:T(8,128)(2,1)S(1)}) fusion(bf16[2,1024,800]{1,2,0:T(8,128)(2,1)S(1)} %get-tuple-element.66, pred[]{:T(512)S(6)} %select_n.726, f32[800]{0:T(1024)S(1)} %reduce.1, f32[800]{0:T(1024)S(1)} %reduce, f32[1024]{0:T(1024)S(1)} %add_rsqrt_fusion.2, f32[1024]{0:T(1024)S(1)} %broadcast_multiply_fusion.24, ...), kind=kLoop, calls=%fused_computation.168 | loop fusion | flops 9011200 | bytes 6568193 | tf_op jit(solution)/shard_map/jit(_where)/select_n | solution.py:65
  94.2 2.0 bitcast_reduce_fusion
  96.9 1.8 multiply_reduce_fusion.9
  100.3 5.7 %fusion.251 = f32[1024,5,400]{0,2,1:T(8,128)} fusion(bf16[1024,400,1]{0,1,2:T(8,128)(2,1)S(1)} %fusion.130, bf16[1,5,400,400]{3,2,1,0:T(8,128)(2,1)S(1)} %copy-done.54, pred[5]{0:T(512)(128)(4,1)S(1)} %iota_compare_fusion), kind=kOutput, calls=%fused_computation.537 | convolution fusion | flops 1639200000 | bytes 10611205 | tf_op jit(solution)/shard_map/tj,kij->tki/dot_general | solution.py:119
  106.0 6.1 %slice_bitcast_fusion.23 = (f32[1024,400]{0,1:T(8,128)}, f32[1024,400]{0,1:T(8,128)}, f32[1024,400]{0,1:T(8,128)}, f32[1024,400]{0,1:T(8,128)}) fusion(f32[1024,5,400]{0,2,1:T(8,128)} %fusion.251), kind=kLoop, calls=%fused_computation.188 | loop fusion | bytes 13107200 | tf_op jit(solution)/shard_map/squeeze | solution.py:122
  112.1 5.6 %multiply_reduce_fusion.10 = (f32[400]{0:T(512)S(1)}, f32[1024]{0:T(1024)S(1)}, f32[1024]{0:T(1024)S(1)}, f32[400]{0:T(512)S(1)}, f32[1024,400]{0,1:T(8,128)S(1)}, /*index=5*/f32[1024,400]{0,1:T(8,128)S(1)}) fusion(f32[400]{0:T(512)S(1)} %bitcast.655, f32[400]{0:T(512)S(1)} %bitcast.664, s32[]{:T(128)S(6)} %select_n.758, f32[1024,400]{0,1:T(8,128)} %get-tuple-element.93, ...), kind=kLoop, calls=%fused_computation.245 | loop fusion | flops 11465952 | bytes 14772497 | tf_op jit(solution)/shard_map/reduce_sum | solution.py:30
  119.0 4.3 multiply_reduce_fusion.1
  123.4 4.9 %select_bitcast_fusion = (bf16[1,1024,800]{1,2,0:T(8,128)(2,1)}, bf16[1024,800]{0,1:T(8,128)(2,1)}) fusion(pred[]{:T(512)S(6)} %select_n.726, f32[1024,800]{0,1:T(8,128)S(1)} %fusion.4, f32[1024]{0:T(1024)S(1)} %broadcast_multiply_fusion.22, f32[1024]{0:T(1024)S(1)} %broadcast_multiply_fusion.23, f32[1024,800]{0,1:T(8,128)} %get-tuple-element.165, ...), kind=kLoop, calls=%fused_computation.252 | loop fusion | flops 8192000 | bytes 11484290 | tf_op jit(solution)/shard_map/jit(dynamic_update_index_in_dim)/broadcast_in_dim | solution.py:65
  128.2 1.7 collective-permute-start.2
  134.0 1.5 copy-done.38
  135.5 1.4 copy-done.41
  139.3 1.3 copy-done.15
  143.5 2.1 fusion.126
  146.6 1.8 fusion.113
  150.3 5.5 %fusion.250 = f32[1024,5,400]{0,2,1:T(8,128)} fusion(bf16[1024,400,1]{0,1,2:T(8,128)(2,1)S(1)} %fusion.132, bf16[1,5,400,400]{3,2,1,0:T(8,128)(2,1)S(1)} %copy-done.55, pred[5]{0:T(512)(128)(4,1)S(1)} %iota_compare_fusion), kind=kOutput, calls=%fused_computation.536 | convolution fusion | flops 1639200000 | bytes 10611205 | tf_op jit(solution)/shard_map/tj,kij->tki/dot_general | solution.py:119
  155.7 5.6 %slice_bitcast_fusion.17 = (f32[1024,400]{0,1:T(8,128)S(1)}, f32[1024,400]{0,1:T(8,128)S(1)}, f32[1024,400]{0,1:T(8,128)}, f32[1024,400]{0,1:T(8,128)}) fusion(f32[1024,5,400]{0,2,1:T(8,128)} %fusion.250), kind=kLoop, calls=%fused_computation.181 | loop fusion | bytes 13107200 | tf_op jit(solution)/shard_map/squeeze | solution.py:122
  161.3 5.9 %fusion.107 = (f32[400]{0:T(512)S(1)}, f32[1024]{0:T(1024)S(1)}, f32[1024]{0:T(1024)S(1)}, f32[400]{0:T(512)S(1)}, f32[1024,400]{0,1:T(8,128)}) fusion(f32[2,1024,400]{1,2,0:T(8,128)S(1)} %bitcast_dynamic-update-slice_fusion.4, s32[]{:T(128)S(6)} %select_n.721, f32[400]{0:T(512)S(1)} %bitcast.657, f32[400]{0:T(512)S(1)} %bitcast.665, s32[]{:T(128)S(6)} %select_n.758, ...), kind=kLoop, calls=%fused_computation.209 | loop fusion | flops 10237152 | bytes 11487508 | tf_op jit(solution)/shard_map/reduce_sum | solution.py:30
  167.3 1.9 fusion.106
  169.2 2.7 fusion.60
  171.9 2.1 bitcast_dynamic-update-slice_fusion.3
  174.0 1.3 collective-permute-start.3
  175.3 1.3 fusion.204
  176.6 6.5 %fusion.271 = f32[5,400,400]{2,1,0:T(8,128)} fusion(bf16[1024,5,400]{0,2,1:T(8,128)(2,1)} %copy-done.40, bf16[1024,400,1]{0,1,2:T(8,128)(2,1)S(1)} %fusion.130), kind=kOutput, calls=%fused_computation.549 | convolution fusion | flops 1638400000 | bytes 8115200 | tf_op jit(solution)/shard_map/tki,tj->kij/dot_general | solution.py:118
  183.2 2.2 fusion.100
  186.1 4.3 fusion.272
  191.0 1.8 multiply_reduce_fusion.7
  194.3 2.3 fusion.249
  197.9 3.8 multiply_reduce_fusion.8
  201.7 2.3 convolution_select_fusion
  204.1 2.2 add_bitcast_fusion.1
  207.7 2.1 add_bitcast_fusion.2
  210.8 5.1 %add_bitcast_fusion = f32[1,5,400,400]{3,2,1,0:T(8,128)} fusion(f32[5,400,400]{2,1,0:T(8,128)S(1)} %copy-done.63, f32[5,400,400]{2,1,0:T(8,128)S(1)} %copy-done.62, pred[5]{0:T(512)(128)(4,1)S(1)} %iota_compare_fusion, pred[]{:T(512)S(6)} %eq.96, pred[]{:T(512)S(6)} %select_n.726, bf16[1024,5,400]{0,2,1:T(8,128)(2,1)S(1)} %copy-done.42, ...), kind=kOutput, calls=%fused_computation.21 | convolution fusion | flops 1644000000 | bytes 14515207 | tf_op jit(solution)/shard_map/tki,tj->kij/dot_general | solution.py:118
  215.9 2.1 copy.52
  218.3 3.5 fusion.99
  221.9 1.7 copy.66
  223.6 1.4 copy-done.26
  225.0 4.3 multiply_reduce_fusion
  229.4 81.7 %all-reduce.32 = (f32[1,800]{1,0:T(1,128)}, f32[1,800]{1,0:T(1,128)}, f32[1,2,400]{2,1,0:T(2,128)}, f32[1,2,400]{2,1,0:T(2,128)}, f32[1,800]{1,0:T(1,128)}) all-reduce(f32[1,800]{1,0:T(1,128)S(1)} %broadcast_in_dim.468, f32[1,800]{1,0:T(1,128)S(1)} %broadcast_in_dim.469, ...), channel_id=1, replica_groups=mesh['section'=2,'dp'=16] {'dp'}, use_global_device_ids=true, to_apply=%region_40.41 | all-reduce | flops 4000 | bytes 32000 | tf_op jit(solution)/shard_map/psum | solution.py:221
  311.1 5.8 %fusion.63 = bf16[1,2,1024,800]{2,3,1,0:T(8,128)(2,1)} fusion(bf16[1,2,1024,800]{2,3,1,0:T(8,128)(2,1)} %copy.66, f32[2,1024,800]{1,2,0:T(8,128)} %copy-done.4, f32[1024,800]{0,1:T(8,128)} %get-tuple-element.169, bf16[1024,800]{0,1:T(8,128)(2,1)S(1)} %copy-done.17, bf16[2,1024,800]{1,2,0:T(8,128)(2,1)} %copy-done.5, f32[1024]{0:T(1024)S(1)} %get-tuple-element.176, ...), kind=kLoop, calls=%fused_computation.135 | loop fusion | flops 7372800 | bytes 11484289 | tf_op jit(solution)/shard_map/jit(dynamic_update_index_in_dim)/dynamic_update_slice | solution.py:65
  316.9 131.2 %all-reduce.36.cloned.1.call-done = (f32[1,800,400]{1,2,0:T(8,128)}, f32[1,400,800]{2,1,0:T(8,128)}, f32[1,5,400,400]{3,2,1,0:T(8,128)}) async-done(((f32[1,800,400]{1,2,0:T(8,128)}, f32[1,400,800]{2,1,0:T(8,128)}, f32[1,5,400,400]{3,2,1,0:T(8,128)}), (f32[1,800,400]{1,2,0:T(8,128)}, f32[1,400,800]{2,1,0:T(8,128)}, f32[1,5,400,400]{3,2,1,0:T(8,128)})) %all-reduce.36.cloned.1.call-update) | async-done | bytes 5760016 | tf_op jit(solution)/shard_map/psum | solution.py:221
  448.1 2.7 copy.83
  451.9 2.0 copy.85
  (272 shorter events, 50.7 us)
Async XLA Ops:
  7.2 30.6 %copy-start = (bf16[1,400,800]{2,1,0:T(8,128)(2,1)S(1)}, bf16[1,400,800]{2,1,0:T(8,128)(2,1)}, u32[]{:S(2)}) copy-start(bf16[1,400,800]{2,1,0:T(8,128)(2,1)} %param.20) | copy-start | bytes 1920004
  7.2 440.9 %all-reduce.36.cloned.1.call-start = ((), (), s32[]{:S(2)}) async-start(), calls=%async_computation | async-start | bytes 13926400 | tf_op jit(solution)/shard_map/psum | solution.py:221
  10.9 5.5 %copy-start.57 = (bf16[1,800,400]{1,2,0:T(8,128)(2,1)S(1)}, bf16[1,800,400]{1,2,0:T(8,128)(2,1)}, u32[]{:S(2)}) copy-start(bf16[1,800,400]{1,2,0:T(8,128)(2,1)} %param.19) | copy-start | bytes 1920004
  12.8 3.6 copy-start.1
  25.0 2.6 copy-start.52
  32.9 1.6 copy-start.50
  34.6 35.1 %copy-start.48 = (f32[800]{0:T(1024)}, f32[800]{0:T(1024)S(1)}, u32[]{:S(2)}) copy-start(f32[800]{0:T(1024)S(1)} %reduce.2) | copy-start | bytes 9604
  34.6 3.2 copy-start.2
  40.1 20.0 %collective-permute-start = (bf16[1024,800]{0,1:T(8,128)(2,1)}, bf16[1024,800]{0,1:T(8,128)(2,1)}, u32[]{:S(2)}, u32[]{:S(2)}) collective-permute-start(bf16[1024,800]{0,1:T(8,128)(2,1)} %fusion.51), channel_id=1, source_target_pairs={{0,16},{1,17},{2,18},{3,19},{4,20},{5,21},{6,22},{7,23},{8,24},{9,... | collective-permute-start | bytes 4915208 | tf_op jit(solution)/shard_map/ppermute | solution.py:15
  49.3 1.9 copy-start.27
  51.2 1.4 copy-start.14
  52.6 1.9 copy-start.3
  61.2 1.7 copy-start.58
  62.9 13.9 %copy-start.10 = (bf16[2,1024,800]{1,2,0:T(8,128)(2,1)}, bf16[2,1024,800]{1,2,0:T(8,128)(2,1)S(1)}, u32[]{:S(2)}) copy-start(bf16[2,1024,800]{1,2,0:T(8,128)(2,1)S(1)} %get-tuple-element.66) | copy-start | bytes 9830404
  65.8 1.6 copy-start.53
  71.1 1.8 copy-start.9
  71.1 4.4 collective-permute-start.1
  74.3 2.0 copy-start.18
  92.6 1.6 copy-start.54
  93.5 2.7 copy-start.40
  96.2 33.8 %copy-start.7 = (f32[1024,400,1]{0,1,2:T(8,128)}, f32[1024,400,1]{0,1,2:T(8,128)S(1)}, u32[]{:S(2)}) copy-start(f32[1024,400,1]{0,1,2:T(8,128)S(1)} %get-tuple-element.163) | copy-start | bytes 4915204
  119.0 4.3 copy-start.32
  123.4 6.7 %copy-start.19 = (bf16[2,1024,400]{1,2,0:T(8,128)(2,1)S(1)}, bf16[2,1024,400]{1,2,0:T(8,128)(2,1)}, u32[]{:S(2)}) copy-start(bf16[2,1024,400]{1,2,0:T(8,128)(2,1)} %copy-done.18) | copy-start | bytes 4915204
  128.2 17.8 %collective-permute-start.2 = (bf16[1024,800]{0,1:T(8,128)(2,1)}, bf16[1024,800]{0,1:T(8,128)(2,1)S(1)}, u32[]{:S(2)}, u32[]{:S(2)}) collective-permute-start(bf16[1024,800]{0,1:T(8,128)(2,1)} %get-tuple-element.77), channel_id=1, source_target_pairs={{16,0},{17,1},{18,2},{19,3},{20,4},{21,5},{22,6},{23,7},{24,8},{25... | collective-permute-start | bytes 4915208 | tf_op jit(solution)/shard_map/ppermute | solution.py:15
  133.1 3.8 copy-start.23
  133.6 2.0 copy-start.38
  134.0 2.9 copy-start.41
  136.9 1.4 copy-start.20
  136.9 2.4 copy-start.11
  138.3 2.3 copy-start.15
  138.4 2.4 copy-start.21
  141.8 1.7 copy-start.12
  146.1 25.9 %copy-start.4 = (f32[2,1024,800]{1,2,0:T(8,128)}, f32[2,1024,800]{1,2,0:T(8,128)S(1)}, u32[]{:S(2)}) copy-start(f32[2,1024,800]{1,2,0:T(8,128)S(1)} %bitcast_dynamic-update-slice_fusion) | copy-start | bytes 19660804
  148.4 1.9 copy-start.55
  167.3 1.9 copy-start.60
  169.2 2.7 copy-start.36
  174.0 9.2 %copy-start.5 = (bf16[2,1024,800]{1,2,0:T(8,128)(2,1)}, bf16[2,1024,800]{1,2,0:T(8,128)(2,1)S(1)}, u32[]{:S(2)}) copy-start(bf16[2,1024,800]{1,2,0:T(8,128)(2,1)S(1)} %get-tuple-element.73) | copy-start | bytes 9830404
  174.0 16.4 %collective-permute-start.3 = (bf16[1024,800]{0,1:T(8,128)(2,1)}, bf16[1024,800]{0,1:T(8,128)(2,1)S(1)}, u32[]{:S(2)}, u32[]{:S(2)}) collective-permute-start(bf16[1024,800]{0,1:T(8,128)(2,1)} %get-tuple-element.74), channel_id=1, source_target_pairs={{16,0},{17,1},{18,2},{19,3},{20,4},{21,5},{22,6},{23,7},{24,8},{25... | collective-permute-start | bytes 4915208 | tf_op jit(solution)/shard_map/ppermute | solution.py:15
  176.6 6.6 %copy-start.13 = (bf16[2,1024,800]{1,2,0:T(8,128)(2,1)S(1)}, bf16[2,1024,800]{1,2,0:T(8,128)(2,1)}, u32[]{:S(2)}) copy-start(bf16[2,1024,800]{1,2,0:T(8,128)(2,1)} %copy-done.12) | copy-start | bytes 9830404
  176.6 6.6 %copy-start.37 = (bf16[1024,400]{0,1:T(8,128)(2,1)S(1)}, bf16[1024,400]{0,1:T(8,128)(2,1)}, u32[]{:S(2)}) copy-start(bf16[1024,400]{0,1:T(8,128)(2,1)} %copy-done.36) | copy-start | bytes 2457604
  183.2 2.2 copy-start.35
  183.2 2.9 copy-start.39
  191.0 10.7 %copy-start.16 = (bf16[1024,800]{0,1:T(8,128)(2,1)}, bf16[1024,800]{0,1:T(8,128)(2,1)S(1)}, u32[]{:S(2)}) copy-start(bf16[1024,800]{0,1:T(8,128)(2,1)S(1)} %get-tuple-element.71) | copy-start | bytes 4915204
  192.8 1.6 copy-start.56
  196.7 1.2 copy-start.44
  196.7 1.2 copy-start.45
  201.7 2.4 copy-start.22
  201.7 2.4 copy-start.30
  204.1 2.2 copy-start.24
  204.1 5.7 %copy-start.63 = (f32[5,400,400]{2,1,0:T(8,128)S(1)}, f32[5,400,400]{2,1,0:T(8,128)}, u32[]{:S(2)}) copy-start(f32[5,400,400]{2,1,0:T(8,128)} %fusion.272) | copy-start | bytes 9600004
  206.3 1.4 copy-start.31
  206.3 3.5 copy-start.62
  207.7 3.1 copy-start.42
  215.9 2.4 copy-start.8
  215.9 2.4 copy-start.49
  215.9 9.1 %slice-start = ((s8[6553600]{0:T(1024)(128)(4,1)}), s8[4194304]{0:T(1024)(128)(4,1)S(1)}, s32[]{:S(2)}) async-start(s8[6553600]{0:T(1024)(128)(4,1)} %bitcast.648), calls=%async_computation.1 | async-start | bytes 8388608
  218.3 3.6 copy-start.6
  218.3 6.7 %slice-start.1 = ((s8[6553600]{0:T(1024)(128)(4,1)}), s8[2359296]{0:T(1024)(128)(4,1)S(1)}, s32[]{:S(2)}) async-start(s8[6553600]{0:T(1024)(128)(4,1)} %bitcast.648), calls=%async_computation.2 | async-start | bytes 4718592
  221.8 3.1 copy-start.26
  221.8 3.1 copy-start.61
  224.9 4.4 copy-start.43
  225.0 86.2 %copy-start.17 = (bf16[1024,800]{0,1:T(8,128)(2,1)S(1)}, bf16[1024,800]{0,1:T(8,128)(2,1)}, u32[]{:S(2)}) copy-start(bf16[1024,800]{0,1:T(8,128)(2,1)} %copy-done.16) | copy-start | bytes 4915204
  448.1 2.7 copy-start.29
  448.1 3.8 copy-start.25
  (7 other events, 7.5 us)
Sparse Core Ops, SparseCore 0:
  216.0 232.1 all-reduce.35
where the time goes:
time: 469 us; the launch traced here: 461 us
  waiting for transfers between devices  132 us (28%)
  other arithmetic  91.1 us (19%)
  blocking collectives  81.7 us (17%)
  matrix products  78.5 us (17%)
  local copies, waits for them, and re-layouts  52.6 us (11%)
  between operations  16.6 us (4%)
  starting transfers between devices  8.23 us (2%)
    psum x1, waiting for transfers between devices, shards(): lax.psum((totals[0], totals[1], totals[2], totals[3], totals[4], totals[5...  131 us
    psum x1, blocking collectives, shards(): lax.psum((totals[0], totals[1], totals[2], totals[3], totals[4], totals[5...  81.7 us
    unnamed x144, local copies, waits for them, and re-layouts  31.9 us
    select_n x13, other arithmetic, place(): jnp.where(active, member, current)  17.2 us
    dot_general x6, matrix products, times_transpose(): lax.dot_general(left_matrix, right_matrix, (((1,), (1,)), ((), ())), pref...  16.6 us
    dot_general x3, matrix products, block_backward(): jnp.einsum('tki,tj->kij', shifted, grad_mixed, preferred_element_type=jnp...  15.9 us
    reduce_sum x3, other arithmetic, norm_back(): jnp.sum(gradient * normed, axis=0)  15.3 us
    broadcast_in_dim x6, other arithmetic, place(): lax.dynamic_update_index_in_dim(stacked, jnp.where(active, member, curren...  14.3 us
  transfers between devices with their start and end apart: 5, of which 2 were waited for; matrix products, arithmetic and copies ran while one was open for 12% of the time, Pallas kernels for 0%

commit v1 on v0

v1 whole, which is shorter than its diff:
```python
import functools

import jax
import jax.numpy as jnp
from jax import lax
from jax.experimental import pallas as pl
from jax.experimental.pallas import tpu as pltpu
from jax.sharding import PartitionSpec as P

DEC_TAPS = 3
EPS = 1e-05
LANES = 128
VEC_ROWS = 48
BF = jnp.bfloat16
F32 = jnp.float32
VMEM_LIMIT = 62 * 2**20


def nn(left, right):
    return jnp.dot(left, right, preferred_element_type=F32)


def nt(left, right):
    return lax.dot_general(left, right, (((1,), (1,)), ((), ())), preferred_element_type=F32)


def column(vector):
    return jnp.broadcast_to(vector, (LANES, vector.shape[1])).T


def lane_block(index):
    return pl.ds(pl.multiple_of(index * LANES, LANES), LANES)


def normalize(values):
    scale = 1.0 / values.shape[0]
    centered = values - jnp.sum(values, 0, keepdims=True) * scale
    inverse_dev = lax.rsqrt(jnp.sum(centered * centered, 0, keepdims=True) * scale + EPS)
    return centered * inverse_dev, inverse_dev


def activate(normed, gain, bias):
    pre = normed * gain + bias
    sig = 0.5 * jnp.tanh(0.5 * pre) + 0.5
    out = pre * sig
    return out, (sig + out - out * sig) * gain


def norm_back(gradient, slope, normed, inverse_dev):
    scale = 1.0 / gradient.shape[0]
    scaled = gradient * slope
    weighted = scaled * normed
    first = jnp.sum(scaled, 0, keepdims=True) * scale
    second = jnp.sum(weighted, 0, keepdims=True) * scale
    return inverse_dev * (scaled - first - normed * second), scaled, weighted


def write_shifts(source, target, begins, offsets):
    feats, tokens = source.shape
    units = tokens // LANES
    lane = lax.broadcasted_iota(jnp.int32, (feats, LANES), 1)

    def one_unit(unit, _):
        here = lane_block(unit)
        ahead_unit = jnp.minimum(unit + 1, units - 1)
        joined_behind = ((unit > 0) & (begins[unit] == 0)).astype(F32)
        joined_ahead = ((unit < units - 1) & (begins[ahead_unit] == 0)).astype(F32)
        current = source[:, here]
        behind = source[:, lane_block(jnp.maximum(unit - 1, 0))] * joined_behind
        ahead = source[:, lane_block(ahead_unit)] * joined_ahead
        for position, (sign, step) in enumerate(offsets):
            if sign == 0:
                moved = current
            elif sign < 0:
                moved = pltpu.roll(jnp.where(lane < LANES - step, current, behind), step, 1)
            else:
                moved = pltpu.roll(jnp.where(lane >= step, current, ahead), LANES - step, 1)
            target[feats * position : feats * (position + 1), here] = moved.astype(BF)
        return 0

    lax.fori_loop(0, units, one_unit, 0)


def tap_offsets(taps, dilation, flip):
    result = []
    for position in range(taps):
        factor = (position - 2) * (-1 if flip else 1)
        result.append(((factor > 0) - (factor < 0), abs(factor) * dilation))
    return result


def forward_kernel(
    taps,
    begins, dilation, x, g1, b1, g2, b2, g3, b3, ob, w_in_t, w_out, conv,
    y, n1, s1, r, n2, s2, n3, s3, hin, shifted, hout,
    hmid, prod, cg1, cb1, cg2, cb2, cg3, cb3, cob, w_out_t, conv_t,
):
    tokens = x.shape[1]
    inner = w_out.shape[0]
    for col, vec in ((cg1, g1), (cb1, b1), (cg2, g2), (cb2, b2), (cg3, g3), (cb3, b3), (cob, ob)):
        col[...] = column(vec[...])
    w_out_t[...] = w_out[...].T
    for k in range(taps):
        conv_t[:, inner * k : inner * (k + 1)] = conv[k].T

    def first(i, _):
        c = lane_block(i)
        normed, dev = normalize(x[:, c].astype(F32))
        hidden, slope = activate(normed, cg1[...], cb1[...])
        n1[:, c] = normed
        s1[:, c] = slope
        r[0:1, c] = dev
        hin[:, c] = hidden.astype(BF)
        return 0

    lax.fori_loop(0, tokens // LANES, first, 0, unroll=2)
    prod[...] = nn(w_in_t[...], hin[...])

    def second(i, _):
        c = lane_block(i)
        normed, dev = normalize(prod[:, c])
        hidden, slope = activate(normed, cg2[...], cb2[...])
        n2[:, c] = normed
        s2[:, c] = slope
        r[1:2, c] = dev
        hmid[:, c] = hidden
        return 0

    lax.fori_loop(0, tokens // LANES, second, 0, unroll=2)
    write_shifts(hmid, shifted, begins, tap_offsets(taps, dilation[0], False))
    prod[...] = nn(conv_t[...], shifted[...])

    def third(i, _):
        c = lane_block(i)
        normed, dev = normalize(prod[:, c])
        hidden, slope = activate(normed, cg3[...], cb3[...])
        n3[:, c] = normed
        s3[:, c] = slope
        r[2:3, c] = dev
        hout[:, c] = hidden.astype(BF)
        return 0

    lax.fori_loop(0, tokens // LANES, third, 0, unroll=2)
    bias = jnp.concatenate([cob[...]] * (tokens // LANES), 1)
    y[...] = (x[...].astype(F32) + nn(w_out_t[...], hout[...]) + bias).astype(BF)


def forward(taps, begins, dilation, x, vecs, w_in_t, w_out, conv):
    width, tokens = x.shape
    inner = w_out.shape[0]
    smem = pl.BlockSpec(memory_space=pltpu.SMEM)
    vmem = pl.BlockSpec(memory_space=pltpu.VMEM)
    of = jax.ShapeDtypeStruct
    return pl.pallas_call(
        functools.partial(forward_kernel, taps),
        in_specs=[smem, smem] + [vmem] * 11,
        out_specs=[vmem] * 11,
        out_shape=[
            of((width, tokens), BF),
            of((width, tokens), F32),
            of((width, tokens), F32),
            of((8, tokens), F32),
            of((inner, tokens), F32),
            of((inner, tokens), F32),
            of((inner, tokens), F32),
            of((inner, tokens), F32),
            of((width, tokens), BF),
            of((inner * taps, tokens), BF),
            of((inner, tokens), BF),
        ],
        scratch_shapes=[pltpu.VMEM((inner, tokens), F32)] * 2
        + [pltpu.VMEM((width, LANES), F32)] * 2
        + [pltpu.VMEM((inner, LANES), F32)] * 4
        + [
            pltpu.VMEM((width, LANES), F32),
            pltpu.VMEM((width, inner), BF),
            pltpu.VMEM((inner, inner * taps), BF),
        ],
        compiler_params=pltpu.CompilerParams(vmem_limit_bytes=VMEM_LIMIT),
        name="forward_%d" % taps,
    )(begins, dilation, x, *vecs, w_in_t, w_out, conv)


def put_slabs(buf, row, matrix):
    rows, cols = matrix.shape
    for q in range(pl.cdiv(cols, LANES)):
        part = matrix[:, LANES * q : min(cols, LANES * (q + 1))]
        if part.shape[1] < LANES:
            part = jnp.concatenate([part, jnp.zeros((rows, LANES - part.shape[1]), F32)], 1)
        buf[row + q * rows : row + (q + 1) * rows, :] = part.astype(BF)


def row_sums(acc):
    return lax.dot_general(
        jnp.ones((8, LANES), F32), acc, (((1,), (1,)), ((), ())),
        precision=lax.Precision.HIGHEST, preferred_element_type=F32,
    )[0:1]


def layout(taps, width, inner):
    wide = pl.cdiv(width, LANES) * inner
    whole = inner // LANES
    taps_at = wide
    tails_at = taps_at + taps * whole * inner
    w_in_at = tails_at + inner
    vec_at = w_in_at + wide
    return taps_at, tails_at, w_in_at, vec_at, vec_at + VEC_ROWS


def backward_kernel(
    taps,
    begins, dilation, gy, n1, s1, r, n2, s2, n3, s3, hin, shifted, hout, g1, g2, g3, w_in_t, w_out, conv,
    gx, buf,
    prod, prod_wide, gm, gm_b, gp, moved, conv_w, w_in, ag1, ab1, ag2, ab2, ag3, ab3, vec,
):
    width, tokens = gy.shape
    inner = w_out.shape[0]
    taps_at, tails_at, w_in_at, vec_at, _ = layout(taps, width, inner)
    whole = inner // LANES
    tail = inner - whole * LANES
    w_in[...] = w_in_t[...].T
    for k in range(taps):
        conv_w[:, inner * k : inner * (k + 1)] = conv[k]
    for acc in (ag1, ab1, ag2, ab2, ag3, ab3):
        acc[...] = jnp.zeros_like(acc)

    prod[...] = nn(w_out[...], gy[...])

    def third(i, _):
        c = lane_block(i)
        value, scaled, weighted = norm_back(prod[:, c], s3[:, c], n3[:, c], r[2:3, c])
        ab3[...] += scaled
        ag3[...] += weighted
        gm[:, c] = value
        gm_b[:, c] = value.astype(BF)
        return 0

    lax.fori_loop(0, tokens // LANES, third, 0, unroll=2)
    put_slabs(buf, 0, nt(hout[...], gy[...]))
    write_shifts(gm, moved, begins, tap_offsets(taps, dilation[0], True))
    prod[...] = nn(conv_w[...], moved[...])
    for k in range(taps):
        grad = nt(shifted[inner * k : inner * (k + 1), :], gm_b[...])
        for q in range(whole):
            at = taps_at + inner * (whole * k + q)
            buf[at : at + inner, :] = grad[:, LANES * q : LANES * (q + 1)].astype(BF)
        buf[tails_at : tails_at + inner, tail * k : tail * (k + 1)] = grad[:, LANES * whole :].astype(BF)
    buf[tails_at : tails_at + inner, tail * taps :] = jnp.zeros((inner, LANES - tail * taps), BF)

    def second(i, _):
        c = lane_block(i)
        value, scaled, weighted = norm_back(prod[:, c], s2[:, c], n2[:, c], r[1:2, c])
        ab2[...] += scaled
        ag2[...] += weighted
        gp[:, c] = value.astype(BF)
        return 0

    lax.fori_loop(0, tokens // LANES, second, 0, unroll=2)
    put_slabs(buf, w_in_at, nt(gp[...], hin[...]))
    prod_wide[...] = nn(w_in[...], gp[...])

    def first(i, _):
        c = lane_block(i)
        value, scaled, weighted = norm_back(prod_wide[:, c], s1[:, c], n1[:, c], r[0:1, c])
        ab1[...] += scaled
        ag1[...] += weighted
        gx[:, c] = (gy[:, c].astype(F32) + value).astype(BF)
        return 0

    lax.fori_loop(0, tokens // LANES, first, 0, unroll=2)

    vec[...] = jnp.zeros_like(vec)
    sums = [
        row_sums(ag1[...]) / g1[...],
        row_sums(ab1[...]) / g1[...],
        row_sums(ag2[...]) / g2[...],
        row_sums(ag3[...]) / g3[...],
        row_sums(ab2[...]) / g2[...],
        row_sums(ab3[...]) / g3[...],
        nt(jnp.ones((16, tokens), BF), gy[...])[0:1],
    ]
    row = 0
    for total in sums:
        for at in range(0, total.shape[1], LANES):
            part = total[:, at : at + LANES]
            vec[row : row + 1, 0 : part.shape[1]] = part
            row += 1
    buf[vec_at : vec_at + VEC_ROWS, :] = vec[...].astype(BF)


def backward(taps, begins, dilation, gy, kept, gains, w_in_t, w_out, conv):
    width, tokens = gy.shape
    inner = w_out.shape[0]
    smem = pl.BlockSpec(memory_space=pltpu.SMEM)
    vmem = pl.BlockSpec(memory_space=pltpu.VMEM)
    of = jax.ShapeDtypeStruct
    return pl.pallas_call(
        functools.partial(backward_kernel, taps),
        in_specs=[smem, smem] + [vmem] * 17,
        out_specs=[vmem] * 2,
        out_shape=[of((width, tokens), BF), of((layout(taps, width, inner)[-1], LANES), BF)],
        scratch_shapes=[
            pltpu.VMEM((inner, tokens), F32),
            pltpu.VMEM((width, tokens), F32),
            pltpu.VMEM((inner, tokens), F32),
            pltpu.VMEM((inner, tokens), BF),
            pltpu.VMEM((inner, tokens), BF),
            pltpu.VMEM((inner * taps, tokens), BF),
            pltpu.VMEM((inner, inner * taps), BF),
            pltpu.VMEM((width, inner), BF),
            pltpu.VMEM((width, LANES), F32),
            pltpu.VMEM((width, LANES), F32),
        ]
        + [pltpu.VMEM((inner, LANES), F32)] * 4
        + [pltpu.VMEM((VEC_ROWS, LANES), F32)],
        compiler_params=pltpu.CompilerParams(vmem_limit_bytes=VMEM_LIMIT),
        name="backward_%d" % taps,
    )(begins, dilation, gy, *kept, *gains, w_in_t, w_out, conv)


def swap_sections(value):
    return lax.ppermute(value, "section", [(0, 1), (1, 0)])


def swap_dp(value, mask):
    count = lax.axis_size("dp")
    return lax.ppermute(value, "dp", [(i, i ^ mask) for i in range(count)])


def add_rounded(*parts):
    total = parts[0].astype(F32)
    for part in parts[1:]:
        total = total + part.astype(F32)
    return total.astype(BF)


def piece(array, index, count):
    size = array.shape[0] // count
    return lax.dynamic_slice_in_dim(array, index * size, size, 0)


def scatter_step(array, index, bits):
    own = (index >> bits[0]) & (2 ** len(bits) - 1)
    count = 2 ** len(bits)
    parts = [piece(array, own, count)]
    for other in range(1, count):
        parts.append(swap_dp(piece(array, own ^ other, count), other << bits[0]))
    return add_rounded(*parts)


def gather_step(array, index, bits):
    own = (index >> bits[0]) & (2 ** len(bits) - 1)
    count = 2 ** len(bits)
    size = array.shape[0]
    whole = jnp.zeros((size * count,) + array.shape[1:], array.dtype)
    whole = lax.dynamic_update_slice_in_dim(whole, array, own * size, 0)
    for other in range(1, count):
        whole = lax.dynamic_update_slice_in_dim(whole, swap_dp(array, other << bits[0]), (own ^ other) * size, 0)
    return whole


def step_orders(count):
    total = count.bit_length() - 1
    rest = []
    at = 2
    while at < total:
        rest.append(list(range(at, min(at + 2, total))))
        at += 2
    return ([[0], [1]] + rest, [[1], [0]] + rest)


def all_reduce_dp(array):
    count = lax.axis_size("dp")
    index = lax.axis_index("dp")
    orders = step_orders(count)
    half = array.shape[0] // 2
    parts = [array[:half], array[half:]]
    for steps in zip(*orders):
        parts = [scatter_step(part, index, bits) for part, bits in zip(parts, steps)]
    for steps in reversed(list(zip(*orders))):
        parts = [gather_step(part, index, bits) for part, bits in zip(parts, steps)]
    return jnp.concatenate(parts, 0)


def reduce_block(buf, section):
    rows = buf.shape[0]
    unit = 2 * 2 * 16 * lax.axis_size("dp")
    padded = jnp.pad(buf, ((0, -rows % unit), (0, 0)))
    mine = add_rounded(piece(padded, section, 2), swap_sections(piece(padded, 1 - section, 2)))
    return all_reduce_dp(mine)


def unpack_kernel(taps_of, index, own0, got0, own1, got1, w_in_t, w_out, conv, gin, bin_, gmid, bmid, out_bias, buf, sem):
    inner, width = w_out.shape
    whole = inner // LANES
    tail = inner - whole * LANES
    slots = conv.shape[0]

    def write(taps, first, second):
        half = first.shape[0]
        copies = [
            pltpu.make_async_copy(first, buf.at[pl.ds(0, half)], sem.at[0]),
            pltpu.make_async_copy(second, buf.at[pl.ds(half, half)], sem.at[1]),
        ]
        for copy in copies:
            copy.start()
        for copy in copies:
            copy.wait()
        taps_at, tails_at, w_in_at, vec_at, _ = layout(taps, width, inner)

        def wide(target, row):
            for at in range(0, width, LANES):
                q = at // LANES
                size = min(LANES, width - at)
                target[:, at : at + size] = buf[row + q * inner : row + (q + 1) * inner, 0:size].astype(F32)

        wide(w_out, 0)
        wide(w_in_t, w_in_at)
        tails = buf[tails_at : tails_at + inner, :].astype(F32)
        for k in range(slots):
            if k >= taps:
                conv[k] = jnp.zeros((inner, inner), F32)
                continue
            for q in range(whole):
                at = taps_at + inner * (whole * k + q)
                conv[k, :, LANES * q : LANES * (q + 1)] = buf[at : at + inner, :].astype(F32)
            conv[k, :, LANES * whole :] = tails[:, tail * k : tail * (k + 1)]
        vec = buf[vec_at : vec_at + VEC_ROWS, :].astype(F32)
        row = 0
        for target, member in ((gin, 0), (bin_, 0), (gmid, 0), (gmid, 1), (bmid, 0), (bmid, 1), (out_bias, 0)):
            for at in range(0, target.shape[1], LANES):
                size = min(LANES, target.shape[1] - at)
                target[member : member + 1, at : at + size] = vec[row : row + 1, 0:size]
                row += 1

    pl.when(index[0] == 0)(lambda: write(taps_of[0], own0, got0))
    pl.when(index[0] != 0)(lambda: write(taps_of[1], got1, own1))


def unpack(taps_of, section, halves, got, width, inner):
    smem = pl.BlockSpec(memory_space=pltpu.SMEM)
    vmem = pl.BlockSpec(memory_space=pltpu.VMEM)
    hbm = pl.BlockSpec(memory_space=pl.ANY)
    of = jax.ShapeDtypeStruct
    rows = max(2 * half.shape[0] for half in halves)
    return pl.pallas_call(
        functools.partial(unpack_kernel, taps_of),
        in_specs=[smem] + [hbm] * 4,
        out_specs=[vmem] * 8,
        out_shape=[
            of((inner, width), F32),
            of((inner, width), F32),
            of((taps_of[0], inner, inner), F32),
            of((1, width), F32),
            of((1, width), F32),
            of((2, inner), F32),
            of((2, inner), F32),
            of((1, width), F32),
        ],
        scratch_shapes=[pltpu.VMEM((rows, LANES), BF), pltpu.SemaphoreType.DMA((2,))],
        compiler_params=pltpu.CompilerParams(vmem_limit_bytes=VMEM_LIMIT),
        name="unpack",
    )(jnp.reshape(section, (1,)), halves[0], got[0], halves[1], got[1])


def shards(
    section_inputs,
    seq_lengths,
    dilations,
    gains_in,
    biases_in,
    gains_mid,
    biases_mid,
    out_bias,
    w_in,
    w_out,
    conv_taps,
):
    section = lax.axis_index("section")
    leading = section == 0
    rows = jnp.swapaxes(section_inputs[0], 1, 2)
    width = rows.shape[1]
    inner = w_out.shape[1]
    taps_of = (conv_taps.shape[1], DEC_TAPS)

    def pick(stacked, index):
        return lax.dynamic_index_in_dim(stacked, index, 0, keepdims=False)

    def both(mine):
        theirs = swap_sections(mine)
        return jnp.where(leading, mine, theirs), jnp.where(leading, theirs, mine)

    own_rows = pick(rows, section)
    got_rows = swap_sections(pick(rows, 1 - section))
    x = jnp.where(leading, own_rows, got_rows)
    cotangent = jnp.where(leading, got_rows, own_rows)
    w_in_t = both(jnp.swapaxes(w_in[0], 0, 1))
    small = both(
        jnp.concatenate(
            [
                gains_in[0], biases_in[0], gains_mid[0, 0], biases_mid[0, 0], gains_mid[0, 1], biases_mid[0, 1],
                out_bias[0], dilations.astype(F32),
            ]
        )
    )
    conv = both(conv_taps[0])
    w_out_both = both(w_out[0])

    vecs_of, dil_of = [], []
    for member in small:
        vecs, at = [], 0
        for size in (width, width, inner, inner, inner, inner, width):
            vecs.append(member[at : at + size][None])
            at += size
        vecs_of.append(vecs)
        dil_of.append(member[at : at + 1].astype(jnp.int32))
    begins = pick(seq_lengths, section)

    encoded = forward(taps_of[0], begins, dil_of[0], x, vecs_of[0], w_in_t[0], w_out_both[0], conv[0])
    decoded = forward(taps_of[1], begins, dil_of[1], encoded[0], vecs_of[1], w_in_t[1], w_out_both[1], conv[1])
    grad_dec, buf_dec = backward(
        taps_of[1], begins, dil_of[1], cotangent, decoded[1:], vecs_of[1][0:5:2], w_in_t[1], w_out_both[1], conv[1]
    )
    half_dec = reduce_block(buf_dec, section)
    got_dec = lax.ppermute(half_dec, "section", [(0, 1)])
    grad_enc, buf_enc = backward(
        taps_of[0], begins, dil_of[0], grad_dec, encoded[1:], vecs_of[0][0:5:2], w_in_t[0], w_out_both[0], conv[0]
    )
    half_enc = reduce_block(buf_enc, section)
    got_enc = lax.ppermute(half_enc, "section", [(1, 0)])

    def own_section(enc, dec):
        keep = jnp.where(leading, enc, dec)
        got = swap_sections(jnp.where(leading, dec, enc))
        pair = jnp.where(leading, jnp.stack([keep, got]), jnp.stack([got, keep]))
        return jnp.swapaxes(pair, 1, 2)[None]

    outputs = own_section(encoded[0], decoded[0])
    input_grads = own_section(grad_enc, grad_dec)
    grads = unpack(taps_of, section, (half_enc, half_dec), (got_enc, got_dec), width, inner)
    return (
        outputs,
        input_grads,
        grads[3],
        grads[4],
        grads[5][None],
        grads[6][None],
        grads[7],
        jnp.swapaxes(grads[0], 0, 1)[None],
        grads[1][None],
        grads[2][None],
    )


def solution(mesh):
    in_specs = (
        P("section", None, "dp", None),
        P(None, "dp"),
        P("section"),
        P("section", None),
        P("section", None),
        P("section", None, None),
        P("section", None, None),
        P("section", None),
        P("section", None, None),
        P("section", None, None),
        P("section", None, None, None),
    )
    out_specs = (
        P("section", None, "dp", None),
        P("section", None, "dp", None),
        P("section", None),
        P("section", None),
        P("section", None, None),
        P("section", None, None),
        P("section", None),
        P("section", None, None),
        P("section", None, None),
        P("section", None, None, None),
    )
    return jax.shard_map(shards, mesh=mesh, in_specs=in_specs, out_specs=out_specs, check_vma=False)
```

time: 469 us -> 294 us (0.63)
  Pallas kernels: 0 us -> 106 us
  blocking collectives: 81.7 us -> 0 us
  matrix products: 78.5 us -> 0 us
  other arithmetic: 91.1 us -> 25.8 us
  waiting for transfers between devices: 132 us -> 82.1 us
  starting transfers between devices: 8.23 us -> 53.8 us
  local copies, waits for them, and re-layouts: 52.6 us -> 19.6 us
  between operations: 16.6 us -> 3.39 us
    psum x1 -> x0, waiting for transfers between devices: 131 us -> none  [shards(): lax.psum((totals[0], totals[1], totals[2], totals[3], totals[4], totals[5...]
    pallas_call x0 -> x5, Pallas kernels: none -> 106 us  [the longest x2 56.7 us: backward(): pl.pallas_call(functools.partial(backward_kernel, taps), in_specs=[smem,...]
    psum x1 -> x0, blocking collectives: 81.7 us -> none  [shards(): lax.psum((totals[0], totals[1], totals[2], totals[3], totals[4], totals[5...]
    ppermute x4 -> x51, waiting for transfers between devices: 1.18 us -> 82.1 us  [the longest x40 82.1 us: swap_dp(): return lax.ppermute(value, 'dp', [(i, i ^ mask) for i in range(count)])]
    dot_general x27 -> x0, matrix products: 78.5 us -> none  [the longest x6 16.6 us: times_transpose(): lax.dot_general(left_matrix, right_matrix, (((1,), (1,)), ((), ())), pref...]
    ppermute x4 -> x51, starting transfers between devices: 8.19 us -> 53.8 us  [the longest x40 46.5 us: swap_dp(): return lax.ppermute(value, 'dp', [(i, i ^ mask) for i in range(count)])]
    unnamed x144 -> x32, local copies, waits for them, and re-layouts: 31.9 us -> 4.41 us
    reduce_sum x17 -> x0, other arithmetic: 26.9 us -> none  [the longest x3 15.3 us: norm_back(): jnp.sum(gradient * normed, axis=0)]
  transfers between devices with their start and end apart: 5 -> 51, of which waited for: 2 -> 29; matrix products, arithmetic and copies ran while one was open for 12% -> 12% of each run, Pallas kernels for 0% -> 10%
where the time goes in v1:
time: 294 us; the launch traced here: 291 us
  Pallas kernels  106 us (36%)
  waiting for transfers between devices  82.1 us (28%)
  starting transfers between devices  53.8 us (18%)
  other arithmetic  25.8 us (9%)
  local copies, waits for them, and re-layouts  19.6 us (7%)
  between operations  3.39 us (1%)
    ppermute x40, waiting for transfers between devices, swap_dp(): return lax.ppermute(value, 'dp', [(i, i ^ mask) for i in range(count)])  82.1 us
    pallas_call x2, Pallas kernels, backward(): pl.pallas_call(functools.partial(backward_kernel, taps), in_specs=[smem,...  56.7 us
    ppermute x40, starting transfers between devices, swap_dp(): return lax.ppermute(value, 'dp', [(i, i ^ mask) for i in range(count)])  46.5 us
    pallas_call x2, Pallas kernels, forward(): pl.pallas_call(functools.partial(forward_kernel, taps), in_specs=[smem, s...  43.5 us
    select_n x4, other arithmetic, both(): return (jnp.where(leading, mine, theirs), jnp.where(leading, theirs, mine))  7.42 us
    broadcast_in_dim x2, other arithmetic, own_section(): return jnp.swapaxes(pair, 1, 2)[None]  5.88 us
  transfers between devices with their start and end apart: 51, of which 29 were waited for; matrix products, arithmetic and copies ran while one was open for 12% of the time, Pallas kernels for 10%

profile of v1, /device:TPU:0, one launch (start us, length us, event | category | flops | bytes accessed | tf_op | source)
XLA Modules:
  0.0 290.5 jit_solution(6047256297008268143)
XLA Ops:
  5.7 2.8 dynamic-slice_bitcast_fusion
  16.8 2.4 broadcast_select_fusion.5
  19.3 2.5 broadcast_select_fusion.4
  21.8 2.5 broadcast_select_fusion
  24.7 3.3 %bitcast_select_fusion = (bf16[800,1024]{1,0:T(8,128)(2,1)}, bf16[800,1024]{1,0:T(8,128)(2,1)}) fusion(bf16[800,1024]{1,0:T(8,128)(2,1)} %collective-permute-done.1, pred[]{:T(512)S(6)} %eq.3, bf16[1,2,1024,800]{2,3,1,0:T(8,128)(2,1)S(1)} %copy-done.9, s32[]{:T(128)S(6)} %select_n.219), kind=kLoop, calls=%fused_computation.12 | loop fusion | flops 1638400 | bytes 6553605 | tf_op jit(solution)/shard_map/jit(_where)/select_n | solution.py:496
  28.1 22.9 %forward_5.1 = (bf16[800,1024]{1,0:T(8,128)(2,1)}, f32[800,1024]{1,0:T(8,128)}, f32[800,1024]{1,0:T(8,128)}, f32[8,1024]{1,0:T(8,128)}, f32[400,1024]{1,0:T(8,12...) custom-call(s32[8]{0:T(128)} %fusion.2.begins, ...), custom_call_target="tpu_custom_call" | custom-call | tf_op jit(solution)/shard_map/forward_5/pallas_call | solution.py:154
  51.0 20.5 %forward_3.1 = (bf16[800,1024]{1,0:T(8,128)(2,1)}, f32[800,1024]{1,0:T(8,128)}, f32[800,1024]{1,0:T(8,128)}, f32[8,1024]{1,0:T(8,128)}, f32[400,1024]{1,0:T(8,12...) custom-call(s32[8]{0:T(128)} %fusion.2.begins, ...), custom_call_target="tpu_custom_call" | custom-call | tf_op jit(solution)/shard_map/forward_3/pallas_call | solution.py:154
  71.6 27.1 %backward_3.1 = (bf16[800,1024]{1,0:T(8,128)(2,1)}, bf16[9648,128]{1,0:T(8,128)(2,1)}) custom-call(s32[8]{0:T(128)} %fusion.2.begins, s32[1]{0:T(128)S(6)} %convert_element_type.165.dilation, bf16[800,1024]{1,0:T(8,128)(2,1)} %get-tuple-element.86.gy, f32[800,1024]{1,0:T(8,128)} %get-tuple-element.46.n1, f32[800,1024]{1,0:T(8,128)} %get-tuple-element.47.s1, ...), custom_call_target="tpu_custom_call" | custom-call | tf_op jit(solution)/shard_map/backward_3/pallas_call | solution.py:297
  98.7 2.6 pad_dynamic-slice_fusion.2
  101.4 2.0 select_bitcast_fusion.1
  103.8 29.6 %backward_5.1 = (bf16[800,1024]{1,0:T(8,128)(2,1)}, bf16[12048,128]{1,0:T(8,128)(2,1)}) custom-call(s32[8]{0:T(128)} %fusion.2.begins, s32[1]{0:T(128)S(6)} %convert_element_type.164.dilation, bf16[800,1024]{1,0:T(8,128)(2,1)} %get-tuple-element.56.gy, f32[800,1024]{1,0:T(8,128)} %get-tuple-element.57.n1, f32[800,1024]{1,0:T(8,128)} %get-tuple-element.58.s1, ...), custom_call_target="tpu_custom_call" | custom-call | tf_op jit(solution)/shard_map/backward_5/pallas_call | solution.py:297
  133.5 1.8 select_bitcast_fusion
  136.2 1.3 copy-done.3
  137.6 1.8 add_convert_fusion.1
  139.5 2.6 collective-permute-start.40
  142.2 1.6 collective-permute-start.30
  144.4 6.1 %collective-permute-done.40 = bf16[1280,128]{1,0:T(8,128)(2,1)S(1)} collective-permute-done((bf16[1280,128]{1,0:T(8,128)(2,1)S(1)}, bf16[1280,128]{1,0:T(8,128)(2,1)S(1)}, u32[]{:S(2)}, u32[]{:S(2)}) %collective-permute-start.40) | collective-permute-done | bytes 327712 | tf_op jit(solution)/shard_map/ppermute | solution.py:327
  150.6 1.8 collective-permute-start.41
  152.5 1.6 collective-permute-start.31
  154.1 2.6 collective-permute-done.41
  156.8 3.7 %collective-permute-start.44 = (bf16[160,128]{1,0:T(8,128)(2,1)S(1)}, bf16[160,128]{1,0:T(8,128)(2,1)S(1)}, u32[]{:S(2)}, u32[]{:S(2)}) collective-permute-start(bf16[160,128]{1,0:T(8,128)(2,1)S(1)} %get-tuple-element.112), channel_id=1, source_target_pairs={{0,12},{1,13},{2,14},{3,15},{4,8},{5,9},{6,10},{7,11},{8,4},{9,5},... | collective-permute-start | bytes 122888 | tf_op jit(solution)/shard_map/ppermute | solution.py:327
  161.3 1.4 collective-permute-done.44
  162.7 3.7 %collective-permute-start.34 = (bf16[160,128]{1,0:T(8,128)(2,1)S(1)}, bf16[160,128]{1,0:T(8,128)(2,1)S(1)}, u32[]{:S(2)}, u32[]{:S(2)}) collective-permute-start(bf16[160,128]{1,0:T(8,128)(2,1)S(1)} %get-tuple-element.109), channel_id=1, source_target_pairs={{0,12},{1,13},{2,14},{3,15},{4,8},{5,9},{6,10},{7,11},{8,4},{9,5},... | collective-permute-start | bytes 122888 | tf_op jit(solution)/shard_map/ppermute | solution.py:327
  167.2 1.5 collective-permute-done.34
  168.6 1.5 collective-permute-start.18
  170.2 1.1 collective-permute-done.33
  171.3 1.5 collective-permute-start.8
  172.9 3.9 %collective-permute-done.45 = bf16[160,128]{1,0:T(8,128)(2,1)S(1)} collective-permute-done((bf16[160,128]{1,0:T(8,128)(2,1)S(1)}, bf16[160,128]{1,0:T(8,128)(2,1)S(1)}, u32[]{:S(2)}, u32[]{:S(2)}) %collective-permute-start.45) | collective-permute-done | bytes 40992 | tf_op jit(solution)/shard_map/ppermute | solution.py:327
  177.8 3.9 %collective-permute-done.46 = bf16[160,128]{1,0:T(8,128)(2,1)S(1)} collective-permute-done((bf16[160,128]{1,0:T(8,128)(2,1)S(1)}, bf16[160,128]{1,0:T(8,128)(2,1)S(1)}, u32[]{:S(2)}, u32[]{:S(2)}) %collective-permute-start.46) | collective-permute-done | bytes 40992 | tf_op jit(solution)/shard_map/ppermute | solution.py:327
  181.7 2.4 collective-permute-start.47
  184.2 3.4 %collective-permute-done.47 = bf16[160,128]{1,0:T(8,128)(2,1)S(1)} collective-permute-done((bf16[160,128]{1,0:T(8,128)(2,1)S(1)}, bf16[160,128]{1,0:T(8,128)(2,1)S(1)}, u32[]{:S(2)}, u32[]{:S(2)}) %collective-permute-start.47) | collective-permute-done | bytes 40992 | tf_op jit(solution)/shard_map/ppermute | solution.py:327
  187.6 4.0 %collective-permute-done.35 = bf16[160,128]{1,0:T(8,128)(2,1)S(1)} collective-permute-done((bf16[160,128]{1,0:T(8,128)(2,1)S(1)}, bf16[160,128]{1,0:T(8,128)(2,1)S(1)}, u32[]{:S(2)}, u32[]{:S(2)}) %collective-permute-start.35) | collective-permute-done | bytes 40992 | tf_op jit(solution)/shard_map/ppermute | solution.py:327
  192.5 3.9 %collective-permute-done.36 = bf16[160,128]{1,0:T(8,128)(2,1)S(1)} collective-permute-done((bf16[160,128]{1,0:T(8,128)(2,1)S(1)}, bf16[160,128]{1,0:T(8,128)(2,1)S(1)}, u32[]{:S(2)}, u32[]{:S(2)}) %collective-permute-start.36) | collective-permute-done | bytes 40992 | tf_op jit(solution)/shard_map/ppermute | solution.py:327
  196.4 2.4 collective-permute-start.37
  198.9 3.4 %collective-permute-done.37 = bf16[160,128]{1,0:T(8,128)(2,1)S(1)} collective-permute-done((bf16[160,128]{1,0:T(8,128)(2,1)S(1)}, bf16[160,128]{1,0:T(8,128)(2,1)S(1)}, u32[]{:S(2)}, u32[]{:S(2)}) %collective-permute-start.37) | collective-permute-done | bytes 40992 | tf_op jit(solution)/shard_map/ppermute | solution.py:327
  202.2 1.3 collective-permute-start.48
  203.7 1.3 collective-permute-start.38
  205.1 1.6 collective-permute-start.19
  207.6 1.9 collective-permute-start.9
  211.0 1.8 collective-permute-start.22
  212.8 2.2 collective-permute-done.9
  215.5 1.4 collective-permute-done.22
  216.9 1.8 collective-permute-start.12
  219.5 1.8 collective-permute-start.10
  221.4 1.4 collective-permute-done.12
  224.6 1.8 collective-permute-start.39
  226.5 4.0 %collective-permute-done.23 = bf16[192,128]{1,0:T(8,128)(2,1)S(1)} collective-permute-done((bf16[192,128]{1,0:T(8,128)(2,1)S(1)}, bf16[192,128]{1,0:T(8,128)(2,1)S(1)}, u32[]{:S(2)}, u32[]{:S(2)}) %collective-permute-start.23) | collective-permute-done | bytes 49184 | tf_op jit(solution)/shard_map/ppermute | solution.py:327
  230.6 5.2 %collective-permute-done.24 = bf16[192,128]{1,0:T(8,128)(2,1)S(1)} collective-permute-done((bf16[192,128]{1,0:T(8,128)(2,1)S(1)}, bf16[192,128]{1,0:T(8,128)(2,1)S(1)}, u32[]{:S(2)}, u32[]{:S(2)}) %collective-permute-start.24) | collective-permute-done | bytes 49184 | tf_op jit(solution)/shard_map/ppermute | solution.py:327
  235.7 1.3 collective-permute-start.25
  237.0 4.6 %collective-permute-done.25 = bf16[192,128]{1,0:T(8,128)(2,1)S(1)} collective-permute-done((bf16[192,128]{1,0:T(8,128)(2,1)S(1)}, bf16[192,128]{1,0:T(8,128)(2,1)S(1)}, u32[]{:S(2)}, u32[]{:S(2)}) %collective-permute-start.25) | collective-permute-done | bytes 49184 | tf_op jit(solution)/shard_map/ppermute | solution.py:327
  241.6 4.1 %collective-permute-done.13 = bf16[192,128]{1,0:T(8,128)(2,1)S(1)} collective-permute-done((bf16[192,128]{1,0:T(8,128)(2,1)S(1)}, bf16[192,128]{1,0:T(8,128)(2,1)S(1)}, u32[]{:S(2)}, u32[]{:S(2)}) %collective-permute-start.13) | collective-permute-done | bytes 49184 | tf_op jit(solution)/shard_map/ppermute | solution.py:327
  245.7 5.0 %collective-permute-done.14 = bf16[192,128]{1,0:T(8,128)(2,1)S(1)} collective-permute-done((bf16[192,128]{1,0:T(8,128)(2,1)S(1)}, bf16[192,128]{1,0:T(8,128)(2,1)S(1)}, u32[]{:S(2)}, u32[]{:S(2)}) %collective-permute-start.14) | collective-permute-done | bytes 49184 | tf_op jit(solution)/shard_map/ppermute | solution.py:327
  250.7 1.4 collective-permute-start.15
  252.1 4.4 %collective-permute-done.15 = bf16[192,128]{1,0:T(8,128)(2,1)S(1)} collective-permute-done((bf16[192,128]{1,0:T(8,128)(2,1)S(1)}, bf16[192,128]{1,0:T(8,128)(2,1)S(1)}, u32[]{:S(2)}, u32[]{:S(2)}) %collective-permute-start.15) | collective-permute-done | bytes 49184 | tf_op jit(solution)/shard_map/ppermute | solution.py:327
  256.6 1.1 collective-permute-start.26
  258.4 3.9 %collective-permute-done.26 = bf16[768,128]{1,0:T(8,128)(2,1)S(1)} collective-permute-done((bf16[768,128]{1,0:T(8,128)(2,1)S(1)}, bf16[768,128]{1,0:T(8,128)(2,1)S(1)}, u32[]{:S(2)}, u32[]{:S(2)}) %collective-permute-start.26) | collective-permute-done | bytes 196640 | tf_op jit(solution)/shard_map/ppermute | solution.py:327
  265.0 5.1 %collective-permute-done.27 = bf16[1536,128]{1,0:T(8,128)(2,1)S(1)} collective-permute-done((bf16[1536,128]{1,0:T(8,128)(2,1)S(1)}, bf16[1536,128]{1,0:T(8,128)(2,1)S(1)}, u32[]{:S(2)}, u32[]{:S(2)}) %collective-permute-start.27) | collective-permute-done | bytes 393248 | tf_op jit(solution)/shard_map/ppermute | solution.py:327
  270.2 1.3 collective-permute-done.17
  271.7 1.6 collective-permute-start.28
  273.4 3.2 %collective-permute-start.50 = (bf16[5120,128]{1,0:T(8,128)(2,1)S(1)}, bf16[5120,128]{1,0:T(8,128)(2,1)S(1)}, u32[]{:S(2)}, u32[]{:S(2)}) collective-permute-start(bf16[5120,128]{1,0:T(8,128)(2,1)S(1)} %pad_maximum_fusion.1.own1), channel_id=1, source_target_pairs={{0,16},{1,17},{2,18},{3,19},{4,20},{5,21},{6,22},{7,23},{8,24},{9,... | collective-permute-start | bytes 3932168 | tf_op jit(solution)/shard_map/ppermute | solution.py:525
  276.6 3.9 %fusion = bf16[1,2,1024,800]{2,3,1,0:T(8,128)(2,1)} fusion(bf16[1,800,1024]{2,1,0:T(8,128)(2,1)} %bitcast.25, bf16[1,800,1024]{2,1,0:T(8,128)(2,1)S(1)} %copy-done.5, pred[]{:T(512)S(6)} %eq.3), kind=kLoop, calls=%fused_computation.1 | loop fusion | flops 4915200 | bytes 6553601 | tf_op jit(solution)/shard_map/broadcast_in_dim | solution.py:536
  280.5 2.0 fusion.1
  283.5 1.1 copy-done.12
  284.7 5.6 %unpack.1 = (f32[400,800]{1,0:T(8,128)}, f32[400,800]{1,0:T(8,128)}, f32[5,400,400]{2,1,0:T(8,128)}, f32[1,800]{1,0:T(1,128)}, f32[1,800]{1,0:T(1,128)}, /*index...) custom-call(s32[1]{0:T(128)} %bitcast.34.index, bf16[6144,128]{1,0:T(8,128)(2,1)} %copy-done.7, ...), custom_call_target="tpu_custom_call" | custom-call | tf_op jit(solution)/shard_map/unpack/pallas_call | solution.py:446
  (174 shorter events, 28.7 us)
Async XLA Ops:
  0.6 8.8 %copy-start = (s32[2,8]{1,0:T(2,128)S(1)}, s32[2,8]{1,0:T(2,128)}, u32[]{:S(2)}) copy-start(s32[2,8]{1,0:T(2,128)} %param.12) | copy-start | bytes 196
  0.7 21.1 %collective-permute-start.4 = (bf16[5,400,400]{2,1,0:T(8,128)(2,1)}, bf16[5,400,400]{2,1,0:T(8,128)(2,1)S(1)}, u32[]{:S(2)}, u32[]{:S(2)}) collective-permute-start(bf16[5,400,400]{2,1,0:T(8,128)(2,1)} %bitcast.60), channel_id=1, source_target_pairs={{0,16},{16,0},{1,17},{17,1},{2,18},{18,2},{3,19},{19,3},{4,20},{20... | collective-permute-start | bytes 4800008 | tf_op jit(solution)/shard_map/ppermute | solution.py:322
  5.6 4.5 %collective-permute-start = (f32[4001]{0:T(1024)S(1)}, f32[4001]{0:T(1024)S(1)}, u32[]{:S(2)}, u32[]{:S(2)}) collective-permute-start(f32[4001]{0:T(1024)S(1)} %concatenate.9), channel_id=1, source_target_pairs={{0,16},{16,0},{1,17},{17,1},{2,18},{18,2},{3,19},{19,3},{4,20},{20... | collective-permute-start | bytes 48020 | tf_op jit(solution)/shard_map/ppermute | solution.py:322
  5.7 3.3 %copy-start.14 = (bf16[1,800,400]{1,2,0:T(8,128)(2,1)S(1)}, bf16[1,800,400]{1,2,0:T(8,128)(2,1)}, u32[]{:S(2)}) copy-start(bf16[1,800,400]{1,2,0:T(8,128)(2,1)} %param.19) | copy-start | bytes 1920004
  5.7 3.3 %copy-start.15 = (bf16[1,400,800]{2,1,0:T(8,128)(2,1)S(1)}, bf16[1,400,800]{2,1,0:T(8,128)(2,1)}, u32[]{:S(2)}) copy-start(bf16[1,400,800]{2,1,0:T(8,128)(2,1)} %param.20) | copy-start | bytes 1920004
  8.5 15.7 %collective-permute-start.1 = (bf16[800,1024]{1,0:T(8,128)(2,1)}, bf16[800,1024]{1,0:T(8,128)(2,1)}, u32[]{:S(2)}, u32[]{:S(2)}) collective-permute-start(bf16[800,1024]{1,0:T(8,128)(2,1)} %dynamic-slice_bitcast_fusion), channel_id=1, source_target_pairs={{0,16},{16,0},{1,17},{17,1},{2,18},{18,2},{3,19},{19,3},{4,20},{20... | collective-permute-start | bytes 4915208 | tf_op jit(solution)/shard_map/ppermute | solution.py:322
  9.0 7.8 %collective-permute-start.2 = (bf16[400,800]{1,0:T(8,128)(2,1)S(1)}, bf16[400,800]{1,0:T(8,128)(2,1)}, u32[]{:S(2)}, u32[]{:S(2)}) collective-permute-start(bf16[400,800]{1,0:T(8,128)(2,1)S(1)} %bitcast.62), channel_id=1, source_target_pairs={{0,16},{16,0},{1,17},{17,1},{2,18},{18,2},{3,19},{19,3},{4,20},{20... | collective-permute-start | bytes 1920008 | tf_op jit(solution)/shard_map/ppermute | solution.py:322
  9.0 10.2 %collective-permute-start.3 = (bf16[400,800]{1,0:T(8,128)(2,1)S(1)}, bf16[400,800]{1,0:T(8,128)(2,1)}, u32[]{:S(2)}, u32[]{:S(2)}) collective-permute-start(bf16[400,800]{1,0:T(8,128)(2,1)S(1)} %bitcast.63), channel_id=1, source_target_pairs={{0,16},{16,0},{1,17},{17,1},{2,18},{18,2},{3,19},{19,3},{4,20},{20... | collective-permute-start | bytes 1920008 | tf_op jit(solution)/shard_map/ppermute | solution.py:322
  19.3 2.5 copy-start.10
  21.7 3.0 %copy-start.9 = (bf16[1,2,1024,800]{2,3,1,0:T(8,128)(2,1)S(1)}, bf16[1,2,1024,800]{2,3,1,0:T(8,128)(2,1)}, u32[]{:S(2)}) copy-start(bf16[1,2,1024,800]{2,3,1,0:T(8,128)(2,1)} %param.11) | copy-start | bytes 9830404
  98.7 2.7 copy-start.6
  98.7 2.7 copy-start.11
  101.3 35.0 %collective-permute-start.29 = (bf16[5120,128]{1,0:T(8,128)(2,1)}, bf16[5120,128]{1,0:T(8,128)(2,1)}, u32[]{:S(2)}, u32[]{:S(2)}) collective-permute-start(bf16[5120,128]{1,0:T(8,128)(2,1)} %pad_dynamic-slice_fusion.2), channel_id=1, source_target_pairs={{0,16},{16,0},{1,17},{17,1},{2,18},{18,2},{3,19},{19,3},{4,20},{20... | collective-permute-start | bytes 3932168 | tf_op jit(solution)/shard_map/ppermute | solution.py:322
  103.4 173.1 %collective-permute-start.5 = (bf16[800,1024]{1,0:T(8,128)(2,1)}, bf16[800,1024]{1,0:T(8,128)(2,1)}, u32[]{:S(2)}, u32[]{:S(2)}) collective-permute-start(bf16[800,1024]{1,0:T(8,128)(2,1)} %get-tuple-element.93), channel_id=1, source_target_pairs={{0,16},{16,0},{1,17},{17,1},{2,18},{18,2},{3,19},{19,3},{4,20},{20... | collective-permute-start | bytes 4915208 | tf_op jit(solution)/shard_map/ppermute | solution.py:322
  103.8 29.6 %copy-start.4 = (bf16[800,1024]{1,0:T(8,128)(2,1)S(1)}, bf16[800,1024]{1,0:T(8,128)(2,1)}, u32[]{:S(2)}) copy-start(bf16[800,1024]{1,0:T(8,128)(2,1)} %get-tuple-element.56.gy) | copy-start | bytes 4915204
  133.5 2.4 copy-start.2
  135.3 145.2 %collective-permute-start.6 = (bf16[800,1024]{1,0:T(8,128)(2,1)S(1)}, bf16[800,1024]{1,0:T(8,128)(2,1)S(1)}, u32[]{:S(2)}, u32[]{:S(2)}) collective-permute-start(bf16[800,1024]{1,0:T(8,128)(2,1)S(1)} %get-tuple-element.91), channel_id=1, source_target_pairs={{0,16},{16,0},{1,17},{17,1},{2,18},{18,2},{3,19},{19,3},{4,20},{20... | collective-permute-start | bytes 4915208 | tf_op jit(solution)/shard_map/ppermute | solution.py:322
  136.1 7.7 %collective-permute-start.7 = (bf16[6144,128]{1,0:T(8,128)(2,1)S(1)}, bf16[6144,128]{1,0:T(8,128)(2,1)S(1)}, u32[]{:S(2)}, u32[]{:S(2)}) collective-permute-start(bf16[6144,128]{1,0:T(8,128)(2,1)S(1)} %pad_dynamic-slice_fusion), channel_id=1, source_target_pairs={{0,16},{16,0},{1,17},{17,1},{2,18},{18,2},{3,19},{19,3},{4,20},{20... | collective-permute-start | bytes 4718600 | tf_op jit(solution)/shard_map/ppermute | solution.py:322
  139.5 11.0 %collective-permute-start.40 = (bf16[1280,128]{1,0:T(8,128)(2,1)S(1)}, bf16[1280,128]{1,0:T(8,128)(2,1)S(1)}, u32[]{:S(2)}, u32[]{:S(2)}) collective-permute-start(bf16[1280,128]{1,0:T(8,128)(2,1)S(1)} %constant_dynamic-slice_fusion.4), channel_id=1, source_target_pairs={{0,2},{1,3},{2,0},{3,1},{4,6},{5,7},{6,4},{7,5},{8,10},{9,11},{10,... | collective-permute-start | bytes 983048 | tf_op jit(solution)/shard_map/ppermute | solution.py:327
  142.2 10.2 %collective-permute-start.30 = (bf16[1280,128]{1,0:T(8,128)(2,1)S(1)}, bf16[1280,128]{1,0:T(8,128)(2,1)S(1)}, u32[]{:S(2)}, u32[]{:S(2)}) collective-permute-start(bf16[1280,128]{1,0:T(8,128)(2,1)S(1)} %constant_dynamic-slice_fusion.9), channel_id=1, source_target_pairs={{0,1},{1,0},{2,3},{3,2},{4,5},{5,4},{6,7},{7,6},{8,9},{9,8},{10,11... | collective-permute-start | bytes 983048 | tf_op jit(solution)/shard_map/ppermute | solution.py:327
  150.6 6.1 %collective-permute-start.41 = (bf16[640,128]{1,0:T(8,128)(2,1)S(1)}, bf16[640,128]{1,0:T(8,128)(2,1)S(1)}, u32[]{:S(2)}, u32[]{:S(2)}) collective-permute-start(bf16[640,128]{1,0:T(8,128)(2,1)S(1)} %constant_dynamic-slice_fusion.3), channel_id=1, source_target_pairs={{0,1},{1,0},{2,3},{3,2},{4,5},{5,4},{6,7},{7,6},{8,9},{9,8},{10,11... | collective-permute-start | bytes 491528 | tf_op jit(solution)/shard_map/ppermute | solution.py:327
  152.5 7.9 %collective-permute-start.31 = (bf16[640,128]{1,0:T(8,128)(2,1)S(1)}, bf16[640,128]{1,0:T(8,128)(2,1)S(1)}, u32[]{:S(2)}, u32[]{:S(2)}) collective-permute-start(bf16[640,128]{1,0:T(8,128)(2,1)S(1)} %constant_dynamic-slice_fusion.8), channel_id=1, source_target_pairs={{0,2},{1,3},{2,0},{3,1},{4,6},{5,7},{6,4},{7,5},{8,10},{9,11},{10,... | collective-permute-start | bytes 491528 | tf_op jit(solution)/shard_map/ppermute | solution.py:327
  156.8 5.9 %collective-permute-start.44 = (bf16[160,128]{1,0:T(8,128)(2,1)S(1)}, bf16[160,128]{1,0:T(8,128)(2,1)S(1)}, u32[]{:S(2)}, u32[]{:S(2)}) collective-permute-start(bf16[160,128]{1,0:T(8,128)(2,1)S(1)} %get-tuple-element.112), channel_id=1, source_target_pairs={{0,12},{1,13},{2,14},{3,15},{4,8},{5,9},{6,10},{7,11},{8,4},{9,5},... | collective-permute-start | bytes 122888 | tf_op jit(solution)/shard_map/ppermute | solution.py:327
  160.5 5.9 %collective-permute-start.43 = (bf16[160,128]{1,0:T(8,128)(2,1)S(1)}, bf16[160,128]{1,0:T(8,128)(2,1)S(1)}, u32[]{:S(2)}, u32[]{:S(2)}) collective-permute-start(bf16[160,128]{1,0:T(8,128)(2,1)S(1)} %get-tuple-element.113), channel_id=1, source_target_pairs={{0,8},{1,9},{2,10},{3,11},{4,12},{5,13},{6,14},{7,15},{8,0},{9,1},... | collective-permute-start | bytes 122888 | tf_op jit(solution)/shard_map/ppermute | solution.py:327
  160.5 5.9 %collective-permute-start.42 = (bf16[160,128]{1,0:T(8,128)(2,1)S(1)}, bf16[160,128]{1,0:T(8,128)(2,1)S(1)}, u32[]{:S(2)}, u32[]{:S(2)}) collective-permute-start(bf16[160,128]{1,0:T(8,128)(2,1)S(1)} %get-tuple-element.111), channel_id=1, source_target_pairs={{0,4},{1,5},{2,6},{3,7},{4,0},{5,1},{6,2},{7,3},{8,12},{9,13},{10,... | collective-permute-start | bytes 122888 | tf_op jit(solution)/shard_map/ppermute | solution.py:327
  162.7 5.9 %collective-permute-start.34 = (bf16[160,128]{1,0:T(8,128)(2,1)S(1)}, bf16[160,128]{1,0:T(8,128)(2,1)S(1)}, u32[]{:S(2)}, u32[]{:S(2)}) collective-permute-start(bf16[160,128]{1,0:T(8,128)(2,1)S(1)} %get-tuple-element.109), channel_id=1, source_target_pairs={{0,12},{1,13},{2,14},{3,15},{4,8},{5,9},{6,10},{7,11},{8,4},{9,5},... | collective-permute-start | bytes 122888 | tf_op jit(solution)/shard_map/ppermute | solution.py:327
  166.4 4.9 %collective-permute-start.33 = (bf16[160,128]{1,0:T(8,128)(2,1)S(1)}, bf16[160,128]{1,0:T(8,128)(2,1)S(1)}, u32[]{:S(2)}, u32[]{:S(2)}) collective-permute-start(bf16[160,128]{1,0:T(8,128)(2,1)S(1)} %get-tuple-element.110), channel_id=1, source_target_pairs={{0,8},{1,9},{2,10},{3,11},{4,12},{5,13},{6,14},{7,15},{8,0},{9,1},... | collective-permute-start | bytes 122888 | tf_op jit(solution)/shard_map/ppermute | solution.py:327
  166.4 6.4 %collective-permute-start.32 = (bf16[160,128]{1,0:T(8,128)(2,1)S(1)}, bf16[160,128]{1,0:T(8,128)(2,1)S(1)}, u32[]{:S(2)}, u32[]{:S(2)}) collective-permute-start(bf16[160,128]{1,0:T(8,128)(2,1)S(1)} %get-tuple-element.108), channel_id=1, source_target_pairs={{0,4},{1,5},{2,6},{3,7},{4,0},{5,1},{6,2},{7,3},{8,12},{9,13},{10,... | collective-permute-start | bytes 122888 | tf_op jit(solution)/shard_map/ppermute | solution.py:327
  168.6 35.1 %collective-permute-start.18 = (bf16[1536,128]{1,0:T(8,128)(2,1)S(1)}, bf16[1536,128]{1,0:T(8,128)(2,1)S(1)}, u32[]{:S(2)}, u32[]{:S(2)}) collective-permute-start(bf16[1536,128]{1,0:T(8,128)(2,1)S(1)} %constant_dynamic-slice_fusion.14), channel_id=1, source_target_pairs={{0,2},{1,3},{2,0},{3,1},{4,6},{5,7},{6,4},{7,5},{8,10},{9,11},{10,... | collective-permute-start | bytes 1179656 | tf_op jit(solution)/shard_map/ppermute | solution.py:327
  171.3 33.8 %collective-permute-start.8 = (bf16[1536,128]{1,0:T(8,128)(2,1)S(1)}, bf16[1536,128]{1,0:T(8,128)(2,1)S(1)}, u32[]{:S(2)}, u32[]{:S(2)}) collective-permute-start(bf16[1536,128]{1,0:T(8,128)(2,1)S(1)} %constant_dynamic-slice_fusion.19), channel_id=1, source_target_pairs={{0,1},{1,0},{2,3},{3,2},{4,5},{5,4},{6,7},{7,6},{8,9},{9,8},{10,11... | collective-permute-start | bytes 1179656 | tf_op jit(solution)/shard_map/ppermute | solution.py:327
  172.8 4.0 %collective-permute-start.45 = (bf16[160,128]{1,0:T(8,128)(2,1)S(1)}, bf16[160,128]{1,0:T(8,128)(2,1)S(1)}, u32[]{:S(2)}, u32[]{:S(2)}) collective-permute-start(bf16[160,128]{1,0:T(8,128)(2,1)S(1)} %get-tuple-element.81), channel_id=1, source_target_pairs={{0,4},{1,5},{2,6},{3,7},{4,0},{5,1},{6,2},{7,3},{8,12},{9,13},{10,... | collective-permute-start | bytes 122888 | tf_op jit(solution)/shard_map/ppermute | solution.py:327
  176.8 4.9 %collective-permute-start.46 = (bf16[160,128]{1,0:T(8,128)(2,1)S(1)}, bf16[160,128]{1,0:T(8,128)(2,1)S(1)}, u32[]{:S(2)}, u32[]{:S(2)}) collective-permute-start(bf16[160,128]{1,0:T(8,128)(2,1)S(1)} %get-tuple-element.81), channel_id=1, source_target_pairs={{0,8},{1,9},{2,10},{3,11},{4,12},{5,13},{6,14},{7,15},{8,0},{9,1},... | collective-permute-start | bytes 122888 | tf_op jit(solution)/shard_map/ppermute | solution.py:327
  181.7 5.8 %collective-permute-start.47 = (bf16[160,128]{1,0:T(8,128)(2,1)S(1)}, bf16[160,128]{1,0:T(8,128)(2,1)S(1)}, u32[]{:S(2)}, u32[]{:S(2)}) collective-permute-start(bf16[160,128]{1,0:T(8,128)(2,1)S(1)} %get-tuple-element.81), channel_id=1, source_target_pairs={{0,12},{1,13},{2,14},{3,15},{4,8},{5,9},{6,10},{7,11},{8,4},{9,5},... | collective-permute-start | bytes 122888 | tf_op jit(solution)/shard_map/ppermute | solution.py:327
  187.5 4.0 %collective-permute-start.35 = (bf16[160,128]{1,0:T(8,128)(2,1)S(1)}, bf16[160,128]{1,0:T(8,128)(2,1)S(1)}, u32[]{:S(2)}, u32[]{:S(2)}) collective-permute-start(bf16[160,128]{1,0:T(8,128)(2,1)S(1)} %get-tuple-element.79), channel_id=1, source_target_pairs={{0,4},{1,5},{2,6},{3,7},{4,0},{5,1},{6,2},{7,3},{8,12},{9,13},{10,... | collective-permute-start | bytes 122888 | tf_op jit(solution)/shard_map/ppermute | solution.py:327
  191.5 4.9 %collective-permute-start.36 = (bf16[160,128]{1,0:T(8,128)(2,1)S(1)}, bf16[160,128]{1,0:T(8,128)(2,1)S(1)}, u32[]{:S(2)}, u32[]{:S(2)}) collective-permute-start(bf16[160,128]{1,0:T(8,128)(2,1)S(1)} %get-tuple-element.79), channel_id=1, source_target_pairs={{0,8},{1,9},{2,10},{3,11},{4,12},{5,13},{6,14},{7,15},{8,0},{9,1},... | collective-permute-start | bytes 122888 | tf_op jit(solution)/shard_map/ppermute | solution.py:327
  196.4 5.8 %collective-permute-start.37 = (bf16[160,128]{1,0:T(8,128)(2,1)S(1)}, bf16[160,128]{1,0:T(8,128)(2,1)S(1)}, u32[]{:S(2)}, u32[]{:S(2)}) collective-permute-start(bf16[160,128]{1,0:T(8,128)(2,1)S(1)} %get-tuple-element.79), channel_id=1, source_target_pairs={{0,12},{1,13},{2,14},{3,15},{4,8},{5,9},{6,10},{7,11},{8,4},{9,5},... | collective-permute-start | bytes 122888 | tf_op jit(solution)/shard_map/ppermute | solution.py:327
  202.2 5.3 %collective-permute-start.48 = (bf16[640,128]{1,0:T(8,128)(2,1)S(1)}, bf16[640,128]{1,0:T(8,128)(2,1)S(1)}, u32[]{:S(2)}, u32[]{:S(2)}) collective-permute-start(bf16[640,128]{1,0:T(8,128)(2,1)S(1)} %constant_dynamic-update-slice_fusion.4), channel_id=1, source_target_pairs={{0,1},{1,0},{2,3},{3,2},{4,5},{5,4},{6,7},{7,6},{8,9},{9,8},{10,11... | collective-permute-start | bytes 491528 | tf_op jit(solution)/shard_map/ppermute | solution.py:327
  203.7 6.0 %collective-permute-start.38 = (bf16[640,128]{1,0:T(8,128)(2,1)S(1)}, bf16[640,128]{1,0:T(8,128)(2,1)S(1)}, u32[]{:S(2)}, u32[]{:S(2)}) collective-permute-start(bf16[640,128]{1,0:T(8,128)(2,1)S(1)} %constant_dynamic-update-slice_fusion.12), channel_id=1, source_target_pairs={{0,2},{1,3},{2,0},{3,1},{4,6},{5,7},{6,4},{7,5},{8,10},{9,11},{10,... | collective-permute-start | bytes 491528 | tf_op jit(solution)/shard_map/ppermute | solution.py:327
  205.1 5.7 %collective-permute-start.19 = (bf16[768,128]{1,0:T(8,128)(2,1)S(1)}, bf16[768,128]{1,0:T(8,128)(2,1)S(1)}, u32[]{:S(2)}, u32[]{:S(2)}) collective-permute-start(bf16[768,128]{1,0:T(8,128)(2,1)S(1)} %constant_dynamic-slice_fusion.13), channel_id=1, source_target_pairs={{0,1},{1,0},{2,3},{3,2},{4,5},{5,4},{6,7},{7,6},{8,9},{9,8},{10,11... | collective-permute-start | bytes 589832 | tf_op jit(solution)/shard_map/ppermute | solution.py:327
  207.6 7.4 %collective-permute-start.9 = (bf16[768,128]{1,0:T(8,128)(2,1)S(1)}, bf16[768,128]{1,0:T(8,128)(2,1)S(1)}, u32[]{:S(2)}, u32[]{:S(2)}) collective-permute-start(bf16[768,128]{1,0:T(8,128)(2,1)S(1)} %constant_dynamic-slice_fusion.18), channel_id=1, source_target_pairs={{0,2},{1,3},{2,0},{3,1},{4,6},{5,7},{6,4},{7,5},{8,10},{9,11},{10,... | collective-permute-start | bytes 589832 | tf_op jit(solution)/shard_map/ppermute | solution.py:327
  211.0 6.0 %collective-permute-start.22 = (bf16[192,128]{1,0:T(8,128)(2,1)S(1)}, bf16[192,128]{1,0:T(8,128)(2,1)S(1)}, u32[]{:S(2)}, u32[]{:S(2)}) collective-permute-start(bf16[192,128]{1,0:T(8,128)(2,1)S(1)} %get-tuple-element.106), channel_id=1, source_target_pairs={{0,12},{1,13},{2,14},{3,15},{4,8},{5,9},{6,10},{7,11},{8,4},{9,5},... | collective-permute-start | bytes 147464 | tf_op jit(solution)/shard_map/ppermute | solution.py:327
  212.8 6.3 %collective-permute-start.21 = (bf16[192,128]{1,0:T(8,128)(2,1)S(1)}, bf16[192,128]{1,0:T(8,128)(2,1)S(1)}, u32[]{:S(2)}, u32[]{:S(2)}) collective-permute-start(bf16[192,128]{1,0:T(8,128)(2,1)S(1)} %get-tuple-element.107), channel_id=1, source_target_pairs={{0,8},{1,9},{2,10},{3,11},{4,12},{5,13},{6,14},{7,15},{8,0},{9,1},... | collective-permute-start | bytes 147464 | tf_op jit(solution)/shard_map/ppermute | solution.py:327
  215.0 4.6 %collective-permute-start.20 = (bf16[192,128]{1,0:T(8,128)(2,1)S(1)}, bf16[192,128]{1,0:T(8,128)(2,1)S(1)}, u32[]{:S(2)}, u32[]{:S(2)}) collective-permute-start(bf16[192,128]{1,0:T(8,128)(2,1)S(1)} %get-tuple-element.105), channel_id=1, source_target_pairs={{0,4},{1,5},{2,6},{3,7},{4,0},{5,1},{6,2},{7,3},{8,12},{9,13},{10,... | collective-permute-start | bytes 147464 | tf_op jit(solution)/shard_map/ppermute | solution.py:327
  216.9 5.9 %collective-permute-start.12 = (bf16[192,128]{1,0:T(8,128)(2,1)S(1)}, bf16[192,128]{1,0:T(8,128)(2,1)S(1)}, u32[]{:S(2)}, u32[]{:S(2)}) collective-permute-start(bf16[192,128]{1,0:T(8,128)(2,1)S(1)} %get-tuple-element.103), channel_id=1, source_target_pairs={{0,12},{1,13},{2,14},{3,15},{4,8},{5,9},{6,10},{7,11},{8,4},{9,5},... | collective-permute-start | bytes 147464 | tf_op jit(solution)/shard_map/ppermute | solution.py:327
  219.1 5.6 %collective-permute-start.11 = (bf16[192,128]{1,0:T(8,128)(2,1)S(1)}, bf16[192,128]{1,0:T(8,128)(2,1)S(1)}, u32[]{:S(2)}, u32[]{:S(2)}) collective-permute-start(bf16[192,128]{1,0:T(8,128)(2,1)S(1)} %get-tuple-element.104), channel_id=1, source_target_pairs={{0,8},{1,9},{2,10},{3,11},{4,12},{5,13},{6,14},{7,15},{8,0},{9,1},... | collective-permute-start | bytes 147464 | tf_op jit(solution)/shard_map/ppermute | solution.py:327
  219.5 6.9 %collective-permute-start.10 = (bf16[192,128]{1,0:T(8,128)(2,1)S(1)}, bf16[192,128]{1,0:T(8,128)(2,1)S(1)}, u32[]{:S(2)}, u32[]{:S(2)}) collective-permute-start(bf16[192,128]{1,0:T(8,128)(2,1)S(1)} %get-tuple-element.102), channel_id=1, source_target_pairs={{0,4},{1,5},{2,6},{3,7},{4,0},{5,1},{6,2},{7,3},{8,12},{9,13},{10,... | collective-permute-start | bytes 147464 | tf_op jit(solution)/shard_map/ppermute | solution.py:327
  222.8 35.1 %collective-permute-start.49 = (bf16[1280,128]{1,0:T(8,128)(2,1)S(1)}, bf16[1280,128]{1,0:T(8,128)(2,1)S(1)}, u32[]{:S(2)}, u32[]{:S(2)}) collective-permute-start(bf16[1280,128]{1,0:T(8,128)(2,1)S(1)} %constant_dynamic-update-slice_fusion.2), channel_id=1, source_target_pairs={{0,2},{1,3},{2,0},{3,1},{4,6},{5,7},{6,4},{7,5},{8,10},{9,11},{10,... | collective-permute-start | bytes 983048 | tf_op jit(solution)/shard_map/ppermute | solution.py:327
  224.6 33.7 %collective-permute-start.39 = (bf16[1280,128]{1,0:T(8,128)(2,1)S(1)}, bf16[1280,128]{1,0:T(8,128)(2,1)S(1)}, u32[]{:S(2)}, u32[]{:S(2)}) collective-permute-start(bf16[1280,128]{1,0:T(8,128)(2,1)S(1)} %constant_dynamic-update-slice_fusion.10), channel_id=1, source_target_pairs={{0,1},{1,0},{2,3},{3,2},{4,5},{5,4},{6,7},{7,6},{8,9},{9,8},{10,11... | collective-permute-start | bytes 983048 | tf_op jit(solution)/shard_map/ppermute | solution.py:327
  226.5 4.1 %collective-permute-start.23 = (bf16[192,128]{1,0:T(8,128)(2,1)S(1)}, bf16[192,128]{1,0:T(8,128)(2,1)S(1)}, u32[]{:S(2)}, u32[]{:S(2)}) collective-permute-start(bf16[192,128]{1,0:T(8,128)(2,1)S(1)} %get-tuple-element.85), channel_id=1, source_target_pairs={{0,4},{1,5},{2,6},{3,7},{4,0},{5,1},{6,2},{7,3},{8,12},{9,13},{10,... | collective-permute-start | bytes 147464 | tf_op jit(solution)/shard_map/ppermute | solution.py:327
  230.5 5.2 %collective-permute-start.24 = (bf16[192,128]{1,0:T(8,128)(2,1)S(1)}, bf16[192,128]{1,0:T(8,128)(2,1)S(1)}, u32[]{:S(2)}, u32[]{:S(2)}) collective-permute-start(bf16[192,128]{1,0:T(8,128)(2,1)S(1)} %get-tuple-element.85), channel_id=1, source_target_pairs={{0,8},{1,9},{2,10},{3,11},{4,12},{5,13},{6,14},{7,15},{8,0},{9,1},... | collective-permute-start | bytes 147464 | tf_op jit(solution)/shard_map/ppermute | solution.py:327
  235.7 5.9 %collective-permute-start.25 = (bf16[192,128]{1,0:T(8,128)(2,1)S(1)}, bf16[192,128]{1,0:T(8,128)(2,1)S(1)}, u32[]{:S(2)}, u32[]{:S(2)}) collective-permute-start(bf16[192,128]{1,0:T(8,128)(2,1)S(1)} %get-tuple-element.85), channel_id=1, source_target_pairs={{0,12},{1,13},{2,14},{3,15},{4,8},{5,9},{6,10},{7,11},{8,4},{9,5},... | collective-permute-start | bytes 147464 | tf_op jit(solution)/shard_map/ppermute | solution.py:327
  241.6 4.1 %collective-permute-start.13 = (bf16[192,128]{1,0:T(8,128)(2,1)S(1)}, bf16[192,128]{1,0:T(8,128)(2,1)S(1)}, u32[]{:S(2)}, u32[]{:S(2)}) collective-permute-start(bf16[192,128]{1,0:T(8,128)(2,1)S(1)} %get-tuple-element.83), channel_id=1, source_target_pairs={{0,4},{1,5},{2,6},{3,7},{4,0},{5,1},{6,2},{7,3},{8,12},{9,13},{10,... | collective-permute-start | bytes 147464 | tf_op jit(solution)/shard_map/ppermute | solution.py:327
  245.7 5.0 %collective-permute-start.14 = (bf16[192,128]{1,0:T(8,128)(2,1)S(1)}, bf16[192,128]{1,0:T(8,128)(2,1)S(1)}, u32[]{:S(2)}, u32[]{:S(2)}) collective-permute-start(bf16[192,128]{1,0:T(8,128)(2,1)S(1)} %get-tuple-element.83), channel_id=1, source_target_pairs={{0,8},{1,9},{2,10},{3,11},{4,12},{5,13},{6,14},{7,15},{8,0},{9,1},... | collective-permute-start | bytes 147464 | tf_op jit(solution)/shard_map/ppermute | solution.py:327
  250.7 5.9 %collective-permute-start.15 = (bf16[192,128]{1,0:T(8,128)(2,1)S(1)}, bf16[192,128]{1,0:T(8,128)(2,1)S(1)}, u32[]{:S(2)}, u32[]{:S(2)}) collective-permute-start(bf16[192,128]{1,0:T(8,128)(2,1)S(1)} %get-tuple-element.83), channel_id=1, source_target_pairs={{0,12},{1,13},{2,14},{3,15},{4,8},{5,9},{6,10},{7,11},{8,4},{9,5},... | collective-permute-start | bytes 147464 | tf_op jit(solution)/shard_map/ppermute | solution.py:327
  256.6 5.7 %collective-permute-start.26 = (bf16[768,128]{1,0:T(8,128)(2,1)S(1)}, bf16[768,128]{1,0:T(8,128)(2,1)S(1)}, u32[]{:S(2)}, u32[]{:S(2)}) collective-permute-start(bf16[768,128]{1,0:T(8,128)(2,1)S(1)} %constant_dynamic-update-slice_fusion.20), channel_id=1, source_target_pairs={{0,1},{1,0},{2,3},{3,2},{4,5},{5,4},{6,7},{7,6},{8,9},{9,8},{10,11... | collective-permute-start | bytes 589832 | tf_op jit(solution)/shard_map/ppermute | solution.py:327
  257.9 5.7 %collective-permute-start.16 = (bf16[768,128]{1,0:T(8,128)(2,1)S(1)}, bf16[768,128]{1,0:T(8,128)(2,1)S(1)}, u32[]{:S(2)}, u32[]{:S(2)}) collective-permute-start(bf16[768,128]{1,0:T(8,128)(2,1)S(1)} %constant_dynamic-update-slice_fusion.28), channel_id=1, source_target_pairs={{0,2},{1,3},{2,0},{3,1},{4,6},{5,7},{6,4},{7,5},{8,10},{9,11},{10,... | collective-permute-start | bytes 589832 | tf_op jit(solution)/shard_map/ppermute | solution.py:327
  262.3 7.8 %collective-permute-start.27 = (bf16[1536,128]{1,0:T(8,128)(2,1)S(1)}, bf16[1536,128]{1,0:T(8,128)(2,1)S(1)}, u32[]{:S(2)}, u32[]{:S(2)}) collective-permute-start(bf16[1536,128]{1,0:T(8,128)(2,1)S(1)} %constant_dynamic-update-slice_fusion.18), channel_id=1, source_target_pairs={{0,2},{1,3},{2,0},{3,1},{4,6},{5,7},{6,4},{7,5},{8,10},{9,11},{10,... | collective-permute-start | bytes 1179656 | tf_op jit(solution)/shard_map/ppermute | solution.py:327
  263.7 7.8 %collective-permute-start.17 = (bf16[1536,128]{1,0:T(8,128)(2,1)S(1)}, bf16[1536,128]{1,0:T(8,128)(2,1)S(1)}, u32[]{:S(2)}, u32[]{:S(2)}) collective-permute-start(bf16[1536,128]{1,0:T(8,128)(2,1)S(1)} %constant_dynamic-update-slice_fusion.26), channel_id=1, source_target_pairs={{0,1},{1,0},{2,3},{3,2},{4,5},{5,4},{6,7},{7,6},{8,9},{9,8},{10,11... | collective-permute-start | bytes 1179656 | tf_op jit(solution)/shard_map/ppermute | solution.py:327
  271.7 8.8 %copy-start.7 = (bf16[6144,128]{1,0:T(8,128)(2,1)}, bf16[6144,128]{1,0:T(8,128)(2,1)S(1)}, u32[]{:S(2)}) copy-start(bf16[6144,128]{1,0:T(8,128)(2,1)S(1)} %pad_maximum_fusion.own0) | copy-start | bytes 4718596
  271.7 4.9 %copy-start.5 = (bf16[1,800,1024]{2,1,0:T(8,128)(2,1)S(1)}, bf16[1,800,1024]{2,1,0:T(8,128)(2,1)}, u32[]{:S(2)}) copy-start(bf16[1,800,1024]{2,1,0:T(8,128)(2,1)} %get-tuple-element.92) | copy-start | bytes 4915204
  271.7 10.8 %collective-permute-start.28 = (bf16[6144,128]{1,0:T(8,128)(2,1)S(1)}, bf16[6144,128]{1,0:T(8,128)(2,1)S(1)}, u32[]{:S(2)}, u32[]{:S(2)}) collective-permute-start(bf16[6144,128]{1,0:T(8,128)(2,1)S(1)} %pad_maximum_fusion.own0), channel_id=1, source_target_pairs={{16,0},{17,1},{18,2},{19,3},{20,4},{21,5},{22,6},{23,7},{24,8},{25... | collective-permute-start | bytes 4718600 | tf_op jit(solution)/shard_map/ppermute | solution.py:530
  273.3 7.2 %copy-start.8 = (bf16[5120,128]{1,0:T(8,128)(2,1)}, bf16[5120,128]{1,0:T(8,128)(2,1)S(1)}, u32[]{:S(2)}) copy-start(bf16[5120,128]{1,0:T(8,128)(2,1)S(1)} %pad_maximum_fusion.1.own1) | copy-start | bytes 3932164
  273.4 9.1 %collective-permute-start.50 = (bf16[5120,128]{1,0:T(8,128)(2,1)S(1)}, bf16[5120,128]{1,0:T(8,128)(2,1)S(1)}, u32[]{:S(2)}, u32[]{:S(2)}) collective-permute-start(bf16[5120,128]{1,0:T(8,128)(2,1)S(1)} %pad_maximum_fusion.1.own1), channel_id=1, source_target_pairs={{0,16},{1,17},{2,18},{3,19},{4,20},{5,21},{6,22},{7,23},{8,24},{9,... | collective-permute-start | bytes 3932168 | tf_op jit(solution)/shard_map/ppermute | solution.py:525
  283.5 6.8 %copy-start.1 = (s32[2,8]{1,0:T(2,128)S(1)}, s32[2,8]{1,0:T(2,128)}, u32[]{:S(2)}) copy-start(s32[2,8]{1,0:T(2,128)} %param.12) | copy-start | bytes 196
  (3 other events, 3.9 us)

commit v2 on v0

v2 whole, which is shorter than its diff:
```python
import functools

import jax
import jax.numpy as jnp
from jax import lax
from jax.experimental import pallas as pl
from jax.experimental.pallas import tpu as pltpu
from jax.sharding import PartitionSpec as P

DEC_TAPS = 3
EPS = 1e-05
LANES = 128
CHUNK = 80
VEC_ROWS = 48
SMALL_ROWS = 8
BF = jnp.bfloat16
F32 = jnp.float32
VMEM_LIMIT = 62 * 2**20
ANY = pl.BlockSpec(memory_space=pl.ANY)
SMEM = pl.BlockSpec(memory_space=pltpu.SMEM)
VMEM = pl.BlockSpec(memory_space=pltpu.VMEM)


def shape(dims, dtype):
    return jax.ShapeDtypeStruct(tuple(dims), dtype)


def nn(left, right):
    return jnp.dot(left, right, preferred_element_type=F32)


def nt(left, right):
    return lax.dot_general(left, right, (((1,), (1,)), ((), ())), preferred_element_type=F32)


def lane_block(index):
    return pl.ds(pl.multiple_of(index * LANES, LANES), LANES)


def chunks(rows):
    size = CHUNK if rows % CHUNK == 0 else 16
    return [slice(at, at + size) for at in range(0, rows, size)]


def folded(values):
    return jnp.sum(values.reshape(values.shape[0] // 8, 8, values.shape[1]), 0)


def column(vector):
    return jnp.broadcast_to(vector, (LANES, vector.shape[1])).T


def norm_forward(source, half_gain, half_bias, normed, slope, hidden, devs, row):
    feats, tokens = source.shape
    scale = 1.0 / feats

    def stats(unit):
        here = lane_block(unit)
        base = source[0:1, here].astype(F32)
        total = jnp.zeros((8, LANES), F32)
        squares = jnp.zeros((8, LANES), F32)
        for part in chunks(feats):
            moved = source[part, here].astype(F32) - base
            total = total + folded(moved)
            squares = squares + folded(moved * moved)
        average = jnp.sum(total, 0, keepdims=True) * scale
        variance = jnp.sum(squares, 0, keepdims=True) * scale - average * average
        inverse_dev = lax.rsqrt(jnp.maximum(variance, 0.0) + EPS)
        return (average + base) * inverse_dev, inverse_dev

    def body(unit, carry):
        following = stats(jnp.minimum(unit + 1, tokens // LANES - 1))
        offset, inverse_dev = carry
        here = lane_block(unit)
        devs[row : row + 1, here] = inverse_dev
        for part in chunks(feats):
            values = source[part, here].astype(F32) * inverse_dev - offset
            gain = half_gain[part, :]
            half = values * gain + half_bias[part, :]
            tan = jnp.tanh(half)
            weight = 1.0 + tan
            out = half * weight
            normed[part, here] = values.astype(BF)
            slope[part, here] = ((weight + out * (1.0 - tan)) * gain).astype(BF)
            hidden[part, here] = out.astype(hidden.dtype)
        return following

    lax.fori_loop(0, tokens // LANES, body, stats(0))


def norm_backward(gradient, slope, normed, devs, row, gain_sums, bias_sums, emit):
    feats, tokens = gradient.shape
    scale = 1.0 / feats
    for part in chunks(feats):
        gain_sums[part, :] = jnp.zeros_like(gain_sums[part, :])
        bias_sums[part, :] = jnp.zeros_like(bias_sums[part, :])

    def means(unit):
        here = lane_block(unit)
        first = jnp.zeros((8, LANES), F32)
        second = jnp.zeros((8, LANES), F32)
        for part in chunks(feats):
            scaled = gradient[part, here] * slope[part, here].astype(F32)
            weighted = scaled * normed[part, here].astype(F32)
            gain_sums[part, :] += weighted
            bias_sums[part, :] += scaled
            first = first + folded(scaled)
            second = second + folded(weighted)
        return jnp.sum(first, 0, keepdims=True) * scale, jnp.sum(second, 0, keepdims=True) * scale

    def finish(unit, first, second):
        here = lane_block(unit)
        inverse_dev = devs[row : row + 1, here]
        first = first * inverse_dev
        second = second * inverse_dev
        for part in chunks(feats):
            scaled = gradient[part, here] * slope[part, here].astype(F32)
            emit(part, here, scaled * inverse_dev - first - normed[part, here].astype(F32) * second)

    def body(unit, carry):
        following = means(unit + 1)
        finish(unit, *carry)
        return following

    last = tokens // LANES - 1
    finish(last, *lax.fori_loop(0, last, body, means(0)))


def write_shifts(source, target, begins, offsets):
    feats, tokens = source.shape
    units = tokens // LANES

    def body(unit, _):
        here = lane_block(unit)
        behind_unit = jnp.maximum(unit - 1, 0)
        ahead_unit = jnp.minimum(unit + 1, units - 1)
        joined_behind = ((unit > 0) & (begins(unit) == 0)).astype(F32)
        joined_ahead = ((unit < units - 1) & (begins(ahead_unit) == 0)).astype(F32)
        for part in chunks(feats):
            size = part.stop - part.start
            lane = lax.broadcasted_iota(jnp.int32, (size, LANES), 1)
            current = source[part, here].astype(F32)
            behind = source[part, lane_block(behind_unit)].astype(F32) * joined_behind
            ahead = source[part, lane_block(ahead_unit)].astype(F32) * joined_ahead
            for position, (sign, step) in enumerate(offsets):
                if sign == 0:
                    moved = current
                elif sign < 0:
                    moved = pltpu.roll(jnp.where(lane < LANES - step, current, behind), step, 1)
                else:
                    moved = pltpu.roll(jnp.where(lane >= step, current, ahead), LANES - step, 1)
                target[feats * position + part.start : feats * position + part.stop, here] = moved.astype(BF)
        return 0

    lax.fori_loop(0, units, body, 0, unroll=2)


def tap_offsets(taps, dilation, flip):
    result = []
    for position in range(taps):
        factor = (position - 2) * (-1 if flip else 1)
        result.append(((factor > 0) - (factor < 0), abs(factor) * dilation))
    return result


def layout(taps, width, inner):
    wide = pl.cdiv(width, LANES) * inner
    taps_at = wide
    tails_at = taps_at + taps * (inner // LANES) * inner
    w_in_at = tails_at + inner
    vec_at = w_in_at + wide
    return taps_at, tails_at, w_in_at, vec_at, vec_at + VEC_ROWS


def scatter_groups(count, full):
    total = count.bit_length() - 1
    rest = [list(range(2, min(4, total)))] if full and total > 2 else []
    return [[[bit] for bit in bits if bit < total] + rest for bits in ((0, 1), (1, 0))]


def share_count(groups):
    return 2 ** sum(len(bits) for bits in groups)


def padded_rows(taps, width, inner, groups):
    unit = 2 * 16 * share_count(groups[0])
    return pl.cdiv(layout(taps, width, inner)[-1], unit) * unit


def put_slabs(buf, row, matrix):
    rows, cols = matrix.shape
    for q in range(pl.cdiv(cols, LANES)):
        part = matrix[:, LANES * q : min(cols, LANES * (q + 1))]
        if part.shape[1] < LANES:
            part = jnp.concatenate([part, jnp.zeros((rows, LANES - part.shape[1]), F32)], 1)
        buf[row + q * rows : row + (q + 1) * rows, :] = part.astype(BF)


def put_taps(buf, taps, width, shifted, grad_mixed):
    inner = grad_mixed.shape[0]
    taps_at, tails_at, _, _, _ = layout(taps, width, inner)
    whole = inner // LANES
    tail = inner - whole * LANES
    for k in range(taps):
        grad = nt(shifted[inner * k : inner * (k + 1), :], grad_mixed[...])
        for q in range(whole):
            at = taps_at + inner * (whole * k + q)
            buf[at : at + inner, :] = grad[:, LANES * q : LANES * (q + 1)].astype(BF)
        buf[tails_at : tails_at + inner, tail * k : tail * (k + 1)] = grad[:, LANES * whole :].astype(BF)
    buf[tails_at : tails_at + inner, tail * taps :] = jnp.zeros((inner, LANES - tail * taps), BF)


def row_sums(acc):
    return lax.dot_general(
        jnp.ones((8, LANES), F32), acc, (((1,), (1,)), ((), ())),
        precision=lax.Precision.HIGHEST, preferred_element_type=F32,
    )[0:1]


def put_vectors(buf, at, vec, sums):
    vec[...] = jnp.zeros_like(vec)
    row = 0
    for total in sums:
        for lane in range(0, total.shape[1], LANES):
            part = total[:, lane : lane + LANES]
            vec[row : row + 1, 0 : part.shape[1]] = part
            row += 1
    buf[at : at + VEC_ROWS, :] = vec[...].astype(BF)


def relative_index(position, groups):
    result = 0
    for bits in reversed(groups):
        size = 2 ** len(bits)
        result = result + (position & (size - 1)) * 2 ** bits[0]
        position = position >> len(bits)
    return result


def owner_of(position, side, groups, index):
    both = [relative_index(position, order) for order in groups]
    mask = sum(2**bit for bits in groups[0] for bit in bits)
    return jnp.where(side == 0, both[0], both[1]) ^ (index & mask)


def send_out(buf, keep, send, section, index, groups, sems):
    half = keep.shape[0]
    count = share_count(groups[0])
    share = half // count

    def body(position, _):
        for slot, (target, side) in enumerate(((keep, section), (send, 1 - section))):
            start = side * half + owner_of(position, side, groups, index) * share
            pltpu.make_async_copy(
                buf.at[pl.ds(pl.multiple_of(start, 16), share)],
                target.at[pl.ds(pl.multiple_of(position * share, 16), share)],
                sems.at[slot],
            ).start()
        return 0

    lax.fori_loop(0, count, body, 0)


def send_wait(buf, keep, send, sems):
    half = keep.shape[0]
    pltpu.make_async_copy(buf.at[pl.ds(0, half)], keep, sems.at[0]).wait()
    pltpu.make_async_copy(buf.at[pl.ds(half, half)], send, sems.at[1]).wait()


def forward_block(taps, begins, dilation, x, y, weights, cols, kept, hmid, prod):
    w_in_t, w_out_t, conv_t = weights
    g1, b1, g2, b2, g3, b3, ob = cols
    n1, s1, r, n2, s2, n3, s3, hin, shifted, hout = kept
    inner = hmid.shape[0]
    tokens = x.shape[1]
    narrow = prod.at[0:inner]
    norm_forward(x, g1, b1, n1, s1, hin, r, 0)
    narrow[...] = nn(w_in_t[...], hin[...])
    norm_forward(narrow, g2, b2, n2, s2, hmid, r, 1)
    write_shifts(hmid, shifted, begins, tap_offsets(taps, dilation, False))
    narrow[...] = nn(conv_t[:, 0 : inner * taps], shifted[...])
    norm_forward(narrow, g3, b3, n3, s3, hout, r, 2)
    prod[...] = nn(w_out_t[...], hout[...])

    def body(unit, _):
        here = lane_block(unit)
        for part in chunks(x.shape[0]):
            y[part, here] = (x[part, here].astype(F32) + prod[part, here] + ob[part, :]).astype(BF)
        return 0

    lax.fori_loop(0, tokens // LANES, body, 0)


def fill_columns(small, cols):
    g1, b1, g2, b2, g3, b3, ob = cols
    width, inner = g1.shape[0], g2.shape[0]
    for target, row, scale in ((g1, 0, 0.5), (b1, 1, 0.5), (ob, 2, 1.0)):
        target[...] = column(small[row : row + 1, 0:width] * scale)
    for target, row in ((g2, 3), (b2, 4), (g3, 5), (b3, 6)):
        target[...] = column(small[row : row + 1, 0:inner] * 0.5)


def back_third(gy, w_out, kept, prod, grad_mixed, gain_sums, bias_sums):
    n3, s3, r = kept
    inner = w_out.shape[0]
    narrow = prod.at[0:inner]
    narrow[...] = nn(w_out[...], gy[...])

    def emit(part, here, value):
        grad_mixed[part, here] = value.astype(BF)

    norm_backward(narrow, s3, n3, r, 2, gain_sums, bias_sums, emit)


def back_second(taps, begins, dilation, conv_w, kept, prod, grad_mixed, moved, grad_projected, gain_sums, bias_sums):
    n2, s2, r = kept
    inner = grad_mixed.shape[0]
    narrow = prod.at[0:inner]
    write_shifts(grad_mixed, moved, begins, tap_offsets(taps, dilation, True))
    narrow[...] = nn(conv_w[...], moved[...])

    def emit(part, here, value):
        grad_projected[part, here] = value.astype(BF)

    norm_backward(narrow, s2, n2, r, 1, gain_sums, bias_sums, emit)


def back_first(gy, w_in, kept, prod, grad_projected, gx, gain_sums, bias_sums):
    n1, s1, r = kept
    prod[...] = nn(w_in[...], grad_projected[...])

    def emit(part, here, value):
        gx[part, here] = (gy[part, here].astype(F32) + value).astype(BF)

    norm_backward(prod, s1, n1, r, 0, gain_sums, bias_sums, emit)


def vector_sums(small, sums, gy):
    ag1, ab1, ag2, ab2, ag3, ab3 = sums
    width, inner = ag1.shape[0], ag2.shape[0]
    g1, g2, g3 = small[0:1, 0:width], small[3:4, 0:inner], small[5:6, 0:inner]
    bias = nt(jnp.ones((16, gy.shape[1]), BF), gy[...])[0:1]
    pairs = ((ag1, g1), (ab1, g1), (ag2, g2), (ag3, g3), (ab2, g2), (ab3, g3))
    return [row_sums(acc[...]) / gain for acc, gain in pairs] + [bias]


def start_all(copies):
    for copy in copies:
        copy.start()


def prepare_kernel(rows, gin, bin_, gmid, bmid, out_bias, dilation, send, small, sem):
    section = lax.axis_index("section")
    copy = pltpu.make_async_copy(rows.at[1 - section], send, sem)
    copy.start()
    width, inner = gin.shape[1], gmid.shape[1]
    small[...] = jnp.zeros_like(small)
    for row, ref in ((0, gin), (1, bin_), (2, out_bias)):
        small[row : row + 1, 0:width] = ref[...]
    for row, ref, which in ((3, gmid, 0), (4, bmid, 0), (5, gmid, 1), (6, bmid, 1)):
        small[row : row + 1, 0:inner] = ref[which : which + 1, :]
    small[7:8, :] = jnp.full((1, small.shape[1]), dilation[0].astype(F32), F32)
    copy.wait()


def prepare(rows, gin, bin_, gmid, bmid, out_bias, dilation):
    return pl.pallas_call(
        prepare_kernel,
        in_specs=[ANY] + [VMEM] * 5 + [SMEM],
        out_specs=[VMEM, VMEM],
        out_shape=[shape(rows.shape[1:], BF), shape((SMALL_ROWS, rows.shape[1]), F32)],
        scratch_shapes=[pltpu.SemaphoreType.DMA],
        name="prepare",
    )(rows, gin, bin_, gmid, bmid, out_bias, dilation)


def kept_shapes(taps, width, inner, tokens):
    wide, narrow = (width, tokens), (inner, tokens)
    return [
        (wide, BF), (wide, BF), ((8, tokens), F32), (narrow, BF), (narrow, BF), (narrow, BF), (narrow, BF),
        (wide, BF), ((inner * taps, tokens), BF), (narrow, BF),
    ]


def column_shapes(width, inner):
    return [(width, LANES)] * 2 + [(inner, LANES)] * 4 + [(width, LANES)]


def sum_shapes(width, inner):
    return [(width, LANES)] * 2 + [(inner, LANES)] * 4


def main_kernel(taps_of, groups, *refs):
    refs = list(refs)

    def take(number):
        taken = refs[:number]
        del refs[:number]
        return taken

    seq, rows, got, small_own, small_got = take(5)
    own_w, got_w = take(3), take(3)
    outs, send_y, grad_out, keep_buf, send_buf = take(5)
    kept_out = take(10)
    x, cot = take(2)
    enc_w, dec_w = take(3), take(3)
    small = take(2)
    enc_kept, dec_kept = take(10), take(10)
    cols = take(7)
    hmid, prod, y_enc, gx, w_out_t, conv_t, w_in, conv_w, grad_mixed, grad_projected, moved, buf = take(12)
    sums = take(6)
    vec, sem = take(2)

    section = lax.axis_index("section")
    index = lax.axis_index("dp")
    leading = section == 0
    width, tokens = x.shape
    inner = hmid.shape[0]
    flag = leading.astype(F32)
    small[0][...] = small_own[...] * flag + small_got[...] * (1.0 - flag)
    small[1][...] = small_own[...] * (1.0 - flag) + small_got[...] * flag
    dilation = [jnp.max(member[7:8, 0:LANES]).astype(jnp.int32) for member in small]

    def begins(unit):
        return seq[section, unit]

    loads = [(x, rows.at[0], got), (enc_w[0], own_w[0], got_w[0]), (enc_w[2], own_w[2], got_w[2])]
    loads += [(enc_w[1], own_w[1], got_w[1]), (dec_w[0], got_w[0], own_w[0]), (dec_w[1], got_w[1], own_w[1])]
    loads += [(dec_w[2], got_w[2].at[0 : taps_of[1]], own_w[2].at[0 : taps_of[1]]), (cot, got, rows.at[1])]

    def load(at):
        target, first, second = loads[at]
        pl.when(leading)(pltpu.make_async_copy(first, target, sem.at[at]).start)
        pl.when(jnp.logical_not(leading))(pltpu.make_async_copy(second, target, sem.at[at]).start)

    for at in range(4):
        load(at)

    def ready(at):
        pltpu.make_async_copy(loads[at][1], loads[at][0], sem.at[at]).wait()

    fill_columns(small[0], cols)
    ready(0)
    ready(1)
    ready(2)
    for k in range(taps_of[0]):
        conv_t[:, inner * k : inner * (k + 1)] = enc_w[2][k].T
    ready(3)
    w_out_t[...] = enc_w[1][...].T
    for at in range(4, 8):
        load(at)
    forward_block(
        taps_of[0], begins, dilation[0], x, y_enc, (enc_w[0], w_out_t, conv_t), cols, enc_kept, hmid, prod
    )
    saves = [pltpu.make_async_copy(a, b, sem.at[8 + i]) for i, (a, b) in enumerate(zip(enc_kept, kept_out))]
    start_all(saves)

    fill_columns(small[1], cols)
    for at in range(4, 8):
        ready(at)
    for k in range(taps_of[1]):
        conv_t[:, inner * k : inner * (k + 1)] = dec_w[2][k].T
        conv_w[:, inner * k : inner * (k + 1)] = dec_w[2][k]
    w_out_t[...] = dec_w[1][...].T
    w_in[...] = dec_w[0][...].T
    y_dec = x
    forward_block(
        taps_of[1], begins, dilation[1], y_enc, y_dec, (dec_w[0], w_out_t, conv_t), cols, dec_kept, hmid, prod
    )
    pl.when(leading)(pltpu.make_async_copy(y_enc, outs.at[0], sem.at[18]).start)
    pl.when(leading)(pltpu.make_async_copy(y_dec, send_y, sem.at[19]).start)
    pl.when(jnp.logical_not(leading))(pltpu.make_async_copy(y_dec, outs.at[1], sem.at[18]).start)
    pl.when(jnp.logical_not(leading))(pltpu.make_async_copy(y_enc, send_y, sem.at[19]).start)

    n1, s1, r, n2, s2, n3, s3, hin, shifted, hout = dec_kept
    ag1, ab1, ag2, ab2, ag3, ab3 = sums
    w_in_at, vec_at, end = layout(taps_of[1], width, inner)[2:]
    back_third(cot, dec_w[1], (n3, s3, r), prod, grad_mixed, ag3, ab3)
    put_slabs(buf, 0, nt(hout[...], cot[...]))
    put_taps(buf, taps_of[1], width, shifted, grad_mixed)
    back_second(
        taps_of[1], begins, dilation[1], conv_w, (n2, s2, r), prod, grad_mixed, moved, grad_projected, ag2, ab2
    )
    put_slabs(buf, w_in_at, nt(grad_projected[...], hin[...]))
    back_first(cot, w_in, (n1, s1, r), prod, grad_projected, gx, ag1, ab1)
    put_vectors(buf, vec_at, vec, vector_sums(small[1], sums, cot))
    if buf.shape[0] > end:
        buf[end:, :] = jnp.zeros((buf.shape[0] - end, LANES), BF)
    send_out(buf, keep_buf, send_buf, section, index, groups, sem.at[21:23])
    last = pltpu.make_async_copy(gx, grad_out, sem.at[20])
    last.start()
    send_wait(buf, keep_buf, send_buf, sem.at[21:23])
    for copy in saves + [last]:
        copy.wait()
    pltpu.make_async_copy(y_enc, outs.at[0], sem.at[18]).wait()
    pltpu.make_async_copy(y_dec, send_y, sem.at[19]).wait()


def main_call(taps_of, groups, seq, rows, got, small_own, small_got, own_w, got_w):
    _, width, tokens = rows.shape
    inner = own_w[1].shape[0]
    half = padded_rows(taps_of[1], width, inner, groups) // 2
    wide, narrow = (width, tokens), (inner, tokens)
    weight_shapes = [(inner, width), (inner, width)]
    scratch = [(wide, BF)] * 2
    for taps in taps_of:
        scratch += [(dims, BF) for dims in weight_shapes + [(taps, inner, inner)]]
    scratch += [((SMALL_ROWS, width), F32)] * 2
    scratch += kept_shapes(taps_of[0], width, inner, tokens) + kept_shapes(taps_of[1], width, inner, tokens)
    scratch += [(dims, F32) for dims in column_shapes(width, inner)]
    scratch += [
        (narrow, BF), (wide, F32), (wide, BF), (wide, BF), ((width, inner), BF), ((inner, inner * taps_of[0]), BF),
        ((width, inner), BF), ((inner, inner * taps_of[1]), BF), (narrow, BF), (narrow, BF),
        ((inner * taps_of[1], tokens), BF), ((2 * half, LANES), BF),
    ]
    scratch += [(dims, F32) for dims in sum_shapes(width, inner)]
    scratch += [((VEC_ROWS, LANES), F32)]
    outs = [shape((2,) + wide, BF), shape(wide, BF), shape(wide, BF), shape((half, LANES), BF), shape((half, LANES), BF)]
    outs += [shape(dims, dtype) for dims, dtype in kept_shapes(taps_of[0], width, inner, tokens)]
    flops = 2 * tokens * inner * (2 * width + taps_of[0] * inner + 3 * (2 * width + taps_of[1] * inner))
    return pl.pallas_call(
        functools.partial(main_kernel, taps_of, groups),
        in_specs=[SMEM, ANY, ANY, VMEM, VMEM] + [ANY] * 6,
        out_specs=[ANY] * len(outs),
        out_shape=outs,
        scratch_shapes=[pltpu.VMEM(dims, dtype) for dims, dtype in scratch] + [pltpu.SemaphoreType.DMA((23,))],
        compiler_params=pltpu.CompilerParams(vmem_limit_bytes=VMEM_LIMIT),
        cost_estimate=pl.CostEstimate(flops=4 * flops, bytes_accessed=60 * 2**20, transcendentals=0),
        name="main_blocks",
    )(seq, rows, got, small_own, small_got, *own_w, *got_w)


def upper_kernel(
    taps,
    gy_in, n3_in, s3_in, r_in, shifted_in, hout_in, own_w, got_w,
    part, grad_mixed_out, ag3, ab3,
    gy, n3, s3, r, shifted, hout, w_out, prod, grad_mixed, buf, sem,
):
    leading = lax.axis_index("section") == 0
    width = gy.shape[0]
    pl.when(leading)(pltpu.make_async_copy(own_w, w_out, sem.at[0]).start)
    pl.when(jnp.logical_not(leading))(pltpu.make_async_copy(got_w, w_out, sem.at[0]).start)
    pairs = ((gy_in, gy), (s3_in, s3), (n3_in, n3), (r_in, r), (hout_in, hout), (shifted_in, shifted))
    loads = [pltpu.make_async_copy(a, b, sem.at[1 + i]) for i, (a, b) in enumerate(pairs)]
    start_all(loads)
    pltpu.make_async_copy(own_w, w_out, sem.at[0]).wait()
    for copy in loads[:4]:
        copy.wait()
    back_third(gy, w_out, (n3, s3, r), prod, grad_mixed, ag3, ab3)
    out = pltpu.make_async_copy(grad_mixed, grad_mixed_out, sem.at[7])
    out.start()
    loads[4].wait()
    put_slabs(buf, 0, nt(hout[...], gy[...]))
    loads[5].wait()
    put_taps(buf, taps, width, shifted, grad_mixed)
    save = pltpu.make_async_copy(buf, part, sem.at[8])
    save.start()
    save.wait()
    out.wait()


def upper_call(taps, gy, kept, own_w, got_w):
    width, tokens = gy.shape
    inner = own_w.shape[0]
    n1, s1, r, n2, s2, n3, s3, hin, shifted, hout = kept
    rows = layout(taps, width, inner)[2]
    wide, narrow = (width, tokens), (inner, tokens)
    scratch = [
        (wide, BF), (narrow, BF), (narrow, BF), ((8, tokens), F32), ((inner * taps, tokens), BF), (narrow, BF),
        ((inner, width), BF), (narrow, F32), (narrow, BF), ((rows, LANES), BF),
    ]
    flops = 2 * tokens * inner * (2 * width + taps * inner)
    return pl.pallas_call(
        functools.partial(upper_kernel, taps),
        in_specs=[ANY] * 8,
        out_specs=[ANY, ANY, VMEM, VMEM],
        out_shape=[shape((rows, LANES), BF), shape(narrow, BF), shape((inner, LANES), F32), shape((inner, LANES), F32)],
        scratch_shapes=[pltpu.VMEM(dims, dtype) for dims, dtype in scratch] + [pltpu.SemaphoreType.DMA((9,))],
        compiler_params=pltpu.CompilerParams(vmem_limit_bytes=VMEM_LIMIT),
        cost_estimate=pl.CostEstimate(flops=4 * flops, bytes_accessed=20 * 2**20, transcendentals=0),
        name="upper_encoder",
    )(gy, n3, s3, r, shifted, hout, own_w, got_w)


def lower_kernel(
    taps, groups,
    seq, gy_in, grad_mixed_in, part, ag3, ab3, small_own, small_got, n1_in, s1_in, r_in, n2_in, s2_in, hin_in,
    own_in, own_conv, got_in, got_conv,
    outs, send_gx, keep_buf, send_buf,
    gy, grad_mixed, n1, s1, r, n2, s2, hin, w_in_t, conv, w_in, conv_w, prod, moved, grad_projected, gx, buf,
    ag1, ab1, ag2, ab2, vec, sem,
):
    section = lax.axis_index("section")
    index = lax.axis_index("dp")
    leading = section == 0
    other = jnp.logical_not(leading)
    width, tokens = gy.shape
    inner = grad_mixed.shape[0]
    for at, (first, second, target) in enumerate(((own_conv, got_conv, conv), (own_in, got_in, w_in_t))):
        pl.when(leading)(pltpu.make_async_copy(first, target, sem.at[at]).start)
        pl.when(other)(pltpu.make_async_copy(second, target, sem.at[at]).start)
    w_in_at, vec_at, end = layout(taps, width, inner)[2:]
    pairs = (
        (grad_mixed_in, grad_mixed), (n2_in, n2), (s2_in, s2), (r_in, r), (hin_in, hin), (n1_in, n1), (s1_in, s1),
        (gy_in, gy), (part, buf.at[0:w_in_at]),
    )
    loads = [pltpu.make_async_copy(a, b, sem.at[2 + i]) for i, (a, b) in enumerate(pairs)]
    start_all(loads)
    flag = leading.astype(F32)
    small = small_own[...] * flag + small_got[...] * (1.0 - flag)
    dilation = jnp.max(small[7:8, 0:LANES]).astype(jnp.int32)
    pltpu.make_async_copy(own_conv, conv, sem.at[0]).wait()
    for k in range(taps):
        conv_w[:, inner * k : inner * (k + 1)] = conv[k]
    for copy in loads[:4]:
        copy.wait()

    def begins(unit):
        return seq[section, unit]

    back_second(taps, begins, dilation, conv_w, (n2, s2, r), prod, grad_mixed, moved, grad_projected, ag2, ab2)
    loads[4].wait()
    put_slabs(buf, w_in_at, nt(grad_projected[...], hin[...]))
    pltpu.make_async_copy(own_in, w_in_t, sem.at[1]).wait()
    w_in[...] = w_in_t[...].T
    for copy in loads[5:]:
        copy.wait()
    back_first(gy, w_in, (n1, s1, r), prod, grad_projected, gx, ag1, ab1)
    put_vectors(buf, vec_at, vec, vector_sums(small, (ag1, ab1, ag2, ab2, ag3, ab3), gy))
    if buf.shape[0] > end:
        buf[end:, :] = jnp.zeros((buf.shape[0] - end, LANES), BF)
    send_out(buf, keep_buf, send_buf, section, index, groups, sem.at[13:15])
    pl.when(leading)(pltpu.make_async_copy(gx, outs.at[0], sem.at[11]).start)
    pl.when(leading)(pltpu.make_async_copy(gy, send_gx, sem.at[12]).start)
    pl.when(other)(pltpu.make_async_copy(gy, outs.at[1], sem.at[11]).start)
    pl.when(other)(pltpu.make_async_copy(gx, send_gx, sem.at[12]).start)
    send_wait(buf, keep_buf, send_buf, sem.at[13:15])
    pltpu.make_async_copy(gx, outs.at[0], sem.at[11]).wait()
    pltpu.make_async_copy(gy, send_gx, sem.at[12]).wait()


def lower_call(taps, groups, seq, gy, upper, kept, small_own, small_got, own_w, got_w):
    width, tokens = gy.shape
    part, grad_mixed, ag3, ab3 = upper
    n1, s1, r, n2, s2, n3, s3, hin, shifted, hout = kept
    inner = grad_mixed.shape[0]
    half = padded_rows(taps, width, inner, groups) // 2
    wide, narrow = (width, tokens), (inner, tokens)
    scratch = [
        (wide, BF), (narrow, BF), (wide, BF), (wide, BF), ((8, tokens), F32), (narrow, BF), (narrow, BF), (wide, BF),
        ((inner, width), BF), ((taps, inner, inner), BF), ((width, inner), BF), ((inner, inner * taps), BF),
        (wide, F32), ((inner * taps, tokens), BF), (narrow, BF), (wide, BF), ((2 * half, LANES), BF),
    ]
    scratch += [(dims, F32) for dims in sum_shapes(width, inner)[:4]]
    scratch += [((VEC_ROWS, LANES), F32)]
    outs = [shape((2,) + wide, BF), shape(wide, BF), shape((half, LANES), BF), shape((half, LANES), BF)]
    flops = 2 * tokens * inner * (2 * width + taps * inner)
    return pl.pallas_call(
        functools.partial(lower_kernel, taps, groups),
        in_specs=[SMEM, ANY, ANY, ANY, VMEM, VMEM, VMEM, VMEM] + [ANY] * 10,
        out_specs=[ANY] * 4,
        out_shape=outs,
        scratch_shapes=[pltpu.VMEM(dims, dtype) for dims, dtype in scratch] + [pltpu.SemaphoreType.DMA((15,))],
        compiler_params=pltpu.CompilerParams(vmem_limit_bytes=VMEM_LIMIT),
        cost_estimate=pl.CostEstimate(flops=4 * flops, bytes_accessed=20 * 2**20, transcendentals=0),
        name="lower_encoder",
    )(
        seq, gy, grad_mixed, part, ag3, ab3, small_own, small_got, n1, s1, r, n2, s2, hin,
        own_w[0], own_w[2], got_w[0], got_w[2],
    )


def unpack_kernel(taps_of, groups_of, *refs):
    refs = list(refs)

    def take(number):
        taken = refs[:number]
        del refs[:number]
        return taken

    own_of, got_of = [], []
    for _ in range(2):
        own_of.append(take(2))
        got_of.append(take(2))
    w_in_t, w_out, conv, gin, bin_, gmid, bmid, out_bias, buf, sem = refs
    inner, width = w_out.shape
    whole = inner // LANES
    tail = inner - whole * LANES
    slots = conv.shape[0]
    section = lax.axis_index("section")
    index = lax.axis_index("dp")

    def write(taps, groups, own, got):
        rows = own[0].shape[0]
        count = share_count(groups[0])
        share = 2 * rows // count

        def body(position, _):
            for which, (pieces, side) in enumerate(((own, section), (got, 1 - section))):
                for at, ref in enumerate(pieces):
                    owner = owner_of(position + at * (count // 2), side, groups, index)
                    start = side * (2 * rows) + owner * share
                    pltpu.make_async_copy(
                        ref.at[pl.ds(pl.multiple_of(position * share, 16), share)],
                        buf.at[pl.ds(pl.multiple_of(start, 16), share)],
                        sem.at[2 * which + at],
                    ).start()
            return 0

        lax.fori_loop(0, count // 2, body, 0)
        for which, pieces in enumerate((own, got)):
            for at, ref in enumerate(pieces):
                pltpu.make_async_copy(ref, buf.at[pl.ds(0, rows)], sem.at[2 * which + at]).wait()
        taps_at, tails_at, w_in_at, vec_at, _ = layout(taps, width, inner)

        def wide(target, row):
            for at in range(0, width, LANES):
                q = at // LANES
                size = min(LANES, width - at)
                target[:, at : at + size] = buf[row + q * inner : row + (q + 1) * inner, 0:size].astype(F32)

        wide(w_out, 0)
        wide(w_in_t, w_in_at)
        tails = buf[tails_at : tails_at + inner, :].astype(F32)
        for k in range(slots):
            if k >= taps:
                conv[k] = jnp.zeros((inner, inner), F32)
                continue
            for q in range(whole):
                at = taps_at + inner * (whole * k + q)
                conv[k, :, LANES * q : LANES * (q + 1)] = buf[at : at + inner, :].astype(F32)
            conv[k, :, LANES * whole :] = tails[:, tail * k : tail * (k + 1)]
        vec = buf[vec_at : vec_at + VEC_ROWS, :].astype(F32)
        row = 0
        for target, member in ((gin, 0), (bin_, 0), (gmid, 0), (gmid, 1), (bmid, 0), (bmid, 1), (out_bias, 0)):
            for at in range(0, target.shape[1], LANES):
                size = min(LANES, target.shape[1] - at)
                target[member : member + 1, at : at + size] = vec[row : row + 1, 0:size]
                row += 1

    pl.when(section == 0)(lambda: write(taps_of[0], groups_of[0], own_of[0], got_of[0]))
    pl.when(section != 0)(lambda: write(taps_of[1], groups_of[1], own_of[1], got_of[1]))


def unpack(taps_of, groups_of, enc, dec, width, inner):
    pieces = enc[0] + enc[1] + dec[0] + dec[1]
    rows = max(4 * part[0].shape[0] for part in (enc[0], dec[0]))
    return pl.pallas_call(
        functools.partial(unpack_kernel, taps_of, groups_of),
        in_specs=[ANY] * len(pieces),
        out_specs=[VMEM] * 8,
        out_shape=[
            shape((inner, width), F32), shape((inner, width), F32), shape((taps_of[0], inner, inner), F32),
            shape((1, width), F32), shape((1, width), F32), shape((2, inner), F32), shape((2, inner), F32),
            shape((1, width), F32),
        ],
        scratch_shapes=[pltpu.VMEM((rows, LANES), BF), pltpu.SemaphoreType.DMA((4,))],
        compiler_params=pltpu.CompilerParams(vmem_limit_bytes=VMEM_LIMIT),
        name="unpack",
    )(*pieces)


def swap_sections(value):
    return lax.ppermute(value, "section", [(0, 1), (1, 0)])


def swap_dp(value, masks):
    count = lax.axis_size("dp")
    pairs = [(s * count + i, s * count + (i ^ masks[s])) for s in range(2) for i in range(count)]
    return lax.ppermute(value, ("section", "dp"), pairs)


def rounded_sum(terms, rows):
    total = terms[0][rows].astype(F32)
    for term in terms[1:]:
        total = total + term[rows].astype(F32)
    return total.astype(BF)


def masks_of(bits, other):
    return [other << own[0] for own in bits]


def reduce_all(keep, send, groups, receiver):
    count = lax.axis_size("dp")
    steps = list(zip(*groups))
    terms = [keep, swap_sections(send)]
    for bits in steps:
        size = terms[0].shape[0] >> len(bits[0])
        came = []
        for other in range(1, 2 ** len(bits[0])):
            part = rounded_sum(terms, slice(other * size, (other + 1) * size))
            came.append(swap_dp(part, masks_of(bits, other)))
        terms = [term[:size] for term in terms] + came
    value = rounded_sum(terms, slice(None))
    for bit in range(sum(len(bits) for bits in groups[0]), count.bit_length() - 1):
        value = rounded_sum([value, swap_dp(value, [1 << bit] * 2)], slice(None))
    pieces = [value]
    for bits in reversed(steps):
        if len(pieces) > 1:
            value = jnp.concatenate(pieces, 0)
        pieces = [value] + [swap_dp(value, masks_of(bits, other)) for other in range(1, 2 ** len(bits[0]))]
    pairs = [(1 - receiver, receiver)]
    return pieces, [lax.ppermute(piece, "section", pairs) for piece in pieces]


def shards(
    section_inputs,
    seq_lengths,
    dilations,
    gains_in,
    biases_in,
    gains_mid,
    biases_mid,
    out_bias,
    w_in,
    w_out,
    conv_taps,
):
    section = lax.axis_index("section")
    count = lax.axis_size("dp")
    groups_of = (scatter_groups(count, True), scatter_groups(count, False))
    rows = jnp.swapaxes(section_inputs[0], 1, 2)
    width = rows.shape[1]
    inner = w_out.shape[1]
    taps_of = (conv_taps.shape[1], DEC_TAPS)

    own_w = (jnp.swapaxes(w_in[0], 0, 1), w_out[0], conv_taps[0])
    send_rows, small = prepare(rows, gains_in, biases_in, gains_mid[0], biases_mid[0], out_bias, dilations)
    got_rows = swap_sections(send_rows)
    got_small = swap_sections(small)
    got_w = tuple(swap_sections(member) for member in own_w)

    outs, send_y, grad_dec, keep_dec, send_dec, *kept = main_call(
        taps_of, groups_of[1], seq_lengths, rows, got_rows, small, got_small, own_w, got_w
    )
    got_y = swap_sections(send_y)
    dec = reduce_all(keep_dec, send_dec, groups_of[1], 1)
    upper = upper_call(taps_of[0], grad_dec, kept, own_w[1], got_w[1])
    grads_x, send_gx, keep_enc, send_enc = lower_call(
        taps_of[0], groups_of[0], seq_lengths, grad_dec, upper, kept, small, got_small, own_w, got_w
    )
    enc = reduce_all(keep_enc, send_enc, groups_of[0], 0)
    got_gx = swap_sections(send_gx)

    def joined(pair, got):
        pair = lax.dynamic_update_slice_in_dim(pair, got[None], 1 - section, 0)
        return jnp.swapaxes(pair, 1, 2)[None]

    grads = unpack(taps_of, groups_of, enc, dec, width, inner)
    return (
        joined(outs, got_y),
        joined(grads_x, got_gx),
        grads[3],
        grads[4],
        grads[5][None],
        grads[6][None],
        grads[7],
        jnp.swapaxes(grads[0], 0, 1)[None],
        grads[1][None],
        grads[2][None],
    )


def solution(mesh):
    in_specs = (
        P("section", None, "dp", None),
        P(None, "dp"),
        P("section"),
        P("section", None),
        P("section", None),
        P("section", None, None),
        P("section", None, None),
        P("section", None),
        P("section", None, None),
        P("section", None, None),
        P("section", None, None, None),
    )
    out_specs = (
        P("section", None, "dp", None),
        P("section", None, "dp", None),
        P("section", None),
        P("section", None),
        P("section", None, None),
        P("section", None, None),
        P("section", None),
        P("section", None, None),
        P("section", None, None),
        P("section", None, None, None),
    )
    return jax.shard_map(shards, mesh=mesh, in_specs=in_specs, out_specs=out_specs, check_vma=False)
```

time: 469 us -> 196 us (0.42); the launches traced: 461 us -> 195 us
  other arithmetic: 91.1 us -> 2.55 us
  Pallas kernels: 0 us -> 85 us
  blocking collectives: 81.7 us -> 0 us
  matrix products: 78.5 us -> 0 us
  waiting for transfers between devices: 132 us -> 57.6 us
  local copies, waits for them, and re-layouts: 52.6 us -> 8.18 us
  starting transfers between devices: 8.23 us -> 40.3 us
  between operations: 16.6 us -> 1.71 us
    psum x1 -> x0, waiting for transfers between devices: 131 us -> none  [shards(): lax.psum((totals[0], totals[1], totals[2], totals[3], totals[4], totals[5...]
    pallas_call x0 -> x5, Pallas kernels: none -> 85 us  [the longest x1 46.4 us: main_call(): pl.pallas_call(functools.partial(main_kernel, taps_of, groups), in_specs=...]
    psum x1 -> x0, blocking collectives: 81.7 us -> none  [shards(): lax.psum((totals[0], totals[1], totals[2], totals[3], totals[4], totals[5...]
    dot_general x27 -> x0, matrix products: 78.5 us -> none  [the longest x6 16.6 us: times_transpose(): lax.dot_general(left_matrix, right_matrix, (((1,), (1,)), ((), ())), pref...]
    ppermute x4 -> x29, waiting for transfers between devices: 1.18 us -> 57.6 us  [the longest x16 46.3 us: swap_dp(): return lax.ppermute(value, ('section', 'dp'), pairs)]
    ppermute x4 -> x29, starting transfers between devices: 8.19 us -> 40.3 us  [the longest x16 27.1 us: swap_dp(): return lax.ppermute(value, ('section', 'dp'), pairs)]
    reduce_sum x17 -> x0, other arithmetic: 26.9 us -> none  [the longest x3 15.3 us: norm_back(): jnp.sum(gradient * normed, axis=0)]
    unnamed x144 -> x31, local copies, waits for them, and re-layouts: 31.9 us -> 5.2 us
  transfers between devices with their start and end apart: 5 -> 29, of which waited for: 2 -> 15; matrix products, arithmetic and copies ran while one was open for 12% -> 3% of each run, Pallas kernels for 0% -> 0%
where the time goes in v2:
time: 196 us; the launch traced here: 195 us
  Pallas kernels  85 us (43%)
  waiting for transfers between devices  57.6 us (29%)
  starting transfers between devices  40.3 us (21%)
  local copies, waits for them, and re-layouts  8.18 us (4%)
  other arithmetic  2.55 us (1%)
    pallas_call x1, Pallas kernels, main_call(): pl.pallas_call(functools.partial(main_kernel, taps_of, groups), in_specs=...  46.4 us
    ppermute x16, waiting for transfers between devices, swap_dp(): return lax.ppermute(value, ('section', 'dp'), pairs)  46.3 us
    ppermute x16, starting transfers between devices, swap_dp(): return lax.ppermute(value, ('section', 'dp'), pairs)  27.1 us
    pallas_call x1, Pallas kernels, lower_call(): pl.pallas_call(functools.partial(lower_kernel, taps, groups), in_specs=[S...  19.2 us
    ppermute x9, waiting for transfers between devices, swap_sections(): return lax.ppermute(value, 'section', [(0, 1), (1, 0)])  11.3 us
    ppermute x4, starting transfers between devices, reduce_all(): return (pieces, [lax.ppermute(piece, 'section', pairs) for piece in pieces])  10.5 us
    pallas_call x1, Pallas kernels, upper_call(): pl.pallas_call(functools.partial(upper_kernel, taps), in_specs=[ANY] * 8,...  10.2 us
    pallas_call x1, Pallas kernels, unpack(): pl.pallas_call(functools.partial(unpack_kernel, taps_of, groups_of), in_s...  5.72 us
  transfers between devices with their start and end apart: 29, of which 15 were waited for; matrix products, arithmetic and copies ran while one was open for 3% of the time, Pallas kernels for 0%

profile of v2, /device:TPU:0, one launch (start us, length us, event | category | flops | bytes accessed | tf_op | source)
XLA Modules:
  0.0 195.3 jit_solution(5938269507914971774)
XLA Ops:
  1.3 3.5 %prepare.1 = (bf16[800,1024]{1,0:T(8,128)(2,1)}, f32[8,800]{1,0:T(8,128)}) custom-call(bf16[2,800,1024]{2,1,0:T(8,128)(2,1)} %bitcast.27, f32[1,800]{1,0:T(1,128)} %gin.1, f32[1,800]{1,0:T(1,128)} %bin_.1, f32[2,400]{1,0:T(2,128)} %bitcast.29, f32[2,400]{1,0:T(2,128)} %bitcast.30, f32[1,800]{1,0:T(1,128)} %out_bias.1, s32[1]{0:T(128)S(6)} %copy.27.dilation), custom_call_target="tpu_custom_call" | custom-call | tf_op jit(solution)/shard_map/prepare/pallas_call | solution.py:367
  4.8 0.5 collective-permute-start
  5.4 0.1 collective-permute-start.4
  5.4 0.4 collective-permute-start.2
  5.9 0.1 collective-permute-start.3
  6.0 0.4 collective-permute-start.1
  6.4 5.9 %collective-permute-done.1.refs_4_.small_got = f32[8,800]{1,0:T(8,128)S(1)} collective-permute-done((f32[8,800]{1,0:T(8,128)}, f32[8,800]{1,0:T(8,128)S(1)}, u32[]{:S(2)}, u32[]{:S(2)}) %collective-permute-start.1) | collective-permute-done | bytes 25632 | tf_op jit(solution)/shard_map/ppermute | solution.py:764
  12.3 1.2 collective-permute-done.3.refs_9_.got_w
  13.5 0.9 copy-done.12
  14.4 1.3 copy-done.7
  15.7 46.4 %main_blocks.1 = (bf16[2,800,1024]{2,1,0:T(8,128)(2,1)}, bf16[800,1024]{1,0:T(8,128)(2,1)}, bf16[800,1024]{1,0:T(8,128)(2,1)}, bf16[4864,128]{1,0:T(8,128)(2,1)}...) custom-call(s32[2,8]{1,0:T(2,128)} %seq.1, ...), custom_call_target="tpu_custom_call" | custom-call | flops 39321600000 | bytes 62914560 | tf_op jit(solution)/shard_map/main_blocks/pallas_call | solution.py:521
  62.1 10.2 %upper_encoder.1 = (bf16[9200,128]{1,0:T(8,128)(2,1)}, bf16[400,1024]{1,0:T(8,128)(2,1)}, f32[400,128]{1,0:T(8,128)}, f32[400,128]{1,0:T(8,128)}) custom-call(bf16[800,1024]{1,0:T(8,128)(2,1)} %get-tuple-element.47.gy_in, bf16[400,1024]{1,0:T(8,128)(2,1)} %get-tuple-element.48.n3_in, bf16[400,1024]{1,0:T(8,128)(2,1)} %get-tuple-element.49.s3_in, ...), custom_call_target="tpu_custom_call" | custom-call | flops 11796480000 | bytes 20971520 | tf_op jit(solution)/shard_map/upper_encoder/pallas_call | solution.py:573
  72.3 19.2 %lower_encoder.1 = (bf16[2,800,1024]{2,1,0:T(8,128)(2,1)}, bf16[800,1024]{1,0:T(8,128)(2,1)}, bf16[6144,128]{1,0:T(8,128)(2,1)}, bf16[6144,128]{1,0:T(8,128)(2,1)}) custom-call(s32[2,8]{1,0:T(2,128)} %seq.1, bf16[800,1024]{1,0:T(8,128)(2,1)} %get-tuple-element.47.gy_in, bf16[400,1024]{1,0:T(8,128)(2,1)} %get-tuple-element.53.grad_mixed_in, ...), custom_call_target="tpu_custom_call" | custom-call | flops 11796480000 | bytes 20971520 | tf_op jit(solution)/shard_map/lower_encoder/pallas_call | solution.py:658
  91.5 0.5 collective-permute-start.7
  92.0 0.1 collective-permute-start.20
  92.1 4.2 %collective-permute-done.7 = bf16[6144,128]{1,0:T(8,128)(2,1)S(1)} collective-permute-done((bf16[6144,128]{1,0:T(8,128)(2,1)}, bf16[6144,128]{1,0:T(8,128)(2,1)S(1)}, u32[]{:S(2)}, u32[]{:S(2)}) %collective-permute-start.7) | collective-permute-done | bytes 1572896 | tf_op jit(solution)/shard_map/ppermute | solution.py:764
  96.3 1.5 add_convert_fusion
  97.8 2.6 %collective-permute-start.8 = (bf16[3072,128]{1,0:T(8,128)(2,1)S(1)}, bf16[3072,128]{1,0:T(8,128)(2,1)S(1)}, u32[]{:S(2)}, u32[]{:S(2)}) collective-permute-start(bf16[3072,128]{1,0:T(8,128)(2,1)S(1)} %add_convert_fusion), channel_id=1, source_target_pairs={{0,1},{1,0},{2,3},{3,2},{4,5},{5,4},{6,7},{7,6},{8,9},{9,8},{10,11... | collective-permute-start | bytes 2359304 | tf_op jit(solution)/shard_map/ppermute | solution.py:770
  100.3 0.2 add_convert_fusion.1
  100.5 0.1 collective-permute-start.21
  100.6 9.7 %collective-permute-done.8 = bf16[3072,128]{1,0:T(8,128)(2,1)S(1)} collective-permute-done((bf16[3072,128]{1,0:T(8,128)(2,1)S(1)}, bf16[3072,128]{1,0:T(8,128)(2,1)S(1)}, u32[]{:S(2)}, u32[]{:S(2)}) %collective-permute-start.8) | collective-permute-done | bytes 786464 | tf_op jit(solution)/shard_map/ppermute | solution.py:770
  110.3 0.2 add_convert_fusion.2
  110.5 2.1 %collective-permute-start.9 = (bf16[1536,128]{1,0:T(8,128)(2,1)S(1)}, bf16[1536,128]{1,0:T(8,128)(2,1)S(1)}, u32[]{:S(2)}, u32[]{:S(2)}) collective-permute-start(bf16[1536,128]{1,0:T(8,128)(2,1)S(1)} %add_convert_fusion.2), channel_id=1, source_target_pairs={{0,2},{1,3},{2,0},{3,1},{4,6},{5,7},{6,4},{7,5},{8,10},{9,11},{10,... | collective-permute-start | bytes 1179656 | tf_op jit(solution)/shard_map/ppermute | solution.py:770
  112.5 8.7 %collective-permute-done.21 = bf16[2432,128]{1,0:T(8,128)(2,1)S(1)} collective-permute-done((bf16[2432,128]{1,0:T(8,128)(2,1)S(1)}, bf16[2432,128]{1,0:T(8,128)(2,1)S(1)}, u32[]{:S(2)}, u32[]{:S(2)}) %collective-permute-start.21) | collective-permute-done | bytes 622624 | tf_op jit(solution)/shard_map/ppermute | solution.py:770
  121.2 0.1 add_convert_fusion.6
  121.3 2.2 %collective-permute-start.22 = (bf16[1216,128]{1,0:T(8,128)(2,1)S(1)}, bf16[1216,128]{1,0:T(8,128)(2,1)S(1)}, u32[]{:S(2)}, u32[]{:S(2)}) collective-permute-start(bf16[1216,128]{1,0:T(8,128)(2,1)S(1)} %add_convert_fusion.6), channel_id=1, source_target_pairs={{0,2},{1,3},{2,0},{3,1},{4,6},{5,7},{6,4},{7,5},{8,10},{9,11},{10,... | collective-permute-start | bytes 933896 | tf_op jit(solution)/shard_map/ppermute | solution.py:770
  123.5 0.2 add_convert_fusion.10
  123.6 1.7 collective-permute-start.10
  125.3 2.5 %collective-permute-start.12 = (bf16[384,128]{1,0:T(8,128)(2,1)S(1)}, bf16[384,128]{1,0:T(8,128)(2,1)S(1)}, u32[]{:S(2)}, u32[]{:S(2)}) collective-permute-start(bf16[384,128]{1,0:T(8,128)(2,1)S(1)} %get-tuple-element.79), channel_id=1, source_target_pairs={{0,12},{1,13},{2,14},{3,15},{4,8},{5,9},{6,10},{7,11},{8,4},{9,5},... | collective-permute-start | bytes 294920 | tf_op jit(solution)/shard_map/ppermute | solution.py:770
  127.8 0.1 collective-permute-start.11
  127.9 0.5 collective-permute-done.22
  128.4 0.2 add_convert_fusion.5
  128.5 2.2 %collective-permute-start.23 = (bf16[1216,128]{1,0:T(8,128)(2,1)S(1)}, bf16[1216,128]{1,0:T(8,128)(2,1)S(1)}, u32[]{:S(2)}, u32[]{:S(2)}) collective-permute-start(bf16[1216,128]{1,0:T(8,128)(2,1)S(1)} %add_convert_fusion.5), channel_id=1, source_target_pairs={{0,4},{1,5},{2,6},{3,7},{4,0},{5,1},{6,2},{7,3},{8,12},{9,13},{10,... | collective-permute-start | bytes 933896 | tf_op jit(solution)/shard_map/ppermute | solution.py:770
  130.7 2.8 %collective-permute-done.12 = bf16[384,128]{1,0:T(8,128)(2,1)S(1)} collective-permute-done((bf16[384,128]{1,0:T(8,128)(2,1)S(1)}, bf16[384,128]{1,0:T(8,128)(2,1)S(1)}, u32[]{:S(2)}, u32[]{:S(2)}) %collective-permute-start.12) | collective-permute-done | bytes 98336 | tf_op jit(solution)/shard_map/ppermute | solution.py:770
  133.5 1.8 collective-permute-done.11
  135.3 0.1 constant_dynamic-update-slice_fusion.4
  135.4 3.3 %collective-permute-start.15 = (bf16[384,128]{1,0:T(8,128)(2,1)S(1)}, bf16[384,128]{1,0:T(8,128)(2,1)S(1)}, u32[]{:S(2)}, u32[]{:S(2)}) collective-permute-start(bf16[384,128]{1,0:T(8,128)(2,1)S(1)} %get-tuple-element.77), channel_id=1, source_target_pairs={{0,12},{1,13},{2,14},{3,15},{4,8},{5,9},{6,10},{7,11},{8,4},{9,5},... | collective-permute-start | bytes 294920 | tf_op jit(solution)/shard_map/ppermute | solution.py:770
  138.7 1.2 collective-permute-start.13
  139.9 2.6 %collective-permute-done.23 = bf16[1216,128]{1,0:T(8,128)(2,1)S(1)} collective-permute-done((bf16[1216,128]{1,0:T(8,128)(2,1)S(1)}, bf16[1216,128]{1,0:T(8,128)(2,1)S(1)}, u32[]{:S(2)}, u32[]{:S(2)}) %collective-permute-start.23) | collective-permute-done | bytes 311328 | tf_op jit(solution)/shard_map/ppermute | solution.py:770
  142.5 0.1 add_convert_fusion.4
  142.5 2.9 %collective-permute-start.24 = (bf16[1216,128]{1,0:T(8,128)(2,1)S(1)}, bf16[1216,128]{1,0:T(8,128)(2,1)S(1)}, u32[]{:S(2)}, u32[]{:S(2)}) collective-permute-start(bf16[1216,128]{1,0:T(8,128)(2,1)S(1)} %add_convert_fusion.4), channel_id=1, source_target_pairs={{0,8},{1,9},{2,10},{3,11},{4,12},{5,13},{6,14},{7,15},{8,0},{9,1},... | collective-permute-start | bytes 933896 | tf_op jit(solution)/shard_map/ppermute | solution.py:770
  145.4 0.5 collective-permute-start.6
  145.9 7.6 %collective-permute-done.14 = bf16[384,128]{1,0:T(8,128)(2,1)S(1)} collective-permute-done((bf16[384,128]{1,0:T(8,128)(2,1)S(1)}, bf16[384,128]{1,0:T(8,128)(2,1)S(1)}, u32[]{:S(2)}, u32[]{:S(2)}) %collective-permute-start.14) | collective-permute-done | bytes 98336 | tf_op jit(solution)/shard_map/ppermute | solution.py:770
  153.6 1.7 collective-permute-start.16
  155.3 3.9 %collective-permute-done.24 = bf16[1216,128]{1,0:T(8,128)(2,1)S(1)} collective-permute-done((bf16[1216,128]{1,0:T(8,128)(2,1)S(1)}, bf16[1216,128]{1,0:T(8,128)(2,1)S(1)}, u32[]{:S(2)}, u32[]{:S(2)}) %collective-permute-start.24) | collective-permute-done | bytes 311328 | tf_op jit(solution)/shard_map/ppermute | solution.py:770
  159.2 0.1 add_convert_fusion.3
  159.3 1.6 collective-permute-start.25
  160.9 0.5 collective-permute-done.16
  161.4 0.1 constant_dynamic-update-slice_fusion.refs_0_
  161.5 1.5 collective-permute-start.17
  163.0 6.5 %collective-permute-done.25 = bf16[1216,128]{1,0:T(8,128)(2,1)S(1)} collective-permute-done((bf16[1216,128]{1,0:T(8,128)(2,1)S(1)}, bf16[1216,128]{1,0:T(8,128)(2,1)S(1)}, u32[]{:S(2)}, u32[]{:S(2)}) %collective-permute-start.25) | collective-permute-done | bytes 311328 | tf_op jit(solution)/shard_map/ppermute | solution.py:770
  169.6 1.7 collective-permute-start.26
  171.2 1.3 collective-permute-start.18
  172.5 1.1 collective-permute-done.17.refs_1_
  173.7 1.3 collective-permute-start.19
  175.0 4.7 %collective-permute-start.27 = (bf16[2432,128]{1,0:T(8,128)(2,1)S(1)}, bf16[2432,128]{1,0:T(8,128)(2,1)}, u32[]{:S(2)}, u32[]{:S(2)}) collective-permute-start(bf16[2432,128]{1,0:T(8,128)(2,1)S(1)} %pad_maximum_fusion.refs_4_), channel_id=1, source_target_pairs={{0,16},{1,17},{2,18},{3,19},{4,20},{5,21},{6,22},{7,23},{8,24},{9,... | collective-permute-start | bytes 1867784 | tf_op jit(solution)/shard_map/ppermute | solution.py:804
  179.7 0.6 collective-permute-done.26.refs_5_
  180.3 3.2 %collective-permute-start.28 = (bf16[2432,128]{1,0:T(8,128)(2,1)}, bf16[2432,128]{1,0:T(8,128)(2,1)}, u32[]{:S(2)}, u32[]{:S(2)}) collective-permute-start(bf16[2432,128]{1,0:T(8,128)(2,1)} %collective-permute-done.26.refs_5_), channel_id=1, source_target_pairs={{0,16},{1,17},{2,18},{3,19},{4,20},{5,21},{6,22},{7,23},{8,24},{9,... | collective-permute-start | bytes 1867784 | tf_op jit(solution)/shard_map/ppermute | solution.py:804
  183.6 1.3 bitcast_dynamic-update-slice_fusion.1
  184.9 1.2 copy-done.4
  186.1 1.6 bitcast_dynamic-update-slice_fusion
  187.7 0.0 copy-start.5
  187.7 1.7 copy-done.5
  189.4 5.7 %unpack.1 = (f32[400,800]{1,0:T(8,128)}, f32[400,800]{1,0:T(8,128)}, f32[5,400,400]{2,1,0:T(8,128)}, f32[1,800]{1,0:T(1,128)}, f32[1,800]{1,0:T(1,128)}, /*index...) custom-call(bf16[3072,128]{1,0:T(8,128)(2,1)} %copy-done.3, bf16[3072,128]{1,0:T(8,128)(2,1)} %collective-permute-done.17.refs_1_, ...), custom_call_target="tpu_custom_call" | custom-call | tf_op jit(solution)/shard_map/unpack/pallas_call | solution.py:748
  (44 shorter events, 0.2 us)
Async XLA Ops:
  1.3 4.1 %copy-start.6 = (bf16[1,5,400,400]{3,2,1,0:T(8,128)(2,1)S(1)}, bf16[1,5,400,400]{3,2,1,0:T(8,128)(2,1)}, u32[]{:S(2)}) copy-start(bf16[1,5,400,400]{3,2,1,0:T(8,128)(2,1)} %param.21) | copy-start | bytes 4800004
  1.3 4.6 %copy-start.10 = (bf16[1,400,800]{2,1,0:T(8,128)(2,1)S(1)}, bf16[1,400,800]{2,1,0:T(8,128)(2,1)}, u32[]{:S(2)}) copy-start(bf16[1,400,800]{2,1,0:T(8,128)(2,1)} %param.20) | copy-start | bytes 1920004
  4.8 10.9 %collective-permute-start = (bf16[800,1024]{1,0:T(8,128)(2,1)}, bf16[800,1024]{1,0:T(8,128)(2,1)}, u32[]{:S(2)}, u32[]{:S(2)}) collective-permute-start(bf16[800,1024]{1,0:T(8,128)(2,1)} %get-tuple-element.43), channel_id=1, source_target_pairs={{0,16},{16,0},{1,17},{17,1},{2,18},{18,2},{3,19},{19,3},{4,20},{20... | collective-permute-start | bytes 4915208 | tf_op jit(solution)/shard_map/ppermute | solution.py:764
  5.4 8.2 %collective-permute-start.4 = (bf16[5,400,400]{2,1,0:T(8,128)(2,1)S(1)}, bf16[5,400,400]{2,1,0:T(8,128)(2,1)S(1)}, u32[]{:S(2)}, u32[]{:S(2)}) collective-permute-start(bf16[5,400,400]{2,1,0:T(8,128)(2,1)S(1)} %bitcast.36), channel_id=1, source_target_pairs={{0,16},{16,0},{1,17},{17,1},{2,18},{18,2},{3,19},{19,3},{4,20},{20... | collective-permute-start | bytes 4800008 | tf_op jit(solution)/shard_map/ppermute | solution.py:764
  5.4 6.8 %collective-permute-start.2 = (bf16[400,800]{1,0:T(8,128)(2,1)}, bf16[400,800]{1,0:T(8,128)(2,1)S(1)}, u32[]{:S(2)}, u32[]{:S(2)}) collective-permute-start(bf16[400,800]{1,0:T(8,128)(2,1)} %bitcast.42), channel_id=1, source_target_pairs={{0,16},{16,0},{1,17},{17,1},{2,18},{18,2},{3,19},{19,3},{4,20},{20... | collective-permute-start | bytes 1920008 | tf_op jit(solution)/shard_map/ppermute | solution.py:764
  5.9 7.6 %collective-permute-start.3 = (bf16[400,800]{1,0:T(8,128)(2,1)S(1)}, bf16[400,800]{1,0:T(8,128)(2,1)S(1)}, u32[]{:S(2)}, u32[]{:S(2)}) collective-permute-start(bf16[400,800]{1,0:T(8,128)(2,1)S(1)} %bitcast.41), channel_id=1, source_target_pairs={{0,16},{16,0},{1,17},{17,1},{2,18},{18,2},{3,19},{19,3},{4,20},{20... | collective-permute-start | bytes 1920008 | tf_op jit(solution)/shard_map/ppermute | solution.py:764
  6.0 6.3 %collective-permute-start.1 = (f32[8,800]{1,0:T(8,128)}, f32[8,800]{1,0:T(8,128)S(1)}, u32[]{:S(2)}, u32[]{:S(2)}) collective-permute-start(f32[8,800]{1,0:T(8,128)} %get-tuple-element.44.refs_3_.small_own), channel_id=1, source_target_pairs={{0,16},{16,0},{1,17},{17,1},{2,18},{18,2},{3,19},{19,3},{4,20},{20... | collective-permute-start | bytes 76808 | tf_op jit(solution)/shard_map/ppermute | solution.py:764
  12.3 3.5 %copy-start.13 = (f32[8,800]{1,0:T(8,128)}, f32[8,800]{1,0:T(8,128)S(1)}, u32[]{:S(2)}) copy-start(f32[8,800]{1,0:T(8,128)S(1)} %collective-permute-done.1.refs_4_.small_got) | copy-start | bytes 76804
  12.3 3.5 %copy-start.11 = (bf16[400,800]{1,0:T(8,128)(2,1)}, bf16[400,800]{1,0:T(8,128)(2,1)S(1)}, u32[]{:S(2)}) copy-start(bf16[400,800]{1,0:T(8,128)(2,1)S(1)} %collective-permute-done.2.refs_8_.got_in) | copy-start | bytes 1920004
  13.5 0.9 copy-start.12
  14.4 1.3 copy-start.7
  72.3 19.7 %copy-start.9 = (bf16[4864,128]{1,0:T(8,128)(2,1)S(1)}, bf16[4864,128]{1,0:T(8,128)(2,1)}, u32[]{:S(2)}) copy-start(bf16[4864,128]{1,0:T(8,128)(2,1)} %get-tuple-element.67) | copy-start | bytes 3735556
  91.5 8.8 %copy-start.2 = (bf16[4864,128]{1,0:T(8,128)(2,1)S(1)}, bf16[4864,128]{1,0:T(8,128)(2,1)}, u32[]{:S(2)}) copy-start(bf16[4864,128]{1,0:T(8,128)(2,1)} %get-tuple-element.66) | copy-start | bytes 3735556
  91.5 4.8 %collective-permute-start.7 = (bf16[6144,128]{1,0:T(8,128)(2,1)}, bf16[6144,128]{1,0:T(8,128)(2,1)S(1)}, u32[]{:S(2)}, u32[]{:S(2)}) collective-permute-start(bf16[6144,128]{1,0:T(8,128)(2,1)} %get-tuple-element.65), channel_id=1, source_target_pairs={{0,16},{16,0},{1,17},{17,1},{2,18},{18,2},{3,19},{19,3},{4,20},{20... | collective-permute-start | bytes 4718600 | tf_op jit(solution)/shard_map/ppermute | solution.py:764
  92.0 8.4 %collective-permute-start.20 = (bf16[4864,128]{1,0:T(8,128)(2,1)S(1)}, bf16[4864,128]{1,0:T(8,128)(2,1)S(1)}, u32[]{:S(2)}, u32[]{:S(2)}) collective-permute-start(bf16[4864,128]{1,0:T(8,128)(2,1)S(1)} %copy-done.9), channel_id=1, source_target_pairs={{0,16},{16,0},{1,17},{17,1},{2,18},{18,2},{3,19},{19,3},{4,20},{20... | collective-permute-start | bytes 3735560 | tf_op jit(solution)/shard_map/ppermute | solution.py:764
  96.3 14.0 %copy-start.1 = (bf16[6144,128]{1,0:T(8,128)(2,1)S(1)}, bf16[6144,128]{1,0:T(8,128)(2,1)}, u32[]{:S(2)}) copy-start(bf16[6144,128]{1,0:T(8,128)(2,1)} %get-tuple-element.64) | copy-start | bytes 4718596
  97.8 12.5 %collective-permute-start.8 = (bf16[3072,128]{1,0:T(8,128)(2,1)S(1)}, bf16[3072,128]{1,0:T(8,128)(2,1)S(1)}, u32[]{:S(2)}, u32[]{:S(2)}) collective-permute-start(bf16[3072,128]{1,0:T(8,128)(2,1)S(1)} %add_convert_fusion), channel_id=1, source_target_pairs={{0,1},{1,0},{2,3},{3,2},{4,5},{5,4},{6,7},{7,6},{8,9},{9,8},{10,11... | collective-permute-start | bytes 2359304 | tf_op jit(solution)/shard_map/ppermute | solution.py:770
  100.5 20.7 %collective-permute-start.21 = (bf16[2432,128]{1,0:T(8,128)(2,1)S(1)}, bf16[2432,128]{1,0:T(8,128)(2,1)S(1)}, u32[]{:S(2)}, u32[]{:S(2)}) collective-permute-start(bf16[2432,128]{1,0:T(8,128)(2,1)S(1)} %add_convert_fusion.1), channel_id=1, source_target_pairs={{0,1},{1,0},{2,3},{3,2},{4,5},{5,4},{6,7},{7,6},{8,9},{9,8},{10,11... | collective-permute-start | bytes 1867784 | tf_op jit(solution)/shard_map/ppermute | solution.py:770
  110.5 13.0 %collective-permute-start.9 = (bf16[1536,128]{1,0:T(8,128)(2,1)S(1)}, bf16[1536,128]{1,0:T(8,128)(2,1)S(1)}, u32[]{:S(2)}, u32[]{:S(2)}) collective-permute-start(bf16[1536,128]{1,0:T(8,128)(2,1)S(1)} %add_convert_fusion.2), channel_id=1, source_target_pairs={{0,2},{1,3},{2,0},{3,1},{4,6},{5,7},{6,4},{7,5},{8,10},{9,11},{10,... | collective-permute-start | bytes 1179656 | tf_op jit(solution)/shard_map/ppermute | solution.py:770
  121.3 7.0 %collective-permute-start.22 = (bf16[1216,128]{1,0:T(8,128)(2,1)S(1)}, bf16[1216,128]{1,0:T(8,128)(2,1)S(1)}, u32[]{:S(2)}, u32[]{:S(2)}) collective-permute-start(bf16[1216,128]{1,0:T(8,128)(2,1)S(1)} %add_convert_fusion.6), channel_id=1, source_target_pairs={{0,2},{1,3},{2,0},{3,1},{4,6},{5,7},{6,4},{7,5},{8,10},{9,11},{10,... | collective-permute-start | bytes 933896 | tf_op jit(solution)/shard_map/ppermute | solution.py:770
  123.6 7.1 %collective-permute-start.10 = (bf16[384,128]{1,0:T(8,128)(2,1)S(1)}, bf16[384,128]{1,0:T(8,128)(2,1)S(1)}, u32[]{:S(2)}, u32[]{:S(2)}) collective-permute-start(bf16[384,128]{1,0:T(8,128)(2,1)S(1)} %get-tuple-element.78), channel_id=1, source_target_pairs={{0,4},{1,5},{2,6},{3,7},{4,0},{5,1},{6,2},{7,3},{8,12},{9,13},{10,... | collective-permute-start | bytes 294920 | tf_op jit(solution)/shard_map/ppermute | solution.py:770
  125.3 8.2 %collective-permute-start.12 = (bf16[384,128]{1,0:T(8,128)(2,1)S(1)}, bf16[384,128]{1,0:T(8,128)(2,1)S(1)}, u32[]{:S(2)}, u32[]{:S(2)}) collective-permute-start(bf16[384,128]{1,0:T(8,128)(2,1)S(1)} %get-tuple-element.79), channel_id=1, source_target_pairs={{0,12},{1,13},{2,14},{3,15},{4,8},{5,9},{6,10},{7,11},{8,4},{9,5},... | collective-permute-start | bytes 294920 | tf_op jit(solution)/shard_map/ppermute | solution.py:770
  127.8 17.6 %copy-start.8 = (bf16[800,1024]{1,0:T(8,128)(2,1)S(1)}, bf16[800,1024]{1,0:T(8,128)(2,1)}, u32[]{:S(2)}) copy-start(bf16[800,1024]{1,0:T(8,128)(2,1)} %get-tuple-element.46) | copy-start | bytes 4915204
  127.8 7.5 %collective-permute-start.11 = (bf16[384,128]{1,0:T(8,128)(2,1)S(1)}, bf16[384,128]{1,0:T(8,128)(2,1)S(1)}, u32[]{:S(2)}, u32[]{:S(2)}) collective-permute-start(bf16[384,128]{1,0:T(8,128)(2,1)S(1)} %get-tuple-element.80), channel_id=1, source_target_pairs={{0,8},{1,9},{2,10},{3,11},{4,12},{5,13},{6,14},{7,15},{8,0},{9,1},... | collective-permute-start | bytes 294920 | tf_op jit(solution)/shard_map/ppermute | solution.py:770
  128.5 13.9 %collective-permute-start.23 = (bf16[1216,128]{1,0:T(8,128)(2,1)S(1)}, bf16[1216,128]{1,0:T(8,128)(2,1)S(1)}, u32[]{:S(2)}, u32[]{:S(2)}) collective-permute-start(bf16[1216,128]{1,0:T(8,128)(2,1)S(1)} %add_convert_fusion.5), channel_id=1, source_target_pairs={{0,4},{1,5},{2,6},{3,7},{4,0},{5,1},{6,2},{7,3},{8,12},{9,13},{10,... | collective-permute-start | bytes 933896 | tf_op jit(solution)/shard_map/ppermute | solution.py:770
  135.4 10.0 %collective-permute-start.15 = (bf16[384,128]{1,0:T(8,128)(2,1)S(1)}, bf16[384,128]{1,0:T(8,128)(2,1)S(1)}, u32[]{:S(2)}, u32[]{:S(2)}) collective-permute-start(bf16[384,128]{1,0:T(8,128)(2,1)S(1)} %get-tuple-element.77), channel_id=1, source_target_pairs={{0,12},{1,13},{2,14},{3,15},{4,8},{5,9},{6,10},{7,11},{8,4},{9,5},... | collective-permute-start | bytes 294920 | tf_op jit(solution)/shard_map/ppermute | solution.py:770
  138.7 14.8 %collective-permute-start.14 = (bf16[384,128]{1,0:T(8,128)(2,1)S(1)}, bf16[384,128]{1,0:T(8,128)(2,1)S(1)}, u32[]{:S(2)}, u32[]{:S(2)}) collective-permute-start(bf16[384,128]{1,0:T(8,128)(2,1)S(1)} %get-tuple-element.77), channel_id=1, source_target_pairs={{0,8},{1,9},{2,10},{3,11},{4,12},{5,13},{6,14},{7,15},{8,0},{9,1},... | collective-permute-start | bytes 294920 | tf_op jit(solution)/shard_map/ppermute | solution.py:770
  138.7 14.8 %collective-permute-start.13 = (bf16[384,128]{1,0:T(8,128)(2,1)S(1)}, bf16[384,128]{1,0:T(8,128)(2,1)S(1)}, u32[]{:S(2)}, u32[]{:S(2)}) collective-permute-start(bf16[384,128]{1,0:T(8,128)(2,1)S(1)} %get-tuple-element.77), channel_id=1, source_target_pairs={{0,4},{1,5},{2,6},{3,7},{4,0},{5,1},{6,2},{7,3},{8,12},{9,13},{10,... | collective-permute-start | bytes 294920 | tf_op jit(solution)/shard_map/ppermute | solution.py:770
  142.5 16.7 %collective-permute-start.24 = (bf16[1216,128]{1,0:T(8,128)(2,1)S(1)}, bf16[1216,128]{1,0:T(8,128)(2,1)S(1)}, u32[]{:S(2)}, u32[]{:S(2)}) collective-permute-start(bf16[1216,128]{1,0:T(8,128)(2,1)S(1)} %add_convert_fusion.4), channel_id=1, source_target_pairs={{0,8},{1,9},{2,10},{3,11},{4,12},{5,13},{6,14},{7,15},{8,0},{9,1},... | collective-permute-start | bytes 933896 | tf_op jit(solution)/shard_map/ppermute | solution.py:770
  145.4 29.5 %collective-permute-start.5 = (bf16[800,1024]{1,0:T(8,128)(2,1)S(1)}, bf16[800,1024]{1,0:T(8,128)(2,1)S(1)}, u32[]{:S(2)}, u32[]{:S(2)}) collective-permute-start(bf16[800,1024]{1,0:T(8,128)(2,1)S(1)} %copy-done.8), channel_id=1, source_target_pairs={{0,16},{16,0},{1,17},{17,1},{2,18},{18,2},{3,19},{19,3},{4,20},{20... | collective-permute-start | bytes 4915208 | tf_op jit(solution)/shard_map/ppermute | solution.py:764
  145.4 39.4 %collective-permute-start.6 = (bf16[800,1024]{1,0:T(8,128)(2,1)}, bf16[800,1024]{1,0:T(8,128)(2,1)}, u32[]{:S(2)}, u32[]{:S(2)}) collective-permute-start(bf16[800,1024]{1,0:T(8,128)(2,1)} %get-tuple-element.63), channel_id=1, source_target_pairs={{0,16},{16,0},{1,17},{17,1},{2,18},{18,2},{3,19},{19,3},{4,20},{20... | collective-permute-start | bytes 4915208 | tf_op jit(solution)/shard_map/ppermute | solution.py:764
  153.6 7.8 %collective-permute-start.16 = (bf16[1536,128]{1,0:T(8,128)(2,1)S(1)}, bf16[1536,128]{1,0:T(8,128)(2,1)S(1)}, u32[]{:S(2)}, u32[]{:S(2)}) collective-permute-start(bf16[1536,128]{1,0:T(8,128)(2,1)S(1)} %pad_maximum_fusion.1), channel_id=1, source_target_pairs={{0,2},{1,3},{2,0},{3,1},{4,6},{5,7},{6,4},{7,5},{8,10},{9,11},{10,... | collective-permute-start | bytes 1179656 | tf_op jit(solution)/shard_map/ppermute | solution.py:770
  159.3 10.2 %collective-permute-start.25 = (bf16[1216,128]{1,0:T(8,128)(2,1)S(1)}, bf16[1216,128]{1,0:T(8,128)(2,1)S(1)}, u32[]{:S(2)}, u32[]{:S(2)}) collective-permute-start(bf16[1216,128]{1,0:T(8,128)(2,1)S(1)} %add_convert_fusion.3), channel_id=1, source_target_pairs={{0,2},{1,3},{2,0},{3,1},{4,6},{5,7},{6,4},{7,5},{8,10},{9,11},{10,... | collective-permute-start | bytes 933896 | tf_op jit(solution)/shard_map/ppermute | solution.py:770
  161.5 23.4 %copy-start.3 = (bf16[3072,128]{1,0:T(8,128)(2,1)}, bf16[3072,128]{1,0:T(8,128)(2,1)S(1)}, u32[]{:S(2)}) copy-start(bf16[3072,128]{1,0:T(8,128)(2,1)S(1)} %constant_dynamic-update-slice_fusion.refs_0_) | copy-start | bytes 2359300
  161.5 12.2 %collective-permute-start.17 = (bf16[3072,128]{1,0:T(8,128)(2,1)S(1)}, bf16[3072,128]{1,0:T(8,128)(2,1)}, u32[]{:S(2)}, u32[]{:S(2)}) collective-permute-start(bf16[3072,128]{1,0:T(8,128)(2,1)S(1)} %constant_dynamic-update-slice_fusion.refs_0_), channel_id=1, source_target_pairs={{0,1},{1,0},{2,3},{3,2},{4,5},{5,4},{6,7},{7,6},{8,9},{9,8},{10,11... | collective-permute-start | bytes 2359304 | tf_op jit(solution)/shard_map/ppermute | solution.py:770
  169.6 15.3 %copy-start = (bf16[2432,128]{1,0:T(8,128)(2,1)}, bf16[2432,128]{1,0:T(8,128)(2,1)S(1)}, u32[]{:S(2)}) copy-start(bf16[2432,128]{1,0:T(8,128)(2,1)S(1)} %pad_maximum_fusion.refs_4_) | copy-start | bytes 1867780
  169.6 10.7 %collective-permute-start.26 = (bf16[2432,128]{1,0:T(8,128)(2,1)S(1)}, bf16[2432,128]{1,0:T(8,128)(2,1)}, u32[]{:S(2)}, u32[]{:S(2)}) collective-permute-start(bf16[2432,128]{1,0:T(8,128)(2,1)S(1)} %pad_maximum_fusion.refs_4_), channel_id=1, source_target_pairs={{0,1},{1,0},{2,3},{3,2},{4,5},{5,4},{6,7},{7,6},{8,9},{9,8},{10,11... | collective-permute-start | bytes 1867784 | tf_op jit(solution)/shard_map/ppermute | solution.py:770
  171.2 16.5 %collective-permute-start.18 = (bf16[3072,128]{1,0:T(8,128)(2,1)S(1)}, bf16[3072,128]{1,0:T(8,128)(2,1)}, u32[]{:S(2)}, u32[]{:S(2)}) collective-permute-start(bf16[3072,128]{1,0:T(8,128)(2,1)S(1)} %constant_dynamic-update-slice_fusion.refs_0_), channel_id=1, source_target_pairs={{16,0},{17,1},{18,2},{19,3},{20,4},{21,5},{22,6},{23,7},{24,8},{25... | collective-permute-start | bytes 2359304 | tf_op jit(solution)/shard_map/ppermute | solution.py:804
  173.7 15.8 %collective-permute-start.19 = (bf16[3072,128]{1,0:T(8,128)(2,1)}, bf16[3072,128]{1,0:T(8,128)(2,1)}, u32[]{:S(2)}, u32[]{:S(2)}) collective-permute-start(bf16[3072,128]{1,0:T(8,128)(2,1)} %collective-permute-done.17.refs_1_), channel_id=1, source_target_pairs={{16,0},{17,1},{18,2},{19,3},{20,4},{21,5},{22,6},{23,7},{24,8},{25... | collective-permute-start | bytes 2359304 | tf_op jit(solution)/shard_map/ppermute | solution.py:804
  175.0 12.8 %collective-permute-start.27 = (bf16[2432,128]{1,0:T(8,128)(2,1)S(1)}, bf16[2432,128]{1,0:T(8,128)(2,1)}, u32[]{:S(2)}, u32[]{:S(2)}) collective-permute-start(bf16[2432,128]{1,0:T(8,128)(2,1)S(1)} %pad_maximum_fusion.refs_4_), channel_id=1, source_target_pairs={{0,16},{1,17},{2,18},{3,19},{4,20},{5,21},{6,22},{7,23},{8,24},{9,... | collective-permute-start | bytes 1867784 | tf_op jit(solution)/shard_map/ppermute | solution.py:804
  180.3 9.1 %collective-permute-start.28 = (bf16[2432,128]{1,0:T(8,128)(2,1)}, bf16[2432,128]{1,0:T(8,128)(2,1)}, u32[]{:S(2)}, u32[]{:S(2)}) collective-permute-start(bf16[2432,128]{1,0:T(8,128)(2,1)} %collective-permute-done.26.refs_5_), channel_id=1, source_target_pairs={{0,16},{1,17},{2,18},{3,19},{4,20},{5,21},{6,22},{7,23},{8,24},{9,... | collective-permute-start | bytes 1867784 | tf_op jit(solution)/shard_map/ppermute | solution.py:804
  183.6 2.5 %copy-start.4 = (bf16[2,800,1024]{2,1,0:T(8,128)(2,1)S(1)}, bf16[2,800,1024]{2,1,0:T(8,128)(2,1)}, u32[]{:S(2)}) copy-start(bf16[2,800,1024]{2,1,0:T(8,128)(2,1)} %get-tuple-element.62) | copy-start | bytes 9830404
  187.7 1.7 copy-start.5

commit v3 on v2

v3 whole, which is shorter than its diff:
```python
import functools

import jax
import jax.numpy as jnp
from jax import lax
from jax.experimental import pallas as pl
from jax.experimental.pallas import tpu as pltpu
from jax.sharding import PartitionSpec as P

DEC_TAPS = 3
EPS = 1e-05
LANES = 128
CHUNK = 80
VEC_ROWS = 48
SMALL_ROWS = 8
PIECES = 5
BF = jnp.bfloat16
F32 = jnp.float32
VMEM_LIMIT = 62 * 2**20
SMALL_LIMIT = 62 * 2**20
SEQ = "ddedeydexdede"
ANY = pl.BlockSpec(memory_space=pl.ANY)
SMEM = pl.BlockSpec(memory_space=pltpu.SMEM)
VMEM = pl.BlockSpec(memory_space=pltpu.VMEM)


def shape(dims, dtype):
    return jax.ShapeDtypeStruct(tuple(dims), dtype)


def nn(left, right):
    return jnp.dot(left, right, preferred_element_type=F32)


def nt(left, right):
    return lax.dot_general(left, right, (((1,), (1,)), ((), ())), preferred_element_type=F32)


def tn(left, right):
    return lax.dot_general(left, right, (((0,), (0,)), ((), ())), preferred_element_type=F32)


def lane_block(index):
    return pl.ds(pl.multiple_of(index * LANES, LANES), LANES)


def chunks(rows):
    size = CHUNK if rows % CHUNK == 0 else 16
    return [slice(at, at + size) for at in range(0, rows, size)]


def folded(values):
    return jnp.sum(values.reshape(values.shape[0] // 8, 8, values.shape[1]), 0)


def column(vector):
    return jnp.broadcast_to(vector, (LANES, vector.shape[1])).T


def norm_forward(source, half_gain, half_bias, normed, slope, hidden, devs, row):
    feats, tokens = source.shape
    scale = 1.0 / feats

    def stats(unit):
        here = lane_block(unit)
        base = source[0:1, here].astype(F32)
        total = jnp.zeros((8, LANES), F32)
        squares = jnp.zeros((8, LANES), F32)
        for part in chunks(feats):
            moved = source[part, here].astype(F32) - base
            total = total + folded(moved)
            squares = squares + folded(moved * moved)
        average = jnp.sum(total, 0, keepdims=True) * scale
        variance = jnp.sum(squares, 0, keepdims=True) * scale - average * average
        inverse_dev = lax.rsqrt(jnp.maximum(variance, 0.0) + EPS)
        return (average + base) * inverse_dev, inverse_dev

    def body(unit, carry):
        following = stats(jnp.minimum(unit + 1, tokens // LANES - 1))
        offset, inverse_dev = carry
        here = lane_block(unit)
        devs[row : row + 1, here] = inverse_dev
        for part in chunks(feats):
            values = source[part, here].astype(F32) * inverse_dev - offset
            gain = half_gain[part, :]
            half = values * gain + half_bias[part, :]
            tan = jnp.tanh(half)
            weight = 1.0 + tan
            out = half * weight
            normed[part, here] = values.astype(BF)
            slope[part, here] = ((weight + out * (1.0 - tan)) * gain).astype(BF)
            hidden[part, here] = out.astype(hidden.dtype)
        return following

    lax.fori_loop(0, tokens // LANES, body, stats(0))


def norm_backward(gradient, slope, normed, devs, row, gain_sums, bias_sums, means, emit):
    feats, tokens = gradient.shape
    units = tokens // LANES
    scale = 1.0 / feats
    size = CHUNK if feats % CHUNK == 0 else 16
    means[...] = jnp.zeros_like(means)

    def collect(index, _):
        rows = pl.ds(pl.multiple_of(index * size, 16), size)
        gain_sum = jnp.zeros((size, LANES), F32)
        bias_sum = jnp.zeros((size, LANES), F32)
        for unit in range(units):
            here = slice(unit * LANES, (unit + 1) * LANES)
            scaled = gradient[rows, here] * slope[rows, here].astype(F32)
            weighted = scaled * normed[rows, here].astype(F32)
            gain_sum = gain_sum + weighted
            bias_sum = bias_sum + scaled
            means[0:8, here] += folded(scaled)
            means[8:16, here] += folded(weighted)
        gain_sums[rows, :] = gain_sum
        bias_sums[rows, :] = bias_sum
        return 0

    lax.fori_loop(0, feats // size, collect, 0)

    def finish(unit, _):
        here = lane_block(unit)
        inverse_dev = devs[row : row + 1, here]
        first = jnp.sum(means[0:8, here], 0, keepdims=True) * (scale * inverse_dev)
        second = jnp.sum(means[8:16, here], 0, keepdims=True) * (scale * inverse_dev)
        for part in chunks(feats):
            scaled = gradient[part, here] * slope[part, here].astype(F32)
            emit(part, here, scaled * inverse_dev - first - normed[part, here].astype(F32) * second)
        return 0

    lax.fori_loop(0, units, finish, 0, unroll=2)


def write_shifts(source, target, begins, offsets):
    feats, tokens = source.shape
    units = tokens // LANES

    def body(unit, _):
        here = lane_block(unit)
        behind_unit = jnp.maximum(unit - 1, 0)
        ahead_unit = jnp.minimum(unit + 1, units - 1)
        joined_behind = ((unit > 0) & (begins(unit) == 0)).astype(F32)
        joined_ahead = ((unit < units - 1) & (begins(ahead_unit) == 0)).astype(F32)
        for part in chunks(feats):
            size = part.stop - part.start
            lane = lax.broadcasted_iota(jnp.int32, (size, LANES), 1)
            current = source[part, here].astype(F32)
            behind = source[part, lane_block(behind_unit)].astype(F32) * joined_behind
            ahead = source[part, lane_block(ahead_unit)].astype(F32) * joined_ahead
            for position, (sign, step) in enumerate(offsets):
                if sign == 0:
                    moved = current
                elif sign < 0:
                    moved = pltpu.roll(jnp.where(lane < LANES - step, current, behind), step, 1)
                else:
                    moved = pltpu.roll(jnp.where(lane >= step, current, ahead), LANES - step, 1)
                target[feats * position + part.start : feats * position + part.stop, here] = moved.astype(BF)
        return 0

    lax.fori_loop(0, units, body, 0, unroll=2)


def tap_offsets(taps, dilation, flip):
    result = []
    for position in range(taps):
        factor = (position - 2) * (-1 if flip else 1)
        result.append(((factor > 0) - (factor < 0), abs(factor) * dilation))
    return result


def layout(taps, width, inner):
    wide = pl.cdiv(width, LANES) * inner
    taps_at = wide
    tails_at = taps_at + taps * (inner // LANES) * inner
    w_in_at = tails_at + inner
    vec_at = w_in_at + wide
    return taps_at, tails_at, w_in_at, vec_at, vec_at + VEC_ROWS


def scatter_groups(count, full):
    total = count.bit_length() - 1
    rest = [list(range(2, min(4, total)))] if full and total > 2 else []
    return [[[bit] for bit in bits if bit < total] + rest for bits in ((0, 1), (1, 0))]


def share_count(groups):
    return 2 ** sum(len(bits) for bits in groups)


def padded_rows(rows, groups):
    unit = 2 * 16 * share_count(groups[0])
    return pl.cdiv(rows, unit) * unit


def put_slabs(buf, row, matrix):
    rows, cols = matrix.shape
    for q in range(pl.cdiv(cols, LANES)):
        part = matrix[:, LANES * q : min(cols, LANES * (q + 1))]
        if part.shape[1] < LANES:
            part = jnp.concatenate([part, jnp.zeros((rows, LANES - part.shape[1]), F32)], 1)
        buf[row + q * rows : row + (q + 1) * rows, :] = part.astype(BF)


def put_taps(buf, taps, width, shifted, grad_mixed, ready):
    inner = grad_mixed.shape[0]
    taps_at, tails_at, _, _, _ = layout(taps, width, inner)
    whole = inner // LANES
    tail = inner - whole * LANES
    for k in range(taps):
        grad = nt(shifted[inner * k : inner * (k + 1), :], grad_mixed[...])
        for q in range(whole):
            at = taps_at + inner * (whole * k + q)
            buf[at : at + inner, :] = grad[:, LANES * q : LANES * (q + 1)].astype(BF)
        buf[tails_at : tails_at + inner, tail * k : tail * (k + 1)] = grad[:, LANES * whole :].astype(BF)
        if k == taps - 2:
            ready(taps_at, taps_at + inner * whole * (taps - 1))
    buf[tails_at : tails_at + inner, tail * taps :] = jnp.zeros((inner, LANES - tail * taps), BF)
    ready(taps_at + inner * whole * (taps - 1), tails_at + inner)


def row_sums(acc):
    return jnp.sum(acc.T, 0, keepdims=True)


def put_vectors(buf, at, vec, sums):
    vec[...] = jnp.zeros_like(vec)
    row = 0
    for total in sums:
        for lane in range(0, total.shape[1], LANES):
            part = total[:, lane : lane + LANES]
            vec[row : row + 1, 0 : part.shape[1]] = part
            row += 1
    buf[at : at + VEC_ROWS, :] = vec[...].astype(BF)


def relative_index(position, groups):
    result = 0
    for bits in reversed(groups):
        size = 2 ** len(bits)
        result = result + (position & (size - 1)) * 2 ** bits[0]
        position = position >> len(bits)
    return result


def owner_of(position, side, groups, index):
    both = [relative_index(position, order) for order in groups]
    mask = sum(2**bit for bits in groups[0] for bit in bits)
    return jnp.where(side == 0, both[0], both[1]) ^ (index & mask)


def position_of(owner, side, groups, index):
    distance = owner ^ index
    position = 0
    for bits in groups[side]:
        position = position * 2 ** len(bits) + ((distance >> bits[0]) & (2 ** len(bits) - 1))
    return position


class RowsOut:
    def __init__(self, buf, keep, send, section, index, groups, sems):
        self.buf, self.keep, self.send, self.sems = buf, keep, send, sems
        self.section, self.index, self.groups = section, index, groups
        self.count = share_count(groups[0])
        self.share = keep.shape[0] // self.count
        self.sizes = []

    def start(self, first, last):
        for number in range(2 * self.count):
            low, high = max(first, number * self.share), min(last, (number + 1) * self.share)
            if low >= high:
                continue
            side, owner = divmod(number, self.count)
            place = position_of(owner, side, self.groups, self.index) * self.share + (low - number * self.share)
            target = pl.ds(pl.multiple_of(place, 16), high - low)
            source = self.buf.at[low:high]
            sem = self.sems.at[len(self.sizes)]
            pl.when(self.section == side)(pltpu.make_async_copy(source, self.keep.at[target], sem).start)
            pl.when(self.section != side)(pltpu.make_async_copy(source, self.send.at[target], sem).start)
            self.sizes.append(high - low)

    def wait(self):
        for number, size in enumerate(self.sizes):
            source, target = self.buf.at[0:size], self.keep.at[0:size]
            pltpu.make_async_copy(source, target, self.sems.at[number]).wait()


def forward_block(taps, begins, dilation, x, y, weights, cols, kept, hmid, prod):
    w_in_t, w_out, conv = weights
    g1, b1, g2, b2, g3, b3, ob = cols
    n1, s1, r, n2, s2, n3, s3, hin, shifted, hout = kept
    inner, tokens = hmid.shape
    narrow = prod.at[0:inner]
    norm_forward(x, g1, b1, n1, s1, hin, r, 0)
    narrow[...] = nn(w_in_t[...], hin[...])
    norm_forward(narrow, g2, b2, n2, s2, hmid, r, 1)
    write_shifts(hmid, shifted, begins, tap_offsets(taps, dilation, False))
    narrow[...] = tn(conv[...].reshape(taps * inner, inner), shifted[...])
    norm_forward(narrow, g3, b3, n3, s3, hout, r, 2)
    bias = jnp.concatenate([ob[...]] * (tokens // LANES), 1)
    y[...] = (x[...].astype(F32) + tn(w_out[...], hout[...]) + bias).astype(BF)


def fill_columns(small, cols):
    g1, b1, g2, b2, g3, b3, ob = cols
    width, inner = g1.shape[0], g2.shape[0]
    for target, row, scale in ((g1, 0, 0.5), (b1, 1, 0.5), (ob, 2, 1.0)):
        target[...] = column(small[row : row + 1, 0:width] * scale)
    for target, row in ((g2, 3), (b2, 4), (g3, 5), (b3, 6)):
        target[...] = column(small[row : row + 1, 0:inner] * 0.5)


def back_third(gy, w_out, kept, prod, means, grad_mixed, gain_sums, bias_sums, ready):
    n3, s3, r = kept
    inner = w_out.shape[0]
    narrow = prod.at[0:inner]
    narrow[...] = nn(w_out[...], gy[...])
    ready()

    def emit(part, here, value):
        grad_mixed[part, here] = value.astype(BF)

    norm_backward(narrow, s3, n3, r, 2, gain_sums, bias_sums, means, emit)


def back_second(
    taps, begins, dilation, conv_w, kept, prod, means, grad_mixed, moved, grad_projected, gain_sums, bias_sums, ready,
    weights=None,
):
    n2, s2, r = kept
    inner = grad_mixed.shape[0]
    narrow = prod.at[0:inner]
    write_shifts(grad_mixed, moved, begins, tap_offsets(taps, dilation, True))
    if weights is not None:
        weights()
    narrow[...] = nn(conv_w[...], moved[...])
    ready()

    def emit(part, here, value):
        grad_projected[part, here] = value.astype(BF)

    norm_backward(narrow, s2, n2, r, 1, gain_sums, bias_sums, means, emit)


def back_first(gy, w_in_t, kept, prod, means, grad_projected, gx, gain_sums, bias_sums, ready):
    n1, s1, r = kept
    prod[...] = tn(w_in_t[...], grad_projected[...])
    ready()

    def emit(part, here, value):
        gx[part, here] = (gy[part, here].astype(F32) + value).astype(BF)

    norm_backward(prod, s1, n1, r, 0, gain_sums, bias_sums, means, emit)


def put_w_out(buf, hout_ones, gy):
    grad = nt(hout_ones[...], gy[...])
    inner = hout_ones.shape[0] - 16
    put_slabs(buf, 0, grad[0:inner])
    return grad[inner : inner + 1]


def gain_and_bias(gain, sums):
    return [row_sums(acc[...]) / gain for acc in sums]


def put_rows(target, rows):
    target[...] = jnp.zeros_like(target)
    for at, row in enumerate(rows):
        target[at : at + 1, 0 : row.shape[1]] = row


def gains_of(small, width, inner):
    return small[0:1, 0:width], small[3:4, 0:inner], small[5:6, 0:inner]


def pick_small(leading, own, got):
    flag = leading.astype(F32)
    return own[...] * flag + got[...] * (1.0 - flag)


def start_all(copies):
    for copy in copies:
        copy.start()


def prepare_kernel(rows, gin, bin_, gmid, bmid, out_bias, dilation, send, small, hold, sem):
    section = lax.axis_index("section")
    size = send.shape[0] // PIECES
    arrive = [pltpu.make_async_copy(rows.at[1 - section, size * i : size * (i + 1)], hold.at[i], sem.at[i]) for i in range(PIECES)]
    leave = [pltpu.make_async_copy(hold.at[i], send.at[size * i : size * (i + 1)], sem.at[PIECES + i]) for i in range(PIECES)]
    start_all(arrive)
    width, inner = gin.shape[1], gmid.shape[1]
    small[...] = jnp.zeros_like(small)
    for row, ref in ((0, gin), (1, bin_), (2, out_bias)):
        small[row : row + 1, 0:width] = ref[...]
    for row, ref, which in ((3, gmid, 0), (4, bmid, 0), (5, gmid, 1), (6, bmid, 1)):
        small[row : row + 1, 0:inner] = ref[which : which + 1, :]
    small[7:8, :] = jnp.full((1, small.shape[1]), dilation[0].astype(F32), F32)
    for come, go in zip(arrive, leave):
        come.wait()
        go.start()
    for go in leave:
        go.wait()


def prepare(rows, gin, bin_, gmid, bmid, out_bias, dilation):
    return pl.pallas_call(
        prepare_kernel,
        in_specs=[ANY] + [VMEM] * 5 + [SMEM],
        out_specs=[ANY, VMEM],
        out_shape=[shape(rows.shape[1:], BF), shape((SMALL_ROWS, rows.shape[1]), F32)],
        scratch_shapes=[
            pltpu.VMEM((PIECES, rows.shape[1] // PIECES, rows.shape[2]), BF), pltpu.SemaphoreType.DMA((2 * PIECES,))
        ],
        compiler_params=pltpu.CompilerParams(vmem_limit_bytes=VMEM_LIMIT),
        name="prepare",
    )(rows, gin, bin_, gmid, bmid, out_bias, dilation)


def kept_shapes(taps, width, inner, tokens):
    wide, narrow = (width, tokens), (inner, tokens)
    return [
        (wide, BF), (wide, BF), ((8, tokens), F32), (narrow, BF), (narrow, BF), (narrow, BF), (narrow, BF),
        (wide, BF), ((inner * taps, tokens), BF), (narrow, BF),
    ]


def column_shapes(width, inner):
    return [(width, LANES)] * 2 + [(inner, LANES)] * 4 + [(width, LANES)]


def main_kernel(taps_of, groups, *refs):
    refs = list(refs)

    def take(number):
        taken = refs[:number]
        del refs[:number]
        return taken

    seq, rows, got, small_own, small_got = take(5)
    own_w, got_w = take(3), take(3)
    outs, send_y, grad_out, keep_buf, send_buf, vec_out = take(6)
    kept_out = take(10)
    x, cot = take(2)
    enc_w, dec_w = take(3), take(3)
    small = take(2)
    enc_kept, dec_kept = take(10), take(10)
    cols = take(7)
    hmid, prod, means, y_enc, gx, conv_w, grad_mixed, grad_projected, moved, buf = take(10)
    ag1, ab1, ag2, ab2, ag3, ab3, vec, sem, row_sems = take(9)

    section = lax.axis_index("section")
    index = lax.axis_index("dp")
    leading = section == 0
    width, tokens = x.shape
    inner = hmid.shape[0]
    small[0][...] = pick_small(leading, small_own, small_got)
    small[1][...] = pick_small(leading, small_got, small_own)
    dilation = [jnp.max(member[7:8, 0:LANES]).astype(jnp.int32) for member in small]

    def begins(unit):
        return seq[section, unit]

    loads = [(x, rows.at[0], got), (enc_w[0], own_w[0], got_w[0]), (enc_w[2], own_w[2], got_w[2])]
    loads += [(enc_w[1], own_w[1], got_w[1]), (dec_w[0], got_w[0], own_w[0]), (dec_w[1], got_w[1], own_w[1])]
    loads += [(dec_w[2], got_w[2].at[0 : taps_of[1]], own_w[2].at[0 : taps_of[1]]), (cot, got, rows.at[1])]

    def load(at):
        target, first, second = loads[at]
        pl.when(leading)(pltpu.make_async_copy(first, target, sem.at[at]).start)
        pl.when(jnp.logical_not(leading))(pltpu.make_async_copy(second, target, sem.at[at]).start)

    for at in range(4):
        load(at)

    def ready(at):
        pltpu.make_async_copy(loads[at][1], loads[at][0], sem.at[at]).wait()

    fill_columns(small[0], cols)
    hout_ones = dec_kept[9]
    dec_kept[9] = hout_ones.at[0:inner]
    hout_ones[inner:, :] = jnp.ones((16, tokens), BF)
    for at in range(4):
        ready(at)
    for at in range(4, 8):
        load(at)
    forward_block(taps_of[0], begins, dilation[0], x, y_enc, enc_w, cols, enc_kept, hmid, prod)
    saves = [pltpu.make_async_copy(a, b, sem.at[8 + i]) for i, (a, b) in enumerate(zip(enc_kept, kept_out))]
    start_all(saves)

    fill_columns(small[1], cols)
    for at in range(4, 8):
        ready(at)
    for k in range(taps_of[1]):
        conv_w[:, inner * k : inner * (k + 1)] = dec_w[2][k]
    y_dec = x
    forward_block(taps_of[1], begins, dilation[1], y_enc, y_dec, dec_w, cols, dec_kept, hmid, prod)
    pl.when(leading)(pltpu.make_async_copy(y_enc, outs.at[0], sem.at[18]).start)
    pl.when(leading)(pltpu.make_async_copy(y_dec, send_y, sem.at[19]).start)
    pl.when(jnp.logical_not(leading))(pltpu.make_async_copy(y_dec, outs.at[1], sem.at[18]).start)
    pl.when(jnp.logical_not(leading))(pltpu.make_async_copy(y_enc, send_y, sem.at[19]).start)

    n1, s1, r, n2, s2, n3, s3, hin, shifted, hout = dec_kept
    rows_out = RowsOut(buf, keep_buf, send_buf, section, index, groups, row_sems)
    w_in_at, end = layout(taps_of[1], width, inner)[2:4]

    def nothing():
        pass

    back_third(cot, dec_w[1], (n3, s3, r), prod, means, grad_mixed, ag3, ab3, nothing)
    bias = put_w_out(buf, hout_ones, cot)
    rows_out.start(0, layout(taps_of[1], width, inner)[0])
    put_taps(buf, taps_of[1], width, shifted, grad_mixed, rows_out.start)
    back_second(
        taps_of[1], begins, dilation[1], conv_w, (n2, s2, r), prod, means, grad_mixed, moved, grad_projected, ag2, ab2,
        nothing,
    )
    put_slabs(buf, w_in_at, nt(grad_projected[...], hin[...]))
    rows_out.start(w_in_at, end)
    back_first(cot, dec_w[0], (n1, s1, r), prod, means, grad_projected, gx, ag1, ab1, nothing)
    last = pltpu.make_async_copy(gx, grad_out, sem.at[20])
    last.start()
    g1, g2, g3 = gains_of(small[1], width, inner)
    first, second, third = gain_and_bias(g1, (ag1, ab1)), gain_and_bias(g2, (ag2, ab2)), gain_and_bias(g3, (ag3, ab3))
    put_vectors(vec_out, 0, vec, first + [second[0], third[0], second[1], third[1], bias])
    rows_out.wait()
    wait_all(saves + [last])
    pltpu.make_async_copy(y_enc, outs.at[0], sem.at[18]).wait()
    pltpu.make_async_copy(y_dec, send_y, sem.at[19]).wait()


def main_call(taps_of, groups, seq, rows, got, small_own, small_got, own_w, got_w):
    _, width, tokens = rows.shape
    inner = own_w[1].shape[0]
    half = padded_rows(layout(taps_of[1], width, inner)[3], groups) // 2
    wide, narrow = (width, tokens), (inner, tokens)
    weight_shapes = [(inner, width), (inner, width)]
    scratch = [(wide, BF)] * 2
    for taps in taps_of:
        scratch += [(dims, BF) for dims in weight_shapes + [(taps, inner, inner)]]
    scratch += [((SMALL_ROWS, width), F32)] * 2
    scratch += kept_shapes(taps_of[0], width, inner, tokens) + kept_shapes(taps_of[1], width, inner, tokens)[:-1]
    scratch += [((inner + 16, tokens), BF)]
    scratch += [(dims, F32) for dims in column_shapes(width, inner)]
    scratch += [
        (narrow, BF), (wide, F32), ((16, tokens), F32), (wide, BF), (wide, BF), ((inner, inner * taps_of[1]), BF),
        (narrow, BF), (narrow, BF), ((inner * taps_of[1], tokens), BF), ((2 * half, LANES), BF),
    ]
    scratch += [((width, LANES), F32)] * 2 + [((inner, LANES), F32)] * 4 + [((VEC_ROWS, LANES), F32)]
    block = shape((half, LANES), BF)
    outs = [shape((2,) + wide, BF), shape(wide, BF), shape(wide, BF), block, block, shape((VEC_ROWS, LANES), BF)]
    outs += [shape(dims, dtype) for dims, dtype in kept_shapes(taps_of[0], width, inner, tokens)]
    flops = 2 * tokens * inner * (2 * width + taps_of[0] * inner + 3 * (2 * width + taps_of[1] * inner))
    return pl.pallas_call(
        functools.partial(main_kernel, taps_of, groups),
        in_specs=[SMEM, ANY, ANY, VMEM, VMEM] + [ANY] * 6,
        out_specs=[ANY] * 5 + [VMEM] + [ANY] * 10,
        out_shape=outs,
        scratch_shapes=[pltpu.VMEM(dims, dtype) for dims, dtype in scratch]
        + [pltpu.SemaphoreType.DMA((24,)), pltpu.SemaphoreType.DMA((8 * share_count(groups[0]),))],
        compiler_params=pltpu.CompilerParams(vmem_limit_bytes=VMEM_LIMIT),
        cost_estimate=pl.CostEstimate(flops=4 * flops, bytes_accessed=60 * 2**20, transcendentals=0),
        name="main_blocks",
    )(seq, rows, got, small_own, small_got, *own_w, *got_w)


def load_weight(leading, own, got, target, sem):
    pl.when(leading)(pltpu.make_async_copy(own, target, sem).start)
    pl.when(jnp.logical_not(leading))(pltpu.make_async_copy(got, target, sem).start)
    return pltpu.make_async_copy(own, target, sem)


def wait_all(copies):
    for copy in copies:
        copy.wait()


def encoder_kernel(
    taps, groups,
    seq, gy_in, small_own, small_got, n3_in, s3_in, r_in, shifted_in, hout_in, n2_in, s2_in, hin_in, own_out, got_out,
    own_conv, got_conv,
    grad_projected_out, vec_out, keep_buf, send_buf,
    gy, n3, s3, r, shifted, hout_ones, n2, s2, hin, w_out, conv, conv_w, prod, means, grad_mixed, moved, grad_projected,
    buf, ag3, ab3, ag2, ab2, sem, row_sems,
):
    section = lax.axis_index("section")
    leading = section == 0
    width, tokens = gy.shape
    inner = w_out.shape[0]
    w_in_at, end = layout(taps, width, inner)[2:4]
    hout = hout_ones.at[0:inner]
    pairs = (
        (gy_in, gy), (s3_in, s3), (n3_in, n3), (r_in, r), (hout_in, hout), (shifted_in, shifted), (n2_in, n2), (s2_in, s2),
        (hin_in, hin),
    )
    loads = [pltpu.make_async_copy(a, b, sem.at[2 + i]) for i, (a, b) in enumerate(pairs)]
    loads[0].start()
    weight = load_weight(leading, own_out, got_out, w_out, sem.at[0])
    start_all(loads[1:5])
    conv_weight = load_weight(leading, own_conv, got_conv, conv, sem.at[1])
    start_all(loads[5:])
    hout_ones[inner:, :] = jnp.ones((16, tokens), BF)
    small = pick_small(leading, small_own, small_got)
    dilation = jnp.max(small[7:8, 0:LANES]).astype(jnp.int32)

    def begins(unit):
        return seq[section, unit]

    def weights():
        conv_weight.wait()
        for k in range(taps):
            conv_w[:, inner * k : inner * (k + 1)] = conv[k]

    wait_all([weight, loads[0]])
    back_third(gy, w_out, (n3, s3, r), prod, means, grad_mixed, ag3, ab3, lambda: wait_all(loads[1:4]))
    back_second(
        taps, begins, dilation, conv_w, (n2, s2, r), prod, means, grad_mixed, moved, grad_projected, ag2, ab2,
        lambda: wait_all(loads[6:8]), weights,
    )
    out = pltpu.make_async_copy(grad_projected, grad_projected_out, sem.at[11])
    out.start()
    rows_out = RowsOut(buf, keep_buf, send_buf, section, lax.axis_index("dp"), groups, row_sems)
    loads[8].wait()
    put_slabs(buf, w_in_at, nt(grad_projected[...], hin[...]))
    rows_out.start(w_in_at, end)
    loads[4].wait()
    bias = put_w_out(buf, hout_ones, gy)
    rows_out.start(0, layout(taps, width, inner)[0])
    loads[5].wait()
    put_taps(buf, taps, width, shifted, grad_mixed, rows_out.start)
    _, g2, g3 = gains_of(small, width, inner)
    second, third = gain_and_bias(g2, (ag2, ab2)), gain_and_bias(g3, (ag3, ab3))
    put_rows(vec_out, [second[0], third[0], second[1], third[1], bias])
    out.wait()
    rows_out.wait()


def encoder_call(taps, groups, seq, gy, small_own, small_got, kept, own_out, got_out, own_conv, got_conv):
    width, tokens = gy.shape
    inner = own_out.shape[0]
    n1, s1, r, n2, s2, n3, s3, hin, shifted, hout = kept
    rows = layout(taps, width, inner)[3]
    half = padded_rows(rows, groups) // 2
    wide, narrow = (width, tokens), (inner, tokens)
    scratch = [
        (wide, BF), (narrow, BF), (narrow, BF), ((8, tokens), F32), ((inner * taps, tokens), BF),
        ((inner + 16, tokens), BF), (narrow, BF), (narrow, BF), (wide, BF), ((inner, width), BF),
        ((taps, inner, inner), BF), ((inner, inner * taps), BF), (narrow, F32), ((16, tokens), F32), (narrow, BF),
        ((inner * taps, tokens), BF), (narrow, BF), ((rows, LANES), BF),
    ]
    scratch += [((inner, LANES), F32)] * 4
    flops = 2 * tokens * inner * (3 * width + 2 * taps * inner)
    block = shape((half, LANES), BF)
    return pl.pallas_call(
        functools.partial(encoder_kernel, taps, groups),
        in_specs=[SMEM, ANY, VMEM, VMEM] + [ANY] * 12,
        out_specs=[ANY, VMEM, ANY, ANY],
        out_shape=[shape(narrow, BF), shape((SMALL_ROWS, width), F32), block, block],
        scratch_shapes=[pltpu.VMEM(dims, dtype) for dims, dtype in scratch]
        + [pltpu.SemaphoreType.DMA((12,)), pltpu.SemaphoreType.DMA((8 * share_count(groups[0]),))],
        compiler_params=pltpu.CompilerParams(vmem_limit_bytes=SMALL_LIMIT),
        cost_estimate=pl.CostEstimate(flops=4 * flops, bytes_accessed=20 * 2**20, transcendentals=0),
        name="encoder_back",
    )(
        seq, gy, small_own, small_got, n3, s3, r, shifted, hout, n2, s2, hin, own_out, got_out, own_conv, got_conv
    )


def first_kernel(
    block, gy_first, gy_second, grad_projected_in, small_own, small_got, vecs, n1_in, s1_in, r_in, own_in, got_in,
    *refs,
):
    outs_of, refs = refs[: 2 - block], refs[2 - block :]
    vec_out, gy, grad_projected, n1, s1, r, w_in_t, prod, means, gx, ag1, ab1, vec, sem = refs
    leading = lax.axis_index("section") == 0
    mine = leading if block == 0 else jnp.logical_not(leading)
    width, inner = gy.shape[0], grad_projected.shape[0]
    pairs = ((grad_projected_in, grad_projected), (s1_in, s1), (n1_in, n1), (r_in, r))
    loads = [pltpu.make_async_copy(a, b, sem.at[2 + i]) for i, (a, b) in enumerate(pairs)]
    loads[0].start()
    weight = load_weight(mine, own_in, got_in, w_in_t, sem.at[0])
    start_all(loads[1:])
    loads.append(load_weight(leading, gy_first, gy_second, gy, sem.at[1]))
    small = pick_small(mine, small_own, small_got)
    wait_all([loads[0], weight])

    def save(value, at_home, away, sem):
        pl.when(leading)(pltpu.make_async_copy(value, at_home, sem).start)
        pl.when(jnp.logical_not(leading))(pltpu.make_async_copy(value, away, sem).start)
        return pltpu.make_async_copy(value, away, sem)

    waits = []

    def ready():
        wait_all(loads[1:])
        if block == 0:
            outs, send = outs_of
            waits.append(save(gy, send, outs.at[1], sem.at[6]))

    back_first(gy, w_in_t, (n1, s1, r), prod, means, grad_projected, gx, ag1, ab1, ready)
    if block == 0:
        outs, send = outs_of
        waits.append(save(gx, outs.at[0], send, sem.at[7]))
    else:
        waits.append(pltpu.make_async_copy(gx, outs_of[0], sem.at[7]))
        waits[-1].start()
    sums = gain_and_bias(gains_of(small, width, inner)[0], (ag1, ab1))
    sums += [vecs[row : row + 1, 0:size] for row, size in enumerate((inner, inner, inner, inner, width))]
    put_vectors(vec_out, 0, vec, sums)
    wait_all(waits)


def first_call(block, gy_first, gy_second, grad_projected, vecs, kept, small_own, small_got, own_in, got_in):
    n1, s1, r = kept
    width, tokens = n1.shape
    inner = grad_projected.shape[0]
    wide, narrow = (width, tokens), (inner, tokens)
    scratch = [
        (wide, BF), (narrow, BF), (wide, BF), (wide, BF), ((8, tokens), F32), ((inner, width), BF), (wide, F32),
        ((16, tokens), F32), (wide, BF), ((width, LANES), F32), ((width, LANES), F32), ((VEC_ROWS, LANES), F32),
    ]
    outs = [shape((2,) + wide, BF), shape(wide, BF)] if block == 0 else [shape(wide, BF)]
    flops = 2 * tokens * inner * width
    return pl.pallas_call(
        functools.partial(first_kernel, block),
        in_specs=[ANY] * 3 + [VMEM] * 3 + [ANY] * 5,
        out_specs=[ANY] * len(outs) + [VMEM],
        out_shape=outs + [shape((VEC_ROWS, LANES), BF)],
        scratch_shapes=[pltpu.VMEM(dims, dtype) for dims, dtype in scratch] + [pltpu.SemaphoreType.DMA((8,))],
        compiler_params=pltpu.CompilerParams(vmem_limit_bytes=SMALL_LIMIT),
        cost_estimate=pl.CostEstimate(flops=8 * flops, bytes_accessed=20 * 2**20, transcendentals=0),
        name="first_%d" % block,
    )(gy_first, gy_second, grad_projected, small_own, small_got, vecs, n1, s1, r, own_in, got_in)


def load_weight(first, one, other, target, sem):
    pl.when(first)(pltpu.make_async_copy(one, target, sem).start)
    pl.when(jnp.logical_not(first))(pltpu.make_async_copy(other, target, sem).start)
    return pltpu.make_async_copy(one, target, sem)


def wait_all(copies):
    for copy in copies:
        copy.wait()


def unpack_kernel(taps_of, groups_of, *refs):
    refs = list(refs)

    def take(number):
        taken = refs[:number]
        del refs[:number]
        return taken

    own_of, got_of = [], []
    for _ in range(2):
        own_of.append(take(2))
        got_of.append(take(2))
    w_in_t_out, w_out_out, conv_out, gin, bin_, gmid, bmid, out_bias, w_in_t, w_out, conv, buf, extra, sem = refs
    inner, width = w_out.shape
    whole = inner // LANES
    tail = inner - whole * LANES
    slots = conv.shape[0]
    section = lax.axis_index("section")
    index = lax.axis_index("dp")

    def write(taps, groups, own, got):
        rows = own[0].shape[0] - VEC_ROWS
        count = share_count(groups[0])
        share = 2 * rows // count

        def body(position, _):
            for which, (pieces, side) in enumerate(((own, section), (got, 1 - section))):
                for at, ref in enumerate(pieces):
                    owner = owner_of(position + at * (count // 2), side, groups, index)
                    start = side * (2 * rows) + owner * share
                    pltpu.make_async_copy(
                        ref.at[pl.ds(pl.multiple_of(position * share, 16), share)],
                        buf.at[pl.ds(pl.multiple_of(start, 16), share)],
                        sem.at[2 * which + at],
                    ).start()
            return 0

        lax.fori_loop(0, count // 2, body, 0)
        pieces = list(own) + list(got)
        vectors = [
            pltpu.make_async_copy(ref.at[pl.ds(rows, VEC_ROWS)], extra.at[at], sem.at[4 + at])
            for at, ref in enumerate(pieces)
        ]
        start_all(vectors)
        for at, ref in enumerate(pieces):
            pltpu.make_async_copy(ref.at[pl.ds(0, rows)], buf.at[pl.ds(0, rows)], sem.at[at]).wait()
        wait_all(vectors)
        taps_at, tails_at, w_in_at, _, _ = layout(taps, width, inner)

        def wide(target, row):
            for at in range(0, width, LANES):
                q = at // LANES
                size = min(LANES, width - at)
                target[:, at : at + size] = buf[row + q * inner : row + (q + 1) * inner, 0:size].astype(F32)

        copies = []

        def leave(source, target):
            copies.append(pltpu.make_async_copy(source, target, sem.at[8 + len(copies)]))
            copies[-1].start()

        wide(w_out, 0)
        leave(w_out, w_out_out)
        tails = buf[tails_at : tails_at + inner, :].astype(F32)
        for k in range(slots):
            if k >= taps:
                conv[k] = jnp.zeros((inner, inner), F32)
            else:
                for q in range(whole):
                    at = taps_at + inner * (whole * k + q)
                    conv[k, :, LANES * q : LANES * (q + 1)] = buf[at : at + inner, :].astype(F32)
                conv[k, :, LANES * whole :] = tails[:, tail * k : tail * (k + 1)]
            leave(conv.at[k], conv_out.at[k])
        wide(w_in_t, w_in_at)
        leave(w_in_t, w_in_t_out)
        vec = sum(extra[at].astype(F32) for at in range(4))
        row = 0
        for target, member in ((gin, 0), (bin_, 0), (gmid, 0), (gmid, 1), (bmid, 0), (bmid, 1), (out_bias, 0)):
            for at in range(0, target.shape[1], LANES):
                size = min(LANES, target.shape[1] - at)
                target[member : member + 1, at : at + size] = vec[row : row + 1, 0:size]
                row += 1
        for copy in copies:
            copy.wait()

    pl.when(section == 0)(lambda: write(taps_of[0], groups_of[0], own_of[0], got_of[0]))
    pl.when(section != 0)(lambda: write(taps_of[1], groups_of[1], own_of[1], got_of[1]))


def unpack(taps_of, groups_of, enc, dec, width, inner):
    pieces = enc[0] + enc[1] + dec[0] + dec[1]
    rows = max(4 * part[0].shape[0] for part in (enc[0], dec[0]))
    return pl.pallas_call(
        functools.partial(unpack_kernel, taps_of, groups_of),
        in_specs=[ANY] * len(pieces),
        out_specs=[ANY] * 3 + [VMEM] * 5,
        out_shape=[
            shape((inner, width), F32), shape((inner, width), F32), shape((taps_of[0], inner, inner), F32),
            shape((1, width), F32), shape((1, width), F32), shape((2, inner), F32), shape((2, inner), F32),
            shape((1, width), F32),
        ],
        scratch_shapes=[
            pltpu.VMEM((inner, width), F32), pltpu.VMEM((inner, width), F32), pltpu.VMEM((taps_of[0], inner, inner), F32),
            pltpu.VMEM((rows, LANES), BF), pltpu.VMEM((4, VEC_ROWS, LANES), BF),
            pltpu.SemaphoreType.DMA((10 + taps_of[0],)),
        ],
        compiler_params=pltpu.CompilerParams(vmem_limit_bytes=SMALL_LIMIT),
        name="unpack",
    )(*pieces)


def swap_sections(value):
    return lax.ppermute(value, "section", [(0, 1), (1, 0)])


def swap_dp(value, masks):
    count = lax.axis_size("dp")
    pairs = [(s * count + i, s * count + (i ^ masks[s])) for s in range(2) for i in range(count)]
    return lax.ppermute(value, ("section", "dp"), pairs)


def rounded_sum(terms, rows):
    total = terms[0][rows].astype(F32)
    for term in terms[1:]:
        total = total + term[rows].astype(F32)
    return total.astype(BF)


def masks_of(bits, other):
    return [other << own[0] for own in bits]


def reduce_steps(keep, got, groups, receiver, vec=None):
    count = lax.axis_size("dp")
    steps = list(zip(*groups))
    terms = [keep, got]

    def loaded(part, riding):
        return part if vec is None or not riding else jnp.concatenate([part, vec], 0)

    for number, bits in enumerate(steps):
        size = terms[0].shape[0] >> len(bits[0])
        others = range(1, 2 ** len(bits[0]))
        parts = [rounded_sum(terms, slice(other * size, (other + 1) * size)) for other in others]
        parts = [loaded(part, number > 0) for part in parts]
        gate = yield parts
        came = after([swap_dp(part, masks_of(bits, other)) for part, other in zip(parts, others)], gate)
        terms = [term[:size] for term in terms] + [part[:size] for part in came]
        if vec is not None and number > 0:
            vec = rounded_sum([vec] + [part[size:] for part in came], slice(None))
    value = rounded_sum(terms, slice(None))
    rest = list(range(sum(len(bits) for bits in groups[0]), count.bit_length() - 1))
    for bits in zip(rest, rest[1:] + rest[:1]):
        size = value.shape[0]
        whole = loaded(value, True)
        gate = yield [whole]
        whole = rounded_sum([whole, after(swap_dp(whole, [1 << bit for bit in bits]), gate)], slice(None))
        value, vec = whole[:size], (None if vec is None else whole[size:])
    pieces = [value]
    for bits in reversed(steps[1:]):
        if len(pieces) > 1:
            value = jnp.concatenate(pieces, 0)
        gate = yield [value]
        came = [swap_dp(value, masks_of(bits, other)) for other in range(1, 2 ** len(bits[0]))]
        pieces = [value] + after(came, gate)
    if vec is not None:
        pieces = pieces + [vec]
    if len(pieces) > 1:
        value = jnp.concatenate(pieces, 0)
    gate = yield [value]
    sender = 1 - receiver
    masks = masks_of(steps[0], 1)
    ways = ((receiver, masks[receiver]), (sender, 0), (sender, masks[sender]))
    came = []
    for source, mask in ways:
        pairs = [(source * count + i, receiver * count + (i ^ mask)) for i in range(count)]
        came.append(lax.ppermute(value, ("section", "dp"), pairs))
    yield [value] + after(came, gate)


class Steps:
    def __init__(self, *args):
        self.steps = reduce_steps(*args)
        self.ready = next(self.steps)

    def step(self, gate=()):
        self.ready = self.steps.send(gate)
        return self.ready

    def finish(self):
        while len(self.ready) != 4:
            self.step()
        return self.ready[:2], self.ready[2:]


def after(values, earlier):
    return lax.optimization_barrier((values, earlier))[0] if earlier else values


def shards(
    section_inputs,
    seq_lengths,
    dilations,
    gains_in,
    biases_in,
    gains_mid,
    biases_mid,
    out_bias,
    w_in,
    w_out,
    conv_taps,
):
    section = lax.axis_index("section")
    count = lax.axis_size("dp")
    groups_of = (scatter_groups(count, False), scatter_groups(count, False))
    rows = jnp.swapaxes(section_inputs[0], 1, 2)
    width = rows.shape[1]
    inner = w_out.shape[1]
    taps_of = (conv_taps.shape[1], DEC_TAPS)

    own_w = (jnp.swapaxes(w_in[0], 0, 1), w_out[0], conv_taps[0])
    send_rows, small = prepare(rows, gains_in, biases_in, gains_mid[0], biases_mid[0], out_bias, dilations)
    got_rows = swap_sections(send_rows)
    got_small = swap_sections(small)
    got_w = tuple(swap_sections(member) for member in own_w)

    outs, send_y, grad_dec, keep_dec, send_dec, vec, *kept = main_call(
        taps_of, groups_of[1], seq_lengths, rows, got_rows, small, got_small, own_w, got_w
    )
    dec = Steps(keep_dec, swap_sections(send_dec), groups_of[1], 1, vec)
    grad_projected, vec, keep_enc, send_enc = encoder_call(
        taps_of[0], groups_of[0], seq_lengths, grad_dec, small, got_small, kept, own_w[1], got_w[1], own_w[2], got_w[2]
    )
    got_y = swap_sections(send_y)
    enc_early = swap_sections(send_enc)
    grad_projected = after(grad_projected, dec.ready)
    grads_x, send_gx, vec = first_call(
        0, grad_dec, grad_dec, grad_projected, vec, kept[0:3], small, got_small, own_w[0], got_w[0]
    )

    def joined(pair, got):
        pair = lax.dynamic_update_slice_in_dim(pair, got[None], 1 - section, 0)
        return jnp.swapaxes(pair, 1, 2)[None]

    enc = Steps(keep_enc, enc_early, groups_of[0], 0, vec)
    got_gx = swap_sections(send_gx)
    outputs = joined(outs, got_y)
    input_grads = joined(grads_x, got_gx)
    named = {"d": dec, "e": enc}
    last = ()
    for name in SEQ:
        if name in named:
            if len(named[name].ready) != 4:
                last = named[name].step(last)
        else:
            last = [*last, outputs if name == "y" else input_grads]
    enc = enc.finish()
    dec = dec.finish()
    grads = unpack(taps_of, groups_of, enc, dec, width, inner)
    return (
        outputs,
        input_grads,
        grads[3],
        grads[4],
        grads[5][None],
        grads[6][None],
        grads[7],
        jnp.swapaxes(grads[0], 0, 1)[None],
        grads[1][None],
        grads[2][None],
    )


def solution(mesh):
    in_specs = (
        P("section", None, "dp", None),
        P(None, "dp"),
        P("section"),
        P("section", None),
        P("section", None),
        P("section", None, None),
        P("section", None, None),
        P("section", None),
        P("section", None, None),
        P("section", None, None),
        P("section", None, None, None),
    )
    out_specs = (
        P("section", None, "dp", None),
        P("section", None, "dp", None),
        P("section", None),
        P("section", None),
        P("section", None, None),
        P("section", None, None),
        P("section", None),
        P("section", None, None),
        P("section", None, None),
        P("section", None, None, None),
    )
    return jax.shard_map(shards, mesh=mesh, in_specs=in_specs, out_specs=out_specs, check_vma=False)
```

time: 196 us -> 174 us (0.89)
  Pallas kernels: 85 us -> 72.2 us
  starting transfers between devices: 40.3 us -> 31.2 us
  other arithmetic: 2.55 us -> 8.98 us
  waiting for transfers between devices: 57.6 us -> 51.4 us
    ppermute x16 -> x10, waiting for transfers between devices: 46.3 us -> 22.8 us  [swap_dp(): return lax.ppermute(value, ('section', 'dp'), pairs)]
    ppermute x4 -> x6, waiting for transfers between devices: 0.01 us -> 21.3 us  [reduce_steps(): came.append(lax.ppermute(value, ('section', 'dp'), pairs))]
    ppermute x16 -> x10, starting transfers between devices: 27.1 us -> 18 us  [swap_dp(): return lax.ppermute(value, ('section', 'dp'), pairs)]
    pallas_call x1, Pallas kernels: 46.4 us -> 38.7 us  [main_call(): pl.pallas_call(functools.partial(main_kernel, taps_of, groups), in_specs=...]
    convert_element_type x8 -> x12, other arithmetic: 2.39 us -> 8.78 us  [rounded_sum(): return total.astype(BF)]
    pallas_call x2, Pallas kernels: 29.3 us -> 24.4 us  [the longest x1 15.7 us: encoder_call(): pl.pallas_call(functools.partial(encoder_kernel, taps, groups), in_specs=...]
    ppermute x9, waiting for transfers between devices: 11.3 us -> 7.36 us  [swap_sections(): return lax.ppermute(value, 'section', [(0, 1), (1, 0)])]
    unnamed x31 -> x34, local copies, waits for them, and re-layouts: 5.2 us -> 4.71 us
  transfers between devices with their start and end apart: 29 -> 25, of which waited for: 15 -> 11; matrix products, arithmetic and copies ran while one was open for 3% -> 6% of each run, Pallas kernels for 0% -> 14%
where the time goes in v3:
time: 174 us; the launch traced here: 172 us
  Pallas kernels  72.2 us (41%)
  waiting for transfers between devices  51.4 us (30%)
  starting transfers between devices  31.2 us (18%)
  other arithmetic  8.98 us (5%)
  local copies, waits for them, and re-layouts  6.27 us (4%)
  between operations  1.78 us (1%)
    pallas_call x1, Pallas kernels, main_call(): pl.pallas_call(functools.partial(main_kernel, taps_of, groups), in_specs=...  38.7 us
    ppermute x10, waiting for transfers between devices, swap_dp(): return lax.ppermute(value, ('section', 'dp'), pairs)  22.8 us
    ppermute x6, waiting for transfers between devices, reduce_steps(): came.append(lax.ppermute(value, ('section', 'dp'), pairs))  21.3 us
    ppermute x10, starting transfers between devices, swap_dp(): return lax.ppermute(value, ('section', 'dp'), pairs)  18 us
    pallas_call x1, Pallas kernels, encoder_call(): pl.pallas_call(functools.partial(encoder_kernel, taps, groups), in_specs=...  15.7 us
    ppermute x6, starting transfers between devices, reduce_steps(): came.append(lax.ppermute(value, ('section', 'dp'), pairs))  10.4 us
    convert_element_type x12, other arithmetic, rounded_sum(): return total.astype(BF)  8.78 us
    pallas_call x1, Pallas kernels, first_call(): pl.pallas_call(functools.partial(first_kernel, block), in_specs=[ANY] * 3...  8.66 us
  transfers between devices with their start and end apart: 25, of which 11 were waited for; matrix products, arithmetic and copies ran while one was open for 6% of the time, Pallas kernels for 14%

profile of v3, /device:TPU:0, one launch (start us, length us, event | category | flops | bytes accessed | tf_op | source)
XLA Modules:
  0.0 171.8 jit_solution(10163919155251065359)
XLA Ops:
  1.3 3.6 %prepare.1 = (bf16[800,1024]{1,0:T(8,128)(2,1)}, f32[8,800]{1,0:T(8,128)}) custom-call(bf16[2,800,1024]{2,1,0:T(8,128)(2,1)} %bitcast.27, f32[1,800]{1,0:T(1,128)} %gin.1, f32[1,800]{1,0:T(1,128)} %bin_.1, f32[2,400]{1,0:T(2,128)} %bitcast.29, f32[2,400]{1,0:T(2,128)} %bitcast.30, f32[1,800]{1,0:T(1,128)} %out_bias.1, s32[1]{0:T(128)S(6)} %copy.23.dilation), custom_call_target="tpu_custom_call" | custom-call | tf_op jit(solution)/shard_map/prepare/pallas_call | solution.py:409
  4.9 0.5 collective-permute-start
  5.4 0.1 collective-permute-start.4
  5.5 0.4 collective-permute-start.2
  5.9 0.1 collective-permute-start.3
  6.0 0.4 collective-permute-start.1
  6.4 7.3 %collective-permute-done.1.refs_4_.small_got = f32[8,800]{1,0:T(8,128)S(1)} collective-permute-done((f32[8,800]{1,0:T(8,128)}, f32[8,800]{1,0:T(8,128)S(1)}, u32[]{:S(2)}, u32[]{:S(2)}) %collective-permute-start.1) | collective-permute-done | bytes 25632 | tf_op jit(solution)/shard_map/ppermute | solution.py:861
  13.8 0.0 collective-permute-done.2.refs_8_.got_in
  13.8 0.0 collective-permute-done.3.refs_9_.got_out
  13.8 0.9 copy-done.14
  14.6 0.0 collective-permute-done.4.refs_10_.got_conv
  14.6 0.9 copy-done.15
  15.5 0.0 collective-permute-done.refs_2_
  15.5 1.2 copy-done.13
  16.7 38.7 %main_blocks.1 = (bf16[2,800,1024]{2,1,0:T(8,128)(2,1)}, bf16[800,1024]{1,0:T(8,128)(2,1)}, bf16[800,1024]{1,0:T(8,128)(2,1)}, bf16[4800,128]{1,0:T(8,128)(2,1)}...) custom-call(s32[2,8]{1,0:T(2,128)} %seq.1, ...), custom_call_target="tpu_custom_call" | custom-call | flops 39321600000 | bytes 62914560 | tf_op jit(solution)/shard_map/main_blocks/pallas_call | solution.py:556
  55.3 0.4 collective-permute-start.6
  55.8 15.7 %encoder_back.1 = (bf16[400,1024]{1,0:T(8,128)(2,1)}, f32[8,800]{1,0:T(8,128)}, bf16[6016,128]{1,0:T(8,128)(2,1)}, bf16[6016,128]{1,0:T(8,128)(2,1)}) custom-call(s32[2,8]{1,0:T(2,128)} %seq.1, bf16[800,1024]{1,0:T(8,128)(2,1)} %get-tuple-element.60.gy_in.gy_first.gy_second, f32[8,800]{1,0:T(8,128)} %get-tuple-element.57.refs_3_.small_own, ...), custom_call_target="tpu_custom_call" | custom-call | flops 20971520000 | bytes 20971520 | tf_op jit(solution)/shard_map/encoder_back/pallas_call | solution.py:656
  71.5 0.1 collective-permute-start.8
  71.7 2.1 %add_convert_fusion.1 = bf16[2400,128]{1,0:T(8,128)(2,1)} fusion(bf16[4800,128]{1,0:T(8,128)(2,1)} %collective-permute-done.6, bf16[4800,128]{1,0:T(8,128)(2,1)S(1)} %copy-done.3), kind=kLoop, calls=%fused_computation.3 | loop fusion | flops 1228800 | bytes 1843200 | tf_op jit(solution)/shard_map/convert_element_type | solution.py:874
  73.7 2.9 %collective-permute-start.10 = (bf16[2400,128]{1,0:T(8,128)(2,1)}, bf16[2400,128]{1,0:T(8,128)(2,1)}, u32[]{:S(2)}, u32[]{:S(2)}) collective-permute-start(bf16[2400,128]{1,0:T(8,128)(2,1)} %add_convert_fusion.1), channel_id=1, source_target_pairs={{0,1},{1,0},{2,3},{3,2},{4,5},{5,4},{6,7},{7,6},{8,9},{9,8},{10,11... | collective-permute-start | bytes 1843208 | tf_op jit(solution)/shard_map/ppermute | solution.py:867
  76.6 8.7 %first_0.1 = (bf16[2,800,1024]{2,1,0:T(8,128)(2,1)}, bf16[800,1024]{1,0:T(8,128)(2,1)}, bf16[48,128]{1,0:T(8,128)(2,1)}) custom-call(bf16[800,1024]{1,0:T(8,128)(2,1)} %get-tuple-element.60.gy_in.gy_first.gy_second, bf16[800,1024]{1,0:T(8,128)(2,1)} %get-tuple-element.60.gy_in.gy_first.gy_second, bf16[400,1024]{1,0:T(8,128)(2,1)} %get-tuple-element.72.grad_projected_in, ...), custom_call_target="tpu_custom_call" | custom-call | flops 5242880000 | bytes 20971520 | tf_op jit(solution)/shard_map/first_0/pallas_call | solution.py:726
  85.3 0.6 collective-permute-start.7
  85.9 1.3 add_convert_fusion.9
  87.2 1.6 collective-permute-start.11
  88.8 1.3 add_convert_fusion
  90.1 1.3 collective-permute-start.9
  91.4 1.3 bitcast_dynamic-update-slice_fusion.1
  92.7 3.4 %collective-permute-done.11 = bf16[1248,128]{1,0:T(8,128)(2,1)S(1)} collective-permute-done((bf16[1248,128]{1,0:T(8,128)(2,1)S(1)}, bf16[1248,128]{1,0:T(8,128)(2,1)S(1)}, u32[]{:S(2)}, u32[]{:S(2)}) %collective-permute-start.11) | collective-permute-done | bytes 319520 | tf_op jit(solution)/shard_map/ppermute | solution.py:867
  96.1 1.3 add_convert_fusion.8
  97.5 1.6 collective-permute-start.13
  99.1 2.9 %collective-permute-done.9 = bf16[3008,128]{1,0:T(8,128)(2,1)S(1)} collective-permute-done((bf16[3008,128]{1,0:T(8,128)(2,1)S(1)}, bf16[3008,128]{1,0:T(8,128)(2,1)S(1)}, u32[]{:S(2)}, u32[]{:S(2)}) %collective-permute-start.9) | collective-permute-done | bytes 770080 | tf_op jit(solution)/shard_map/ppermute | solution.py:867
  102.0 1.2 add_convert_fusion.5
  103.2 1.2 collective-permute-start.12
  104.5 2.3 %collective-permute-done.13 = bf16[1248,128]{1,0:T(8,128)(2,1)S(1)} collective-permute-done((bf16[1248,128]{1,0:T(8,128)(2,1)S(1)}, bf16[1248,128]{1,0:T(8,128)(2,1)S(1)}, u32[]{:S(2)}, u32[]{:S(2)}) %collective-permute-start.13) | collective-permute-done | bytes 319520 | tf_op jit(solution)/shard_map/ppermute | solution.py:867
  106.8 0.1 add_convert_fusion.7
  106.9 2.7 %collective-permute-start.15 = (bf16[1248,128]{1,0:T(8,128)(2,1)S(1)}, bf16[1248,128]{1,0:T(8,128)(2,1)S(1)}, u32[]{:S(2)}, u32[]{:S(2)}) collective-permute-start(bf16[1248,128]{1,0:T(8,128)(2,1)S(1)} %add_convert_fusion.7), channel_id=1, source_target_pairs={{0,8},{1,9},{2,10},{3,11},{4,12},{5,13},{6,14},{7,15},{8,0},{9,1},... | collective-permute-start | bytes 958472 | tf_op jit(solution)/shard_map/ppermute | solution.py:867
  109.6 1.5 collective-permute-done.12
  111.1 1.2 add_convert_fusion.4
  112.3 0.0 copy-start.11
  112.4 1.6 collective-permute-start.14
  114.0 10.1 %collective-permute-done.15 = bf16[1248,128]{1,0:T(8,128)(2,1)S(1)} collective-permute-done((bf16[1248,128]{1,0:T(8,128)(2,1)S(1)}, bf16[1248,128]{1,0:T(8,128)(2,1)S(1)}, u32[]{:S(2)}, u32[]{:S(2)}) %collective-permute-start.15) | collective-permute-done | bytes 319520 | tf_op jit(solution)/shard_map/ppermute | solution.py:867
  124.1 0.1 add_convert_fusion.6
  124.2 1.8 %collective-permute-start.17 = (bf16[1200,128]{1,0:T(8,128)(2,1)S(1)}, bf16[1200,128]{1,0:T(8,128)(2,1)S(1)}, u32[]{:S(2)}, u32[]{:S(2)}) collective-permute-start(bf16[1200,128]{1,0:T(8,128)(2,1)S(1)} %slice.122), channel_id=1, source_target_pairs={{0,2},{1,3},{2,0},{3,1},{4,6},{5,7},{6,4},{7,5},{8,10},{9,11},{10,... | collective-permute-start | bytes 921608 | tf_op jit(solution)/shard_map/ppermute | solution.py:867
  126.1 0.1 add_convert_fusion.3
  126.2 2.8 %collective-permute-start.16 = (bf16[1552,128]{1,0:T(8,128)(2,1)S(1)}, bf16[1552,128]{1,0:T(8,128)(2,1)S(1)}, u32[]{:S(2)}, u32[]{:S(2)}) collective-permute-start(bf16[1552,128]{1,0:T(8,128)(2,1)S(1)} %add_convert_fusion.3), channel_id=1, source_target_pairs={{0,8},{1,9},{2,10},{3,11},{4,12},{5,13},{6,14},{7,15},{8,0},{9,1},... | collective-permute-start | bytes 1191944 | tf_op jit(solution)/shard_map/ppermute | solution.py:867
  129.0 0.2 bitcast_dynamic-update-slice_fusion
  129.2 0.0 copy-start.12
  129.2 1.9 %collective-permute-done.17 = bf16[1200,128]{1,0:T(8,128)(2,1)S(1)} collective-permute-done((bf16[1200,128]{1,0:T(8,128)(2,1)S(1)}, bf16[1200,128]{1,0:T(8,128)(2,1)S(1)}, u32[]{:S(2)}, u32[]{:S(2)}) %collective-permute-start.17) | collective-permute-done | bytes 307232 | tf_op jit(solution)/shard_map/ppermute | solution.py:867
  131.2 0.7 collective-permute-start.19
  131.9 1.8 %collective-permute-start.20 = (bf16[2448,128]{1,0:T(8,128)(2,1)S(1)}, bf16[2448,128]{1,0:T(8,128)(2,1)S(1)}, u32[]{:S(2)}, u32[]{:S(2)}) collective-permute-start(bf16[2448,128]{1,0:T(8,128)(2,1)S(1)} %pad_maximum_fusion.1.refs_4_), channel_id=1, source_target_pairs={{0,16},{1,17},{2,18},{3,19},{4,20},{5,21},{6,22},{7,23},{8,24},{9,... | collective-permute-start | bytes 1880072 | tf_op jit(solution)/shard_map/ppermute | solution.py:925
  133.7 2.1 %collective-permute-start.21 = (bf16[2448,128]{1,0:T(8,128)(2,1)S(1)}, bf16[2448,128]{1,0:T(8,128)(2,1)S(1)}, u32[]{:S(2)}, u32[]{:S(2)}) collective-permute-start(bf16[2448,128]{1,0:T(8,128)(2,1)S(1)} %pad_maximum_fusion.1.refs_4_), channel_id=1, source_target_pairs={{0,17},{1,16},{2,19},{3,18},{4,21},{5,20},{6,23},{7,22},{8,25},{9,... | collective-permute-start | bytes 1880072 | tf_op jit(solution)/shard_map/ppermute | solution.py:925
  135.9 0.7 collective-permute-done.16
  136.5 0.1 add_convert_fusion.2
  136.7 0.4 collective-permute-start.18
  137.1 10.2 %collective-permute-done.21.refs_7_ = bf16[2448,128]{1,0:T(8,128)(2,1)S(1)} collective-permute-done((bf16[2448,128]{1,0:T(8,128)(2,1)S(1)}, bf16[2448,128]{1,0:T(8,128)(2,1)S(1)}, u32[]{:S(2)}, u32[]{:S(2)}) %collective-permute-start.21) | collective-permute-done | bytes 626720 | tf_op jit(solution)/shard_map/ppermute | solution.py:925
  147.3 0.8 copy-done.8
  148.1 0.1 pad_maximum_fusion.refs_0_
  148.2 3.2 %collective-permute-start.22 = (bf16[3056,128]{1,0:T(8,128)(2,1)S(1)}, bf16[3056,128]{1,0:T(8,128)(2,1)S(1)}, u32[]{:S(2)}, u32[]{:S(2)}) collective-permute-start(bf16[3056,128]{1,0:T(8,128)(2,1)S(1)} %pad_maximum_fusion.refs_0_), channel_id=1, source_target_pairs={{0,1},{1,0},{2,3},{3,2},{4,5},{5,4},{6,7},{7,6},{8,9},{9,8},{10,11... | collective-permute-start | bytes 2347016 | tf_op jit(solution)/shard_map/ppermute | solution.py:925
  151.4 1.3 collective-permute-start.23
  152.7 1.3 collective-permute-start.24
  154.0 8.0 %collective-permute-done.22.refs_1_ = bf16[3056,128]{1,0:T(8,128)(2,1)S(1)} collective-permute-done((bf16[3056,128]{1,0:T(8,128)(2,1)S(1)}, bf16[3056,128]{1,0:T(8,128)(2,1)S(1)}, u32[]{:S(2)}, u32[]{:S(2)}) %collective-permute-start.22) | collective-permute-done | bytes 782368 | tf_op jit(solution)/shard_map/ppermute | solution.py:925
  162.0 0.9 copy-done.5
  163.0 3.1 %collective-permute-done.24.refs_3_ = bf16[3056,128]{1,0:T(8,128)(2,1)} collective-permute-done((bf16[3056,128]{1,0:T(8,128)(2,1)S(1)}, bf16[3056,128]{1,0:T(8,128)(2,1)}, u32[]{:S(2)}, u32[]{:S(2)}) %collective-permute-start.24) | collective-permute-done | bytes 782368 | tf_op jit(solution)/shard_map/ppermute | solution.py:925
  166.0 5.6 %unpack.1 = (f32[400,800]{1,0:T(8,128)}, f32[400,800]{1,0:T(8,128)}, f32[5,400,400]{2,1,0:T(8,128)}, f32[1,800]{1,0:T(1,128)}, f32[1,800]{1,0:T(1,128)}, /*index...) custom-call(bf16[3056,128]{1,0:T(8,128)(2,1)} %copy-done, bf16[3056,128]{1,0:T(8,128)(2,1)} %copy-done.4, ...), custom_call_target="tpu_custom_call" | custom-call | tf_op jit(solution)/shard_map/unpack/pallas_call | solution.py:841
  (49 shorter events, 0.3 us)
Async XLA Ops:
  4.9 10.6 %collective-permute-start = (bf16[800,1024]{1,0:T(8,128)(2,1)}, bf16[800,1024]{1,0:T(8,128)(2,1)S(1)}, u32[]{:S(2)}, u32[]{:S(2)}) collective-permute-start(bf16[800,1024]{1,0:T(8,128)(2,1)} %get-tuple-element.56), channel_id=1, source_target_pairs={{0,16},{16,0},{1,17},{17,1},{2,18},{18,2},{3,19},{19,3},{4,20},{20... | collective-permute-start | bytes 4915208 | tf_op jit(solution)/shard_map/ppermute | solution.py:861
  5.4 9.3 %collective-permute-start.4 = (bf16[5,400,400]{2,1,0:T(8,128)(2,1)}, bf16[5,400,400]{2,1,0:T(8,128)(2,1)}, u32[]{:S(2)}, u32[]{:S(2)}) collective-permute-start(bf16[5,400,400]{2,1,0:T(8,128)(2,1)} %bitcast.34), channel_id=1, source_target_pairs={{0,16},{16,0},{1,17},{17,1},{2,18},{18,2},{3,19},{19,3},{4,20},{20... | collective-permute-start | bytes 4800008 | tf_op jit(solution)/shard_map/ppermute | solution.py:861
  5.5 8.3 %collective-permute-start.2 = (bf16[400,800]{1,0:T(8,128)(2,1)}, bf16[400,800]{1,0:T(8,128)(2,1)S(1)}, u32[]{:S(2)}, u32[]{:S(2)}) collective-permute-start(bf16[400,800]{1,0:T(8,128)(2,1)} %bitcast.42), channel_id=1, source_target_pairs={{0,16},{16,0},{1,17},{17,1},{2,18},{18,2},{3,19},{19,3},{4,20},{20... | collective-permute-start | bytes 1920008 | tf_op jit(solution)/shard_map/ppermute | solution.py:861
  5.9 7.9 %collective-permute-start.3 = (bf16[400,800]{1,0:T(8,128)(2,1)}, bf16[400,800]{1,0:T(8,128)(2,1)S(1)}, u32[]{:S(2)}, u32[]{:S(2)}) collective-permute-start(bf16[400,800]{1,0:T(8,128)(2,1)} %bitcast.39), channel_id=1, source_target_pairs={{0,16},{16,0},{1,17},{17,1},{2,18},{18,2},{3,19},{19,3},{4,20},{20... | collective-permute-start | bytes 1920008 | tf_op jit(solution)/shard_map/ppermute | solution.py:861
  6.0 7.8 %collective-permute-start.1 = (f32[8,800]{1,0:T(8,128)}, f32[8,800]{1,0:T(8,128)S(1)}, u32[]{:S(2)}, u32[]{:S(2)}) collective-permute-start(f32[8,800]{1,0:T(8,128)} %get-tuple-element.57.refs_3_.small_own), channel_id=1, source_target_pairs={{0,16},{16,0},{1,17},{17,1},{2,18},{18,2},{3,19},{19,3},{4,20},{20... | collective-permute-start | bytes 76808 | tf_op jit(solution)/shard_map/ppermute | solution.py:861
  13.8 1.8 %copy-start.16 = (f32[8,800]{1,0:T(8,128)}, f32[8,800]{1,0:T(8,128)S(1)}, u32[]{:S(2)}) copy-start(f32[8,800]{1,0:T(8,128)S(1)} %collective-permute-done.1.refs_4_.small_got) | copy-start | bytes 76804
  13.8 0.9 copy-start.14
  14.6 0.9 copy-start.15
  15.5 1.2 copy-start.13
  55.3 16.3 %collective-permute-start.6 = (bf16[4800,128]{1,0:T(8,128)(2,1)}, bf16[4800,128]{1,0:T(8,128)(2,1)}, u32[]{:S(2)}, u32[]{:S(2)}) collective-permute-start(bf16[4800,128]{1,0:T(8,128)(2,1)} %get-tuple-element.71), channel_id=1, source_target_pairs={{0,16},{16,0},{1,17},{17,1},{2,18},{18,2},{3,19},{19,3},{4,20},{20... | collective-permute-start | bytes 3686408 | tf_op jit(solution)/shard_map/ppermute | solution.py:861
  55.8 15.9 %copy-start.3 = (bf16[4800,128]{1,0:T(8,128)(2,1)S(1)}, bf16[4800,128]{1,0:T(8,128)(2,1)}, u32[]{:S(2)}) copy-start(bf16[4800,128]{1,0:T(8,128)(2,1)} %get-tuple-element.70) | copy-start | bytes 3686404
  71.5 17.3 %collective-permute-start.8 = (bf16[6016,128]{1,0:T(8,128)(2,1)}, bf16[6016,128]{1,0:T(8,128)(2,1)}, u32[]{:S(2)}, u32[]{:S(2)}) collective-permute-start(bf16[6016,128]{1,0:T(8,128)(2,1)} %get-tuple-element.79), channel_id=1, source_target_pairs={{0,16},{16,0},{1,17},{17,1},{2,18},{18,2},{3,19},{19,3},{4,20},{20... | collective-permute-start | bytes 4620296 | tf_op jit(solution)/shard_map/ppermute | solution.py:861
  73.7 12.2 %collective-permute-start.10 = (bf16[2400,128]{1,0:T(8,128)(2,1)}, bf16[2400,128]{1,0:T(8,128)(2,1)}, u32[]{:S(2)}, u32[]{:S(2)}) collective-permute-start(bf16[2400,128]{1,0:T(8,128)(2,1)} %add_convert_fusion.1), channel_id=1, source_target_pairs={{0,1},{1,0},{2,3},{3,2},{4,5},{5,4},{6,7},{7,6},{8,9},{9,8},{10,11... | collective-permute-start | bytes 1843208 | tf_op jit(solution)/shard_map/ppermute | solution.py:867
  76.6 14.8 %collective-permute-start.5 = (bf16[800,1024]{1,0:T(8,128)(2,1)}, bf16[800,1024]{1,0:T(8,128)(2,1)S(1)}, u32[]{:S(2)}, u32[]{:S(2)}) collective-permute-start(bf16[800,1024]{1,0:T(8,128)(2,1)} %get-tuple-element.59), channel_id=1, source_target_pairs={{0,16},{16,0},{1,17},{17,1},{2,18},{18,2},{3,19},{19,3},{4,20},{20... | collective-permute-start | bytes 4915208 | tf_op jit(solution)/shard_map/ppermute | solution.py:861
  76.6 10.5 %copy-start.9 = (bf16[48,128]{1,0:T(8,128)(2,1)S(1)}, bf16[48,128]{1,0:T(8,128)(2,1)}, u32[]{:S(2)}) copy-start(bf16[48,128]{1,0:T(8,128)(2,1)} %get-tuple-element.80) | copy-start | bytes 36868
  85.3 3.5 %copy-start.2 = (bf16[6016,128]{1,0:T(8,128)(2,1)S(1)}, bf16[6016,128]{1,0:T(8,128)(2,1)}, u32[]{:S(2)}) copy-start(bf16[6016,128]{1,0:T(8,128)(2,1)} %get-tuple-element.78) | copy-start | bytes 4620292
  85.3 43.7 %collective-permute-start.7 = (bf16[800,1024]{1,0:T(8,128)(2,1)}, bf16[800,1024]{1,0:T(8,128)(2,1)S(1)}, u32[]{:S(2)}, u32[]{:S(2)}) collective-permute-start(bf16[800,1024]{1,0:T(8,128)(2,1)} %get-tuple-element.77), channel_id=1, source_target_pairs={{0,16},{16,0},{1,17},{17,1},{2,18},{18,2},{3,19},{19,3},{4,20},{20... | collective-permute-start | bytes 4915208 | tf_op jit(solution)/shard_map/ppermute | solution.py:861
  87.2 8.9 %collective-permute-start.11 = (bf16[1248,128]{1,0:T(8,128)(2,1)S(1)}, bf16[1248,128]{1,0:T(8,128)(2,1)S(1)}, u32[]{:S(2)}, u32[]{:S(2)}) collective-permute-start(bf16[1248,128]{1,0:T(8,128)(2,1)S(1)} %pad_maximum_fusion.4), channel_id=1, source_target_pairs={{0,2},{1,3},{2,0},{3,1},{4,6},{5,7},{6,4},{7,5},{8,10},{9,11},{10,... | collective-permute-start | bytes 958472 | tf_op jit(solution)/shard_map/ppermute | solution.py:867
  90.1 11.9 %collective-permute-start.9 = (bf16[3008,128]{1,0:T(8,128)(2,1)S(1)}, bf16[3008,128]{1,0:T(8,128)(2,1)S(1)}, u32[]{:S(2)}, u32[]{:S(2)}) collective-permute-start(bf16[3008,128]{1,0:T(8,128)(2,1)S(1)} %add_convert_fusion), channel_id=1, source_target_pairs={{0,1},{1,0},{2,3},{3,2},{4,5},{5,4},{6,7},{7,6},{8,9},{9,8},{10,11... | collective-permute-start | bytes 2310152 | tf_op jit(solution)/shard_map/ppermute | solution.py:867
  96.1 7.1 %copy-start.10 = (bf16[48,128]{1,0:T(8,128)(2,1)S(1)}, bf16[48,128]{1,0:T(8,128)(2,1)}, u32[]{:S(2)}) copy-start(bf16[48,128]{1,0:T(8,128)(2,1)} %get-tuple-element.83) | copy-start | bytes 36868
  97.5 9.4 %collective-permute-start.13 = (bf16[1248,128]{1,0:T(8,128)(2,1)S(1)}, bf16[1248,128]{1,0:T(8,128)(2,1)S(1)}, u32[]{:S(2)}, u32[]{:S(2)}) collective-permute-start(bf16[1248,128]{1,0:T(8,128)(2,1)S(1)} %pad_maximum_fusion.5), channel_id=1, source_target_pairs={{0,4},{1,5},{2,6},{3,7},{4,0},{5,1},{6,2},{7,3},{8,12},{9,13},{10,... | collective-permute-start | bytes 958472 | tf_op jit(solution)/shard_map/ppermute | solution.py:867
  103.2 7.9 %collective-permute-start.12 = (bf16[1552,128]{1,0:T(8,128)(2,1)S(1)}, bf16[1552,128]{1,0:T(8,128)(2,1)S(1)}, u32[]{:S(2)}, u32[]{:S(2)}) collective-permute-start(bf16[1552,128]{1,0:T(8,128)(2,1)S(1)} %pad_maximum_fusion.2), channel_id=1, source_target_pairs={{0,2},{1,3},{2,0},{3,1},{4,6},{5,7},{6,4},{7,5},{8,10},{9,11},{10,... | collective-permute-start | bytes 1191944 | tf_op jit(solution)/shard_map/ppermute | solution.py:867
  106.9 17.2 %collective-permute-start.15 = (bf16[1248,128]{1,0:T(8,128)(2,1)S(1)}, bf16[1248,128]{1,0:T(8,128)(2,1)S(1)}, u32[]{:S(2)}, u32[]{:S(2)}) collective-permute-start(bf16[1248,128]{1,0:T(8,128)(2,1)S(1)} %add_convert_fusion.7), channel_id=1, source_target_pairs={{0,8},{1,9},{2,10},{3,11},{4,12},{5,13},{6,14},{7,15},{8,0},{9,1},... | collective-permute-start | bytes 958472 | tf_op jit(solution)/shard_map/ppermute | solution.py:867
  112.3 16.6 %copy-start.11 = (bf16[2,800,1024]{2,1,0:T(8,128)(2,1)S(1)}, bf16[2,800,1024]{2,1,0:T(8,128)(2,1)}, u32[]{:S(2)}) copy-start(bf16[2,800,1024]{2,1,0:T(8,128)(2,1)} %get-tuple-element.76) | copy-start | bytes 9830404
  112.4 13.7 %collective-permute-start.14 = (bf16[1552,128]{1,0:T(8,128)(2,1)S(1)}, bf16[1552,128]{1,0:T(8,128)(2,1)S(1)}, u32[]{:S(2)}, u32[]{:S(2)}) collective-permute-start(bf16[1552,128]{1,0:T(8,128)(2,1)S(1)} %pad_maximum_fusion.3), channel_id=1, source_target_pairs={{0,4},{1,5},{2,6},{3,7},{4,0},{5,1},{6,2},{7,3},{8,12},{9,13},{10,... | collective-permute-start | bytes 1191944 | tf_op jit(solution)/shard_map/ppermute | solution.py:867
  124.2 6.9 %collective-permute-start.17 = (bf16[1200,128]{1,0:T(8,128)(2,1)S(1)}, bf16[1200,128]{1,0:T(8,128)(2,1)S(1)}, u32[]{:S(2)}, u32[]{:S(2)}) collective-permute-start(bf16[1200,128]{1,0:T(8,128)(2,1)S(1)} %slice.122), channel_id=1, source_target_pairs={{0,2},{1,3},{2,0},{3,1},{4,6},{5,7},{6,4},{7,5},{8,10},{9,11},{10,... | collective-permute-start | bytes 921608 | tf_op jit(solution)/shard_map/ppermute | solution.py:867
  126.2 10.4 %collective-permute-start.16 = (bf16[1552,128]{1,0:T(8,128)(2,1)S(1)}, bf16[1552,128]{1,0:T(8,128)(2,1)S(1)}, u32[]{:S(2)}, u32[]{:S(2)}) collective-permute-start(bf16[1552,128]{1,0:T(8,128)(2,1)S(1)} %add_convert_fusion.3), channel_id=1, source_target_pairs={{0,8},{1,9},{2,10},{3,11},{4,12},{5,13},{6,14},{7,15},{8,0},{9,1},... | collective-permute-start | bytes 1191944 | tf_op jit(solution)/shard_map/ppermute | solution.py:867
  129.2 32.8 %copy-start.12 = (bf16[2,800,1024]{2,1,0:T(8,128)(2,1)}, bf16[2,800,1024]{2,1,0:T(8,128)(2,1)S(1)}, u32[]{:S(2)}) copy-start(bf16[2,800,1024]{2,1,0:T(8,128)(2,1)S(1)} %bitcast_dynamic-update-slice_fusion) | copy-start | bytes 9830404
  131.2 17.0 %copy-start.1 = (bf16[2448,128]{1,0:T(8,128)(2,1)}, bf16[2448,128]{1,0:T(8,128)(2,1)S(1)}, u32[]{:S(2)}) copy-start(bf16[2448,128]{1,0:T(8,128)(2,1)S(1)} %pad_maximum_fusion.1.refs_4_) | copy-start | bytes 1880068
  131.2 5.9 %collective-permute-start.19 = (bf16[2448,128]{1,0:T(8,128)(2,1)S(1)}, bf16[2448,128]{1,0:T(8,128)(2,1)S(1)}, u32[]{:S(2)}, u32[]{:S(2)}) collective-permute-start(bf16[2448,128]{1,0:T(8,128)(2,1)S(1)} %pad_maximum_fusion.1.refs_4_), channel_id=1, source_target_pairs={{16,18},{17,19},{18,16},{19,17},{20,22},{21,23},{22,20},{23,21},{2... | collective-permute-start | bytes 1880072 | tf_op jit(solution)/shard_map/ppermute | solution.py:925
  131.9 5.2 %collective-permute-start.20 = (bf16[2448,128]{1,0:T(8,128)(2,1)S(1)}, bf16[2448,128]{1,0:T(8,128)(2,1)S(1)}, u32[]{:S(2)}, u32[]{:S(2)}) collective-permute-start(bf16[2448,128]{1,0:T(8,128)(2,1)S(1)} %pad_maximum_fusion.1.refs_4_), channel_id=1, source_target_pairs={{0,16},{1,17},{2,18},{3,19},{4,20},{5,21},{6,22},{7,23},{8,24},{9,... | collective-permute-start | bytes 1880072 | tf_op jit(solution)/shard_map/ppermute | solution.py:925
  133.7 13.5 %collective-permute-start.21 = (bf16[2448,128]{1,0:T(8,128)(2,1)S(1)}, bf16[2448,128]{1,0:T(8,128)(2,1)S(1)}, u32[]{:S(2)}, u32[]{:S(2)}) collective-permute-start(bf16[2448,128]{1,0:T(8,128)(2,1)S(1)} %pad_maximum_fusion.1.refs_4_), channel_id=1, source_target_pairs={{0,17},{1,16},{2,19},{3,18},{4,21},{5,20},{6,23},{7,22},{8,25},{9,... | collective-permute-start | bytes 1880072 | tf_op jit(solution)/shard_map/ppermute | solution.py:925
  136.7 11.4 %collective-permute-start.18 = (bf16[1504,128]{1,0:T(8,128)(2,1)S(1)}, bf16[1504,128]{1,0:T(8,128)(2,1)S(1)}, u32[]{:S(2)}, u32[]{:S(2)}) collective-permute-start(bf16[1504,128]{1,0:T(8,128)(2,1)S(1)} %slice.124), channel_id=1, source_target_pairs={{0,2},{1,3},{2,0},{3,1},{4,6},{5,7},{6,4},{7,5},{8,10},{9,11},{10,... | collective-permute-start | bytes 1155080 | tf_op jit(solution)/shard_map/ppermute | solution.py:867
  137.1 10.2 %copy-start.6 = (bf16[2448,128]{1,0:T(8,128)(2,1)}, bf16[2448,128]{1,0:T(8,128)(2,1)S(1)}, u32[]{:S(2)}) copy-start(bf16[2448,128]{1,0:T(8,128)(2,1)S(1)} %collective-permute-done.19.refs_5_) | copy-start | bytes 1880068
  137.1 10.2 %copy-start.7 = (bf16[2448,128]{1,0:T(8,128)(2,1)}, bf16[2448,128]{1,0:T(8,128)(2,1)S(1)}, u32[]{:S(2)}) copy-start(bf16[2448,128]{1,0:T(8,128)(2,1)S(1)} %collective-permute-done.20.refs_6_) | copy-start | bytes 1880068
  147.3 0.8 copy-start.8
  148.2 17.9 %copy-start = (bf16[3056,128]{1,0:T(8,128)(2,1)}, bf16[3056,128]{1,0:T(8,128)(2,1)S(1)}, u32[]{:S(2)}) copy-start(bf16[3056,128]{1,0:T(8,128)(2,1)S(1)} %pad_maximum_fusion.refs_0_) | copy-start | bytes 2347012
  148.2 13.8 %collective-permute-start.22 = (bf16[3056,128]{1,0:T(8,128)(2,1)S(1)}, bf16[3056,128]{1,0:T(8,128)(2,1)S(1)}, u32[]{:S(2)}, u32[]{:S(2)}) collective-permute-start(bf16[3056,128]{1,0:T(8,128)(2,1)S(1)} %pad_maximum_fusion.refs_0_), channel_id=1, source_target_pairs={{0,1},{1,0},{2,3},{3,2},{4,5},{5,4},{6,7},{7,6},{8,9},{9,8},{10,11... | collective-permute-start | bytes 2347016 | tf_op jit(solution)/shard_map/ppermute | solution.py:925
  151.4 10.7 %collective-permute-start.23 = (bf16[3056,128]{1,0:T(8,128)(2,1)S(1)}, bf16[3056,128]{1,0:T(8,128)(2,1)S(1)}, u32[]{:S(2)}, u32[]{:S(2)}) collective-permute-start(bf16[3056,128]{1,0:T(8,128)(2,1)S(1)} %pad_maximum_fusion.refs_0_), channel_id=1, source_target_pairs={{16,0},{17,1},{18,2},{19,3},{20,4},{21,5},{22,6},{23,7},{24,8},{25... | collective-permute-start | bytes 2347016 | tf_op jit(solution)/shard_map/ppermute | solution.py:925
  152.7 13.4 %collective-permute-start.24 = (bf16[3056,128]{1,0:T(8,128)(2,1)S(1)}, bf16[3056,128]{1,0:T(8,128)(2,1)}, u32[]{:S(2)}, u32[]{:S(2)}) collective-permute-start(bf16[3056,128]{1,0:T(8,128)(2,1)S(1)} %pad_maximum_fusion.refs_0_), channel_id=1, source_target_pairs={{16,2},{17,3},{18,0},{19,1},{20,6},{21,7},{22,4},{23,5},{24,10},{2... | collective-permute-start | bytes 2347016 | tf_op jit(solution)/shard_map/ppermute | solution.py:925
  162.0 4.0 %copy-start.4 = (bf16[3056,128]{1,0:T(8,128)(2,1)}, bf16[3056,128]{1,0:T(8,128)(2,1)S(1)}, u32[]{:S(2)}) copy-start(bf16[3056,128]{1,0:T(8,128)(2,1)S(1)} %collective-permute-done.22.refs_1_) | copy-start | bytes 2347012
  162.0 0.9 copy-start.5
